TPU v7x, 32 devices: a whole 2x2x4 slice. The times are simulated.
32 devices in a mesh: ctx: 8 (over y, x, core), fsdp: 4 (over z).
Axes of the slice: x: 2, y: 2, z: 4, core: 2. Of those that a mesh axis runs over, the one named last changes fastest.
Arguments:
- tokens: bfloat16 [4, 1536, 2048], P('fsdp', 'ctx'), may hold values from -6 to 6
- lengths: int32 [4, 2], P('fsdp'), may hold values from 1 to 1535, as said below
- deal: int32 [4, 8, 8], P('fsdp'), may hold values from 0 to 7, each once within a row
- attn_gain: bfloat16 [2048], P('fsdp'), may hold values from 0.5 to 1.5
- query_weight: bfloat16 [2048, 2048], P('fsdp'), may hold values from -0.5 to 0.5
- key_matrix: bfloat16 [2048, 512], P('fsdp'), may hold values from -0.5 to 0.5
- value_matrix: bfloat16 [2048, 512], P('fsdp'), may hold values from -0.125 to 0.125
- out_weight: bfloat16 [2048, 2048], P('fsdp'), may hold values from -1.5 to 1.5
- mlp_gain: bfloat16 [2048], P('fsdp'), may hold values from 0.5 to 1.5
- gate_weight: bfloat16 [2048, 8192], P('fsdp'), may hold values from -0.125 to 0.125
- up_weight: bfloat16 [2048, 8192], P('fsdp'), may hold values from -0.125 to 0.125
- down_weight: bfloat16 [8192, 2048], P('fsdp'), may hold values from -0.25 to 0.25
- cotangent: bfloat16 [4, 1536, 2048], P('fsdp', 'ctx'), may hold values from -6 to 6
Outputs:
- activations: bfloat16 [4, 1536, 2048], P('fsdp', 'ctx')
- token_grad: float32 [4, 1536, 2048], P('fsdp', 'ctx')
- attn_gain_grad: float32 [2048], P('fsdp')
- query_grad: float32 [2048, 2048], P('fsdp')
- key_grad: float32 [2048, 512], P('fsdp')
- value_grad: float32 [2048, 512], P('fsdp')
- out_grad: float32 [2048, 2048], P('fsdp')
- mlp_gain_grad: float32 [2048], P('fsdp')
- gate_grad: float32 [2048, 8192], P('fsdp')
- up_grad: float32 [2048, 8192], P('fsdp')
- down_grad: float32 [8192, 2048], P('fsdp')
Inputs may be any that keep to these rules, and one draw needn't show every extreme that they name: Each row holds the lengths of the two sequences of one group laid end to end; they sum to 1536 and the longer holds at least 1024 tokens. deal[f, i, k] is the device along ctx that holds, in dealt order, the k-th block of 24 tokens of ctx device i of group f; each row is a permutation.
All inputs are finite; a program needn't handle non-finite values.
Results may differ from a plain program's by a relative error of at most 0.024.
Values may be sent and summed in bfloat16 or wider, within the bound.
A program may use at most 576 MiB of HBM per device.

v0:
```python
import jax
import jax.numpy as jnp
from jax import lax
from jax.sharding import PartitionSpec as P

QUERY_HEADS = 32
KEY_VALUE_HEADS = 8
HEAD_SIZE = 64


EPSILON = 1e-05
ROPE_BASE = 10000000.0
SCORE_SCALE = 0.015625
RESIDUAL_SCALE = 0.22
NEGATIVE_BIG = -1e30


def rms_scale(rows_in):
    return lax.rsqrt(jnp.mean(rows_in * rows_in, axis=-1, keepdims=True) + EPSILON)


def rotary(positions):
    freq_index = jnp.arange(HEAD_SIZE // 2, dtype=jnp.float32)
    inverse = ROPE_BASE ** (-2.0 * freq_index / HEAD_SIZE)
    angles = positions.astype(jnp.float32)[:, None] * inverse[None, :]
    return (jnp.cos(angles)[:, None, :], jnp.sin(angles)[:, None, :])


def apply_rotary(heads_in, cosine_values, sine_values):
    first_half = heads_in[..., : HEAD_SIZE // 2]
    second_half = heads_in[..., HEAD_SIZE // 2 :]
    return jnp.concatenate(
        [
            first_half * cosine_values - second_half * sine_values,
            second_half * cosine_values + first_half * sine_values,
        ],
        axis=-1,
    )


def reverse_rotary(grads_in, cosine_values, sine_values):
    first_half = grads_in[..., : HEAD_SIZE // 2]
    second_half = grads_in[..., HEAD_SIZE // 2 :]
    return jnp.concatenate(
        [
            first_half * cosine_values + second_half * sine_values,
            second_half * cosine_values - first_half * sine_values,
        ],
        axis=-1,
    )


def given_table(deal_rows, n_ctx, tokens_per_device):
    block_rows = tokens_per_device // n_ctx
    slot_ids = jnp.arange(n_ctx, dtype=jnp.int32)
    matched = deal_rows[:, :, None] == slot_ids[None, None, :]
    source_slot = jnp.sum(jnp.where(matched, slot_ids[None, :, None], 0), axis=1)
    first_block = slot_ids[:, None] * n_ctx + source_slot
    offsets = jnp.arange(block_rows, dtype=jnp.int32)
    table = first_block.T[:, :, None] * block_rows + offsets[None, None, :]
    return table.reshape(n_ctx, tokens_per_device)


def times_transpose(left_op, right_op):
    return lax.dot_general(
        left_op, right_op, (((1,), (1,)), ((), ())), preferred_element_type=jnp.float32
    )


def collect(gain_a, weight_q, weight_k, weight_v, weight_o, gain_m, weight_g, weight_u, weight_d):
    return (
        lax.all_gather(gain_a, "fsdp", axis=0, tiled=True),
        lax.all_gather(weight_q, "fsdp", axis=0, tiled=True),
        lax.all_gather(weight_k, "fsdp", axis=0, tiled=True),
        lax.all_gather(weight_v, "fsdp", axis=0, tiled=True),
        lax.all_gather(weight_o, "fsdp", axis=0, tiled=True),
        lax.all_gather(gain_m, "fsdp", axis=0, tiled=True),
        lax.all_gather(weight_g, "fsdp", axis=0, tiled=True),
        lax.all_gather(weight_u, "fsdp", axis=0, tiled=True),
        lax.all_gather(weight_d, "fsdp", axis=0, tiled=True),
    )


def gather_kv(key_rot, value_matrix_rows):
    return (
        lax.all_gather(key_rot, "ctx", axis=0, tiled=True),
        lax.all_gather(value_matrix_rows, "ctx", axis=0, tiled=True),
    )


def project(weights, token_rows, cosine_values, sine_values):
    token_matrix = token_rows.shape[0]
    attn_scale = rms_scale(token_rows)
    normalized_rows = (token_rows * attn_scale * weights[0]).astype(jnp.bfloat16)
    queries = jnp.dot(normalized_rows, weights[1], preferred_element_type=jnp.float32).reshape(
        token_matrix, QUERY_HEADS, HEAD_SIZE
    )
    keys_before_rotary = jnp.dot(
        normalized_rows, weights[2], preferred_element_type=jnp.float32
    ).reshape(token_matrix, KEY_VALUE_HEADS, HEAD_SIZE)
    query_rotated = apply_rotary(queries, cosine_values, sine_values).astype(jnp.bfloat16)
    key_rot = (
        apply_rotary(keys_before_rotary, cosine_values, sine_values)
        .astype(jnp.bfloat16)
        .reshape(token_matrix, KEY_VALUE_HEADS * HEAD_SIZE)
    )
    value_matrix_rows = jnp.dot(
        normalized_rows, weights[3], preferred_element_type=jnp.float32
    ).astype(jnp.bfloat16)
    return (attn_scale, normalized_rows, query_rotated, key_rot, value_matrix_rows)


def mlp_inputs(weights, hidden):
    mlp_scale = rms_scale(hidden)
    normed2 = (hidden * mlp_scale * weights[5]).astype(jnp.bfloat16)
    gate_rows = jnp.dot(normed2, weights[6], preferred_element_type=jnp.float32)
    up_rows = jnp.dot(normed2, weights[7], preferred_element_type=jnp.float32)
    mixed_rows = (jax.nn.silu(gate_rows) * up_rows).astype(jnp.bfloat16)
    return (mlp_scale, normed2, gate_rows, up_rows, mixed_rows)


def key_blocks(every_key, every_value, mask_info):
    own_given, own_segment, key_given, key_segment = mask_info
    rows_per_group = every_key.shape[0]
    width_of_keys = min(512, rows_per_group)
    count_of_blocks = rows_per_group // width_of_keys
    return (
        every_key.reshape(count_of_blocks, width_of_keys, KEY_VALUE_HEADS, HEAD_SIZE),
        every_value.reshape(count_of_blocks, width_of_keys, KEY_VALUE_HEADS, HEAD_SIZE),
        key_given.reshape(count_of_blocks, width_of_keys),
        key_segment.reshape(count_of_blocks, width_of_keys),
    )


def block_scores(grouped_queries, key_block, given_blk, segment_blk, mask_info):
    own_given, own_segment = (mask_info[0], mask_info[1])
    raw_scores = (
        jnp.einsum("omua,fma->muof", grouped_queries, key_block, preferred_element_type=jnp.float32)
        * SCORE_SCALE
    )
    allowed = (segment_blk[None, :] == own_segment[:, None]) & (
        given_blk[None, :] <= own_given[:, None]
    )
    return (raw_scores, allowed)


def attention_forward(query_rotated, every_key, every_value, mask_info):
    token_matrix = query_rotated.shape[0]
    heads_per_key = QUERY_HEADS // KEY_VALUE_HEADS
    grouped_queries = query_rotated.reshape(token_matrix, KEY_VALUE_HEADS, heads_per_key, HEAD_SIZE)
    blocks = key_blocks(every_key, every_value, mask_info)

    def total_step(run_state, packed_tokens):
        run_max, run_sum = run_state
        raw_scores, allowed = block_scores(
            grouped_queries, packed_tokens[0], packed_tokens[2], packed_tokens[3], mask_info
        )
        masked = jnp.where(allowed, raw_scores, NEGATIVE_BIG)
        new_max = jnp.maximum(run_max, jnp.max(masked, axis=-1))
        added = jnp.sum(jnp.where(allowed, jnp.exp(raw_scores - new_max[..., None]), 0.0), axis=-1)
        return ((new_max, run_sum * jnp.exp(run_max - new_max) + added), None)

    initial_maximum = jnp.full(
        (KEY_VALUE_HEADS, heads_per_key, token_matrix), NEGATIVE_BIG, jnp.float32
    )
    initial_sum = jnp.zeros((KEY_VALUE_HEADS, heads_per_key, token_matrix), jnp.float32)
    (run_max, run_sum), unused = lax.scan(total_step, (initial_maximum, initial_sum), blocks)
    log_total = run_max + jnp.log(run_sum)

    def value_step(run_state, packed_tokens):
        raw_scores, allowed = block_scores(
            grouped_queries, packed_tokens[0], packed_tokens[2], packed_tokens[3], mask_info
        )
        reduced_probabilities = jnp.where(
            allowed, jnp.exp(raw_scores - log_total[..., None]), 0.0
        ).astype(jnp.bfloat16)
        return (
            run_state
            + jnp.einsum(
                "oauc,coq->uoaq",
                reduced_probabilities,
                packed_tokens[1],
                preferred_element_type=jnp.float32,
            ),
            None,
        )

    initial_output = jnp.zeros(
        (token_matrix, KEY_VALUE_HEADS, heads_per_key, HEAD_SIZE), jnp.float32
    )
    attended_forward, unused = lax.scan(value_step, initial_output, blocks)
    return (attended_forward.reshape(token_matrix, QUERY_HEADS * HEAD_SIZE), log_total)


def attention_backward(
    query_rotated, every_key, every_value, attended_forward, attended_gradient, log_total, mask_info
):
    token_matrix = query_rotated.shape[0]
    rows_per_group = every_key.shape[0]
    heads_per_key = QUERY_HEADS // KEY_VALUE_HEADS
    grouped_queries = query_rotated.reshape(token_matrix, KEY_VALUE_HEADS, heads_per_key, HEAD_SIZE)
    gradient_groups = attended_gradient.reshape(
        token_matrix, KEY_VALUE_HEADS, heads_per_key, HEAD_SIZE
    )
    delta_rows = jnp.sum(
        attended_gradient.astype(jnp.float32).reshape(
            token_matrix, KEY_VALUE_HEADS, heads_per_key, HEAD_SIZE
        )
        * attended_forward.reshape(token_matrix, KEY_VALUE_HEADS, heads_per_key, HEAD_SIZE),
        axis=-1,
    ).transpose(1, 2, 0)
    blocks = key_blocks(every_key, every_value, mask_info)

    def block_step(query_sum, packed_tokens):
        key_block, value_block = (packed_tokens[0], packed_tokens[1])
        raw_scores, allowed = block_scores(
            grouped_queries, key_block, packed_tokens[2], packed_tokens[3], mask_info
        )
        prob_rows = jnp.where(allowed, jnp.exp(raw_scores - log_total[..., None]), 0.0)
        reduced_probabilities = prob_rows.astype(jnp.bfloat16)
        prob_grad = jnp.einsum(
            "omua,fma->muof", gradient_groups, value_block, preferred_element_type=jnp.float32
        )
        score_gradient = (prob_rows * (prob_grad - delta_rows[..., None])).astype(jnp.bfloat16)
        query_sum = query_sum + jnp.einsum(
            "oauc,coq->uoaq", score_gradient, key_block, preferred_element_type=jnp.float32
        )
        key_part = (
            jnp.einsum(
                "kupq,pkun->qkn",
                score_gradient,
                grouped_queries,
                preferred_element_type=jnp.float32,
            )
            * SCORE_SCALE
        )
        value_part = jnp.einsum(
            "kupq,pkun->qkn",
            reduced_probabilities,
            gradient_groups,
            preferred_element_type=jnp.float32,
        )
        return (query_sum, (key_part, value_part))

    initial_sum = jnp.zeros((token_matrix, KEY_VALUE_HEADS, heads_per_key, HEAD_SIZE), jnp.float32)
    query_sum, (key_pieces, value_pieces) = lax.scan(block_step, initial_sum, blocks)
    return (
        (query_sum * SCORE_SCALE).reshape(token_matrix, QUERY_HEADS, HEAD_SIZE),
        key_pieces.reshape(rows_per_group, KEY_VALUE_HEADS * HEAD_SIZE),
        value_pieces.reshape(rows_per_group, KEY_VALUE_HEADS * HEAD_SIZE),
    )


def row_term(left_op, right_op):
    return lax.dot_general(
        left_op, right_op, (((0,), (0,)), ((), ())), preferred_element_type=jnp.float32
    )


def settle(left_op, right_op):
    partial_value = lax.psum_scatter(
        row_term(left_op, right_op).astype(jnp.bfloat16), "fsdp", scatter_dimension=0, tiled=True
    )
    return lax.psum(partial_value, "ctx").astype(jnp.float32)


def norm_backward(normed_grad, rows_in, scale_col, gain_full):
    weighted = normed_grad * gain_full
    gain_local = jnp.sum(normed_grad * rows_in * scale_col, axis=0)
    rows_grad = scale_col * weighted - rows_in * scale_col**3 * jnp.mean(
        weighted * rows_in, axis=-1, keepdims=True
    )
    return (rows_grad, gain_local)


def local(
    tokens,
    lengths,
    deal,
    attn_gain,
    query_weight,
    key_matrix,
    value_matrix,
    out_weight,
    mlp_gain,
    gate_weight,
    up_weight,
    down_weight,
    cotangent,
):
    n_ctx = lax.axis_size("ctx")
    ctx_index = lax.axis_index("ctx")
    fsdp_index = lax.axis_index("fsdp")
    tokens_per_device = tokens.shape[1]
    block_rows = tokens_per_device // n_ctx
    deal_rows = deal[0]
    first_len = lengths[0, 0]
    given_idx = given_table(deal_rows, n_ctx, tokens_per_device)
    segment = (given_idx >= first_len).astype(jnp.int32)
    position = given_idx - segment * first_len
    own_given = lax.dynamic_index_in_dim(given_idx, ctx_index, 0, keepdims=False)
    own_segment = lax.dynamic_index_in_dim(segment, ctx_index, 0, keepdims=False)
    own_position = lax.dynamic_index_in_dim(position, ctx_index, 0, keepdims=False)
    mask_info = (own_given, own_segment, given_idx.reshape(-1), segment.reshape(-1))
    cosine_values, sine_values = rotary(own_position)
    own_deal = lax.dynamic_index_in_dim(deal_rows, ctx_index, 0, keepdims=False)
    slot_ids = jnp.arange(n_ctx, dtype=jnp.int32)
    send_order = jnp.sum(
        jnp.where(own_deal[None, :] == slot_ids[:, None], slot_ids[None, :], 0), axis=1
    )
    outgoing = jnp.take(tokens[0].reshape(n_ctx, block_rows, -1), send_order, axis=0)
    dealt_rows = lax.all_to_all(outgoing, "ctx", split_axis=0, concat_axis=0, tiled=True)
    token_rows = dealt_rows.reshape(tokens_per_device, -1).astype(jnp.float32)
    weights = collect(
        attn_gain,
        query_weight,
        key_matrix,
        value_matrix,
        out_weight,
        mlp_gain,
        gate_weight,
        up_weight,
        down_weight,
    )
    attn_scale, normalized_rows, query_rotated, key_rot, value_matrix_rows = project(
        weights, token_rows, cosine_values, sine_values
    )
    every_key, every_value = gather_kv(key_rot, value_matrix_rows)
    attended_forward, log_total = attention_forward(
        query_rotated, every_key, every_value, mask_info
    )
    attended = attended_forward.astype(jnp.bfloat16)
    hidden = token_rows + RESIDUAL_SCALE * jnp.dot(
        attended, weights[4], preferred_element_type=jnp.float32
    )
    mlp_scale, normed2, gate_rows, up_rows, mixed_rows = mlp_inputs(weights, hidden)
    result = hidden + RESIDUAL_SCALE * jnp.dot(
        mixed_rows, weights[8], preferred_element_type=jnp.float32
    )
    activations = result.astype(jnp.bfloat16)[None]
    weights = collect(
        attn_gain,
        query_weight,
        key_matrix,
        value_matrix,
        out_weight,
        mlp_gain,
        gate_weight,
        up_weight,
        down_weight,
    )
    attn_scale, normalized_rows, query_rotated, key_rot, value_matrix_rows = project(
        weights, token_rows, cosine_values, sine_values
    )
    every_key, every_value = gather_kv(key_rot, value_matrix_rows)
    mlp_scale, normed2, gate_rows, up_rows, mixed_rows = mlp_inputs(weights, hidden)
    grad_rows = cotangent[0].astype(jnp.float32)
    mlp_grad = (RESIDUAL_SCALE * grad_rows).astype(jnp.bfloat16)
    down_grad = settle(mixed_rows, mlp_grad)
    mixed_grad = times_transpose(mlp_grad, weights[8])
    sigmoid_gate = jax.nn.sigmoid(gate_rows)
    gate_rows_grad = (
        mixed_grad * up_rows * sigmoid_gate * (1.0 + gate_rows * (1.0 - sigmoid_gate))
    ).astype(jnp.bfloat16)
    up_rows_grad = (mixed_grad * gate_rows * sigmoid_gate).astype(jnp.bfloat16)
    gate_grad = settle(normed2, gate_rows_grad)
    up_grad = settle(normed2, up_rows_grad)
    normed2_grad = times_transpose(gate_rows_grad, weights[6]) + times_transpose(
        up_rows_grad, weights[7]
    )
    hidden_grad, mlp_gain_local = norm_backward(normed2_grad, hidden, mlp_scale, weights[5])
    hidden_grad = hidden_grad + grad_rows
    attn_branch_grad = (RESIDUAL_SCALE * hidden_grad).astype(jnp.bfloat16)
    out_grad = settle(attended, attn_branch_grad)
    attended_gradient = times_transpose(attn_branch_grad, weights[4]).astype(jnp.bfloat16)
    query_rot_grad, key_all_grad, value_all_grad = attention_backward(
        query_rotated,
        every_key,
        every_value,
        attended_forward,
        attended_gradient,
        log_total,
        mask_info,
    )
    key_local_gradient, value_own_grad = (
        lax.psum_scatter(
            key_all_grad.astype(jnp.bfloat16), "ctx", scatter_dimension=0, tiled=True
        ).astype(jnp.float32),
        lax.psum_scatter(
            value_all_grad.astype(jnp.bfloat16), "ctx", scatter_dimension=0, tiled=True
        ).astype(jnp.float32),
    )
    query_pre_grad = (
        reverse_rotary(query_rot_grad, cosine_values, sine_values)
        .astype(jnp.bfloat16)
        .reshape(tokens_per_device, -1)
    )
    key_pre_grad = (
        reverse_rotary(
            key_local_gradient.reshape(tokens_per_device, KEY_VALUE_HEADS, HEAD_SIZE),
            cosine_values,
            sine_values,
        )
        .astype(jnp.bfloat16)
        .reshape(tokens_per_device, -1)
    )
    value_pre_grad = value_own_grad.astype(jnp.bfloat16)
    query_grad = settle(normalized_rows, query_pre_grad)
    key_grad = settle(normalized_rows, key_pre_grad)
    value_grad = settle(normalized_rows, value_pre_grad)
    normed_grad = (
        times_transpose(query_pre_grad, weights[1])
        + times_transpose(key_pre_grad, weights[2])
        + times_transpose(value_pre_grad, weights[3])
    )
    token_grad_rows, attn_gain_local = norm_backward(
        normed_grad, token_rows, attn_scale, weights[0]
    )
    token_grad_rows = token_grad_rows + hidden_grad
    returned = lax.all_to_all(
        token_grad_rows.reshape(n_ctx, block_rows, -1).astype(jnp.bfloat16),
        "ctx",
        split_axis=0,
        concat_axis=0,
        tiled=True,
    ).astype(jnp.float32)
    token_grad = jnp.take(returned, own_deal, axis=0).reshape(1, tokens_per_device, -1)
    gain_totals = lax.psum((attn_gain_local, mlp_gain_local), ("ctx", "fsdp"))
    shard_len = attn_gain.shape[0]
    attn_gain_grad = lax.dynamic_slice_in_dim(gain_totals[0], fsdp_index * shard_len, shard_len)
    mlp_gain_grad = lax.dynamic_slice_in_dim(gain_totals[1], fsdp_index * shard_len, shard_len)
    return (
        activations,
        token_grad,
        attn_gain_grad,
        query_grad,
        key_grad,
        value_grad,
        out_grad,
        mlp_gain_grad,
        gate_grad,
        up_grad,
        down_grad,
    )


def solution(mesh):
    placed = (
        P("fsdp", "ctx", None),
        P("fsdp", None),
        P("fsdp", None, None),
        P("fsdp"),
        P("fsdp", None),
        P("fsdp", None),
        P("fsdp", None),
        P("fsdp", None),
        P("fsdp"),
        P("fsdp", None),
        P("fsdp", None),
        P("fsdp", None),
        P("fsdp", "ctx", None),
    )
    return jax.shard_map(
        local,
        mesh=mesh,
        in_specs=placed,
        out_specs=(
            P("fsdp", "ctx", None),
            P("fsdp", "ctx", None),
            P("fsdp"),
            P("fsdp", None),
            P("fsdp", None),
            P("fsdp", None),
            P("fsdp", None),
            P("fsdp"),
            P("fsdp", None),
            P("fsdp", None),
            P("fsdp", None),
        ),
        check_vma=False,
    )
```

profile of v0, /device:TPU:9, one launch (start us, length us, event | category | flops | bytes accessed | tf_op | source)
XLA Modules:
  0.0 4875.1 jit_solution(11819154494422664039)
XLA Ops:
  27.1 27.9 all-gather.12.cloned.1.call-done
  59.0 42.3 all-gather.16.cloned.1.call-done
  167.5 138.9 %all-gather.20.cloned.1.call-done = bf16[2048,2048]{1,0:T(8,128)(2,1)} async-done(((bf16[512,2048]{1,0:T(8,128)(2,1)}), bf16[2048,2048]{1,0:T(8,128)(2,1)}) %all-gather.20.cloned.1.call-update) | async-done | bytes 8388624 | tf_op jit(solution)/shard_map/all_gather | solution.py:73
  325.8 51.0 %while.39 = (s32[]{:T(128)}, f32[8,4,192]{2,1,0:T(4,128)S(1)}, f32[8,4,192]{2,1,0:T(4,128)}, s32[3,512]{1,0:T(4,128)}, s32[192]{0:T(256)S(1)}, /*index=5*/s32[3,...) while((s32[]{:T(128)}, f32[8,4,192]{2,1,0:T(4,128)S(1)}, ...), condition=%wide.region_6.7_spmd.clone, body=%wide.region_3.6_spmd.clone.sunk | while | flops 424998912 | bytes 27563712 | solution.py:167
  378.2 25.0 while.40
  405.9 49.8 %all-gather.22.cloned.1.call-done = bf16[2048,2048]{1,0:T(8,128)(2,1)} async-done(((bf16[512,2048]{1,0:T(8,128)(2,1)}), bf16[2048,2048]{1,0:T(8,128)(2,1)}) %all-gather.22.cloned.1.call-update) | async-done | bytes 8388624 | tf_op jit(solution)/shard_map/all_gather | solution.py:76
  462.8 554.1 %all-gather.24.cloned.1.call-done = bf16[2048,8192]{1,0:T(8,128)(2,1)} async-done(((bf16[512,8192]{1,0:T(8,128)(2,1)}), bf16[2048,8192]{1,0:T(8,128)(2,1)}) %all-gather.24.cloned.1.call-update) | async-done | bytes 33554448 | tf_op jit(solution)/shard_map/all_gather | solution.py:78
  1016.9 18.3 fusion.79
  1035.2 542.9 %all-gather.26.cloned.1.call-done = bf16[2048,8192]{1,0:T(8,128)(2,1)} async-done(((bf16[512,8192]{1,0:T(8,128)(2,1)}), bf16[2048,8192]{1,0:T(8,128)(2,1)}) %all-gather.26.cloned.1.call-update) | async-done | bytes 33554448 | tf_op jit(solution)/shard_map/all_gather | solution.py:79
  1578.1 18.3 fusion.80
  1596.4 542.9 %all-gather.28.cloned.1.call-done = bf16[8192,2048]{1,0:T(8,128)(2,1)} async-done(((bf16[2048,2048]{1,0:T(8,128)(2,1)}), bf16[8192,2048]{1,0:T(8,128)(2,1)}) %all-gather.28.cloned.1.call-update) | async-done | bytes 33554448 | tf_op jit(solution)/shard_map/all_gather | solution.py:80
  2139.3 21.8 multiply_convert_fusion
  2179.4 19.8 multiply_reduce_fusion.1
  2212.5 83.0 %while.41 = (s32[]{:T(128)}, f32[192,8,4,64]{0,3,2,1:T(8,128)}, bf16[3,512,8,64]{1,3,2,0:T(8,128)(2,1)}, bf16[3,512,8,64]{1,3,2,0:T(8,128)(2,1)}, bf16[3,512,8,6...) while((s32[]{:T(128)}, f32[192,8,4,64]{0,3,2,1:T(8,128)}, ...), condition=%wide.region_13.14_spmd.clone, body=%wide.region_12.13_spmd.clone.sunk | while | flops 2046066688 | bytes 199350096 | solution.py:246
  2314.9 30.6 reduce-scatter.28.cloned.1.call-done
  2349.6 38.2 reduce-scatter.30.cloned.1.call-done
  2456.5 20.6 reduce-scatter.24.cloned.1.call-done
  2477.1 148.8 %reduce-scatter.20.cloned.1.call-done = bf16[512,2048]{1,0:T(8,128)(2,1)} async-done(((bf16[2048,2048]{1,0:T(8,128)(2,1)}), bf16[512,2048]{1,0:T(8,128)(2,1)}) %reduce-scatter.20.cloned.1.call-update) | async-done | bytes 2097168 | tf_op jit(solution)/shard_map/reduce_scatter | solution.py:261
  2625.9 148.0 %reduce-scatter.26.cloned.1.call-done = bf16[512,2048]{1,0:T(8,128)(2,1)} async-done(((bf16[2048,2048]{1,0:T(8,128)(2,1)}), bf16[512,2048]{1,0:T(8,128)(2,1)}) %reduce-scatter.26.cloned.1.call-update) | async-done | bytes 2097168 | tf_op jit(solution)/shard_map/reduce_scatter | solution.py:261
  2773.9 552.2 %reduce-scatter.32.cloned.1.call-done = bf16[512,8192]{1,0:T(8,128)(2,1)} async-done(((bf16[2048,8192]{1,0:T(8,128)(2,1)}), bf16[512,8192]{1,0:T(8,128)(2,1)}) %reduce-scatter.32.cloned.1.call-update) | async-done | bytes 8388624
  3326.1 555.1 %reduce-scatter.34.cloned.1.call-done = bf16[512,8192]{1,0:T(8,128)(2,1)} async-done(((bf16[2048,8192]{1,0:T(8,128)(2,1)}), bf16[512,8192]{1,0:T(8,128)(2,1)}) %reduce-scatter.34.cloned.1.call-update) | async-done | bytes 8388624
  3881.2 555.0 %reduce-scatter.36.cloned.1.call-done = bf16[2048,2048]{1,0:T(8,128)(2,1)} async-done(((bf16[8192,2048]{1,0:T(8,128)(2,1)}), bf16[2048,2048]{1,0:T(8,128)(2,1)}) %reduce-scatter.36.cloned.1.call-update) | async-done | bytes 8388624
  4469.7 44.7 all-reduce.3
  4520.4 303.4 %all-reduce.7.cloned.1.call-done = (bf16[512,2048]{1,0:T(8,128)(2,1)}, bf16[512,512]{1,0:T(8,128)(2,1)}, bf16[512,512]{1,0:T(8,128)(2,1)}, bf16[512,2048]{1,0:T(...) async-done(((bf16[512,2048]{1,0:T(8,128)(2,1)}, bf16[512,512]{1,0:T(8,128)(2,1)}, bf16[512,512]{1,0:T(8,128)(2,1)}, ...) | async-done | bytes 30408720 | tf_op jit(solution)/shard_map/psum | solution.py:264
  (340 shorter events, 485.6 us)
Async XLA Ops:
  7.2 47.8 all-gather.12.cloned.1.call-start
  7.9 93.4 %all-gather.16.cloned.1.call-start = ((), (), s32[]{:S(2)}) async-start(), calls=%async_computation.13 | async-start | bytes 2621440 | tf_op jit(solution)/shard_map/all_gather | solution.py:74
  11.8 14.7 all-to-all-start
  16.2 114.4 %all-gather.14.cloned.1.call-start = ((), (), s32[]{:S(2)}) async-start(), calls=%async_computation.12 | async-start | bytes 1769472 | tf_op jit(solution)/shard_map/all_gather | solution.py:87
  26.5 429.3 %copy-start.6 = (bf16[8,24,2048]{2,1,0:T(8,128)(2,1)}, bf16[8,24,2048]{2,1,0:T(8,128)(2,1)S(1)}, u32[]{:S(2)}) copy-start(bf16[8,24,2048]{2,1,0:T(8,128)(2,1)S(1)} %all-to-all-done) | copy-start | bytes 2359300
  57.9 100.7 %all-gather.18.cloned.1.call-start = ((), (), s32[]{:S(2)}) async-start(), calls=%async_computation.14 | async-start | bytes 1769472 | tf_op jit(solution)/shard_map/all_gather | solution.py:86
  58.7 266.5 %copy-start.34 = (f32[192,32]{0,1:T(8,128)}, f32[192,32]{0,1:T(8,128)S(1)}, u32[]{:S(2)}) copy-start(f32[192,32]{0,1:T(8,128)S(1)} %get-tuple-element.526) | copy-start | bytes 73732
  108.5 197.9 %all-gather.20.cloned.1.call-start = ((), (), s32[]{:S(2)}) async-start(), calls=%async_computation.15 | async-start | bytes 10485760 | tf_op jit(solution)/shard_map/all_gather | solution.py:73
  109.1 346.6 %all-gather.22.cloned.1.call-start = ((), (), s32[]{:S(2)}) async-start(), calls=%async_computation.16 | async-start | bytes 10485760 | tf_op jit(solution)/shard_map/all_gather | solution.py:76
  109.7 907.3 %all-gather.24.cloned.1.call-start = ((), (), s32[]{:S(2)}) async-start(), calls=%async_computation.17 | async-start | bytes 41943040 | tf_op jit(solution)/shard_map/all_gather | solution.py:78
  110.4 1467.7 %all-gather.26.cloned.1.call-start = ((), (), s32[]{:S(2)}) async-start(), calls=%async_computation.18 | async-start | bytes 41943040 | tf_op jit(solution)/shard_map/all_gather | solution.py:79
  111.2 2028.2 %all-gather.28.cloned.1.call-start = ((), (), s32[]{:S(2)}) async-start(), calls=%async_computation.19 | async-start | bytes 41943040 | tf_op jit(solution)/shard_map/all_gather | solution.py:80
  111.9 2233.6 %reduce-scatter.28.cloned.1.call-start = ((), (), s32[]{:S(2)}) async-start(), calls=%async_computation.24 | async-start | bytes 1769472
  462.8 1115.3 %copy-start.19 = (bf16[192,2048]{1,0:T(8,128)(2,1)}, bf16[192,2048]{1,0:T(8,128)(2,1)S(1)}, u32[]{:S(2)}) copy-start(bf16[192,2048]{1,0:T(8,128)(2,1)S(1)} %multiply_convert_fusion.4) | copy-start | bytes 2359300
  2305.9 82.0 %reduce-scatter.30.cloned.1.call-start = ((), (), s32[]{:S(2)}) async-start(), calls=%async_computation.25 | async-start | bytes 1769472
  2314.8 141.7 %reduce-scatter.22.cloned.1.call-start = ((), (), s32[]{:S(2)}) async-start(), calls=%async_computation.21 | async-start | bytes 2621440 | tf_op jit(solution)/shard_map/reduce_scatter | solution.py:261
  2349.6 127.5 %reduce-scatter.24.cloned.1.call-start = ((), (), s32[]{:S(2)}) async-start(), calls=%async_computation.22 | async-start | bytes 2621440 | tf_op jit(solution)/shard_map/reduce_scatter | solution.py:261
  2391.1 234.7 %reduce-scatter.20.cloned.1.call-start = ((), (), s32[]{:S(2)}) async-start(), calls=%async_computation.20 | async-start | bytes 10485760 | tf_op jit(solution)/shard_map/reduce_scatter | solution.py:261
  2399.0 374.9 %reduce-scatter.26.cloned.1.call-start = ((), (), s32[]{:S(2)}) async-start(), calls=%async_computation.23 | async-start | bytes 10485760 | tf_op jit(solution)/shard_map/reduce_scatter | solution.py:261
  2406.4 919.6 %reduce-scatter.32.cloned.1.call-start = ((), (), s32[]{:S(2)}) async-start(), calls=%async_computation.26 | async-start | bytes 41943040
  2423.3 1457.9 %reduce-scatter.34.cloned.1.call-start = ((), (), s32[]{:S(2)}) async-start(), calls=%async_computation.27 | async-start | bytes 41943040
  2439.3 1996.9 %reduce-scatter.36.cloned.1.call-start = ((), (), s32[]{:S(2)}) async-start(), calls=%async_computation.28 | async-start | bytes 41943040
  2456.4 2367.4 %all-reduce.7.cloned.1.call-start = ((), (), s32[]{:S(2)}) async-start(), calls=%async_computation.29 | async-start | bytes 60817408 | tf_op jit(solution)/shard_map/psum | solution.py:264
  4449.0 66.8 %all-to-all-start.1 = ((bf16[8,24,2048]{2,1,0:T(8,128)(2,1)}), bf16[8,24,2048]{2,1,0:T(8,128)(2,1)S(1)}, u32[]{:S(2)}, u32[]{:S(2)}) async-start(bf16[8,24,2048]{2,1,0:T(8,128)(2,1)} %bitcast.33), calls=%async_computation.1 | async-start | bytes 1572864 | tf_op jit(solution)/shard_map/all_to_all | solution.py:420
  (64 other events, 1081.5 us)
Sparse Core Ops, SparseCore 0:
  9.6 45.3 all-gather.11
  56.6 44.7 all-gather.15
  103.8 26.6 all-gather.13
  132.8 25.6 all-gather.17
  160.0 146.3 all-gather.19
  307.8 147.8 all-gather.21
  457.3 559.6 all-gather.23
  1018.5 559.5 all-gather.25
  1579.7 559.5 all-gather.27
  2306.0 39.4 reduce-scatter.27
  2349.4 38.4 reduce-scatter.29
  2390.0 41.4 reduce-scatter.21
  2433.9 43.1 reduce-scatter.23
  2479.9 145.9 reduce-scatter.19
  2628.6 145.1 reduce-scatter.25
  2776.1 549.9 reduce-scatter.31
  3328.4 552.7 reduce-scatter.33
  3883.5 552.7 reduce-scatter.35
  4442.1 381.6 all-reduce.6
where the time goes:
time: 4880 us
  waiting for transfers between devices  4280 us (88%)
  matrix products  320 us (7%)
  local copies, waits for them, and re-layouts  95 us (2%)
  other arithmetic  88.9 us (2%)
  blocking collectives  64.6 us (1%)
    unnamed x24, waiting for transfers between devices  1740 us
    all_gather x1, waiting for transfers between devices, collect(): lax.all_gather(weight_g, 'fsdp', axis=0, tiled=True)  554 us
    all_gather x1, waiting for transfers between devices, collect(): lax.all_gather(weight_d, 'fsdp', axis=0, tiled=True)  543 us
    all_gather x1, waiting for transfers between devices, collect(): lax.all_gather(weight_u, 'fsdp', axis=0, tiled=True)  543 us
    reduce_scatter x4, waiting for transfers between devices, settle(): lax.psum_scatter(row_term(left_op, right_op).astype(jnp.bfloat16), 'fsdp'...  317 us
    psum x1, waiting for transfers between devices, settle(): return lax.psum(partial_value, 'ctx').astype(jnp.float32)  303 us
    all_gather x1, waiting for transfers between devices, collect(): lax.all_gather(weight_q, 'fsdp', axis=0, tiled=True)  139 us
  transfers between devices with their start and end apart: 21, of which 18 were waited for; matrix products, arithmetic and copies ran while one was open for 6% of the time, Pallas kernels for 0%

commit v1 on v0

v1 whole, which is shorter than its diff:
```python
import jax
import jax.numpy as jnp
from jax import lax
from jax.experimental import pallas as pl
from jax.experimental.pallas import tpu as pltpu
from jax.sharding import PartitionSpec as P

QUERY_HEADS = 32
KEY_VALUE_HEADS = 8
HEAD_SIZE = 64
EPSILON = 1e-05
ROPE_BASE = 10000000.0
SCORE_SCALE = 0.015625
RESIDUAL_SCALE = 0.22
NEGATIVE_BIG = -1e30
LANES = 128
ROWS = 256
BF16 = jnp.bfloat16
F32 = jnp.float32
VMEM_LIMIT = 56 * 1024 * 1024


def dot_nn(a, b):
    return lax.dot_general(a, b, (((1,), (0,)), ((), ())), preferred_element_type=F32)


def dot_nt(a, b):
    return lax.dot_general(a, b, (((1,), (1,)), ((), ())), preferred_element_type=F32)


def dot_tn(a, b):
    return lax.dot_general(a, b, (((0,), (0,)), ((), ())), preferred_element_type=F32)


def swap_halves(x):
    lane = lax.broadcasted_iota(jnp.int32, x.shape, 1)
    first = lax.rem(lane, HEAD_SIZE) < HEAD_SIZE // 2
    return jnp.where(first, pltpu.roll(x, LANES - HEAD_SIZE // 2, 1), pltpu.roll(x, HEAD_SIZE // 2, 1))


def low_half(shape):
    return lax.broadcasted_iota(jnp.int32, shape, 1) < HEAD_SIZE


def mask_bias(first_len, row0, rows, cols):
    query = row0 + lax.broadcasted_iota(jnp.int32, (rows, cols), 0)
    key = lax.broadcasted_iota(jnp.int32, (rows, cols), 1)
    start = jnp.where(query >= first_len, first_len, 0)
    return jnp.where((key <= query) & (key >= start), 0.0, NEGATIVE_BIG)


def attention_forward_kernel(length_ref, q_ref, kv_ref, cos_ref, sin_ref, out_ref, q_out, k_out, v_out, lse_ref):
    pair = pl.program_id(0)
    tokens = q_ref.shape[0]
    cos, sin = cos_ref[...], sin_ref[...]

    @pl.when(pair == 0)
    def _():
        kv = kv_ref[...]
        turned = pltpu.roll(kv, HEAD_SIZE, 1)
        low = low_half(kv.shape)
        k = jnp.where(low, kv, turned)
        k_out[...] = (k * cos + swap_halves(k) * sin).astype(BF16)
        v_out[...] = jnp.where(low, turned, kv).astype(BF16)

    q = q_ref[...]
    q_out[...] = ((q * cos + swap_halves(q) * sin) * SCORE_SCALE).astype(BF16)
    first_len = length_ref[0]
    for block in range(tokens // ROWS):
        rows = pl.ds(block * ROWS, ROWS)
        end = (block + 1) * ROWS
        bias = mask_bias(first_len, block * ROWS, ROWS, end)
        query = q_out[rows, :]
        low = low_half(query.shape)
        keys, values = k_out[:end, :], v_out[:end, :]
        parts = []
        for half in range(2):
            chosen = low if half == 0 else jnp.logical_not(low)
            scores = dot_nt(jnp.where(chosen, query, jnp.zeros_like(query)), keys) + bias
            top = jnp.max(scores, axis=-1, keepdims=True)
            weights = jnp.exp(scores - top)
            total = jnp.sum(weights, axis=-1, keepdims=True)
            probs = (weights * (1.0 / total)).astype(BF16)
            parts.append(dot_nn(probs, values))
            lse_ref[0, rows, half : half + 1] = top + jnp.log(total)
        out_ref[rows, :] = jnp.where(low_half(parts[0].shape), parts[0], parts[1]).astype(BF16)


def attention_forward(qkv, cos, sin, lengths, heads):
    tokens = qkv.shape[0]
    pairs = heads // 2
    return pl.pallas_call(
        attention_forward_kernel,
        grid=(pairs,),
        in_specs=[
            pl.BlockSpec(memory_space=pltpu.SMEM),
            pl.BlockSpec((tokens, LANES), lambda j: (0, j)),
            pl.BlockSpec((tokens, LANES), lambda j: (0, pairs)),
            pl.BlockSpec((tokens, LANES), lambda j: (0, 0)),
            pl.BlockSpec((tokens, LANES), lambda j: (0, 0)),
        ],
        out_specs=[
            pl.BlockSpec((tokens, LANES), lambda j: (0, j)),
            pl.BlockSpec((tokens, LANES), lambda j: (0, j)),
            pl.BlockSpec((tokens, LANES), lambda j: (0, 0)),
            pl.BlockSpec((tokens, LANES), lambda j: (0, 0)),
            pl.BlockSpec((1, tokens, LANES), lambda j: (j, 0, 0)),
        ],
        out_shape=[
            jax.ShapeDtypeStruct((tokens, pairs * LANES), BF16),
            jax.ShapeDtypeStruct((tokens, pairs * LANES), BF16),
            jax.ShapeDtypeStruct((tokens, LANES), BF16),
            jax.ShapeDtypeStruct((tokens, LANES), BF16),
            jax.ShapeDtypeStruct((pairs, tokens, LANES), F32),
        ],
        compiler_params=pltpu.CompilerParams(vmem_limit_bytes=VMEM_LIMIT),
        cost_estimate=pl.CostEstimate(
            flops=4 * tokens * tokens * LANES * heads // 2,
            bytes_accessed=12 * tokens * pairs * LANES,
            transcendentals=tokens * tokens * heads // 2,
        ),
        name="attend",
    )(lengths, qkv, qkv, cos, sin)


def attention_backward_kernel(length_ref, g_ref, q_ref, k_ref, v_ref, lse_ref, cos_ref, sin_ref, dq_ref, dkv_ref, dk_sum, dv_sum):
    pair = pl.program_id(0)
    tokens = q_ref.shape[0]

    @pl.when(pair == 0)
    def _():
        dk_sum[...] = jnp.zeros_like(dk_sum)
        dv_sum[...] = jnp.zeros_like(dv_sum)

    first_len = length_ref[0]
    for block in range(tokens // ROWS):
        rows = pl.ds(block * ROWS, ROWS)
        end = (block + 1) * ROWS
        bias = mask_bias(first_len, block * ROWS, ROWS, end)
        query, grad = q_ref[rows, :], g_ref[rows, :]
        low = low_half(query.shape)
        keys, values = k_ref[:end, :], v_ref[:end, :]
        parts = []
        for half in range(2):
            chosen = low if half == 0 else jnp.logical_not(low)
            own_query = jnp.where(chosen, query, jnp.zeros_like(query))
            own_grad = jnp.where(chosen, grad, jnp.zeros_like(grad))
            scores = dot_nt(own_query, keys) + bias
            probs = jnp.exp(scores - lse_ref[0, rows, half : half + 1])
            prob_grad = dot_nt(own_grad, values)
            delta = jnp.sum(probs * prob_grad, axis=-1, keepdims=True)
            score_grad = (probs * (prob_grad - delta)).astype(BF16)
            parts.append(dot_nn(score_grad, keys))
            dk_sum[:end, :] += dot_tn(score_grad, own_query)
            dv_sum[:end, :] += dot_tn(probs.astype(BF16), own_grad)
        dq = jnp.where(low_half(parts[0].shape), parts[0], parts[1]) * SCORE_SCALE
        dq_ref[rows, :] = (dq * cos_ref[rows, :] - swap_halves(dq) * sin_ref[rows, :]).astype(BF16)

    @pl.when(pair == pl.num_programs(0) - 1)
    def _():
        dk = dk_sum[...]
        dk = dk + pltpu.roll(dk, HEAD_SIZE, 1)
        dk = dk * cos_ref[...] - swap_halves(dk) * sin_ref[...]
        dv = dv_sum[...]
        dv = dv + pltpu.roll(dv, HEAD_SIZE, 1)
        dkv_ref[...] = jnp.where(low_half(dk.shape), dk, dv).astype(BF16)


def attention_backward(grads, q_rot, k_rot, v_rows, lse, cos, sin, lengths):
    tokens = q_rot.shape[0]
    pairs = q_rot.shape[1] // LANES
    one = pl.BlockSpec((tokens, LANES), lambda j: (0, 0))
    each = pl.BlockSpec((tokens, LANES), lambda j: (0, j))
    return pl.pallas_call(
        attention_backward_kernel,
        grid=(pairs,),
        in_specs=[
            pl.BlockSpec(memory_space=pltpu.SMEM),
            each,
            each,
            one,
            one,
            pl.BlockSpec((1, tokens, LANES), lambda j: (j, 0, 0)),
            one,
            one,
        ],
        out_specs=[each, one],
        out_shape=[
            jax.ShapeDtypeStruct((tokens, pairs * LANES), BF16),
            jax.ShapeDtypeStruct((tokens, LANES), BF16),
        ],
        scratch_shapes=[pltpu.VMEM((tokens, LANES), F32), pltpu.VMEM((tokens, LANES), F32)],
        compiler_params=pltpu.CompilerParams(vmem_limit_bytes=VMEM_LIMIT),
        cost_estimate=pl.CostEstimate(
            flops=10 * tokens * tokens * LANES * pairs,
            bytes_accessed=12 * tokens * pairs * LANES,
            transcendentals=tokens * tokens * pairs,
        ),
        name="attend_back",
    )(lengths, grads, q_rot, k_rot, v_rows, lse, cos, sin)


def own_columns(array, index, width):
    return lax.dynamic_slice_in_dim(array, index * width, width, axis=1)


def local(
    tokens,
    lengths,
    deal,
    attn_gain,
    query_weight,
    key_matrix,
    value_matrix,
    out_weight,
    mlp_gain,
    gate_weight,
    up_weight,
    down_weight,
    cotangent,
):
    n_ctx = lax.axis_size("ctx")
    n_fsdp = lax.axis_size("fsdp")
    me = lax.axis_index("ctx")
    plane = lax.axis_index("fsdp")
    per_device, width = tokens.shape[1], tokens.shape[2]
    total = per_device * n_ctx
    block_rows = per_device // n_ctx
    heads = QUERY_HEADS // n_ctx
    sharing = n_ctx // KEY_VALUE_HEADS
    own_width = width // n_ctx
    ff = gate_weight.shape[1]
    slab = ff // (n_fsdp * n_ctx)
    own_ff = slab * n_fsdp
    rows_shard = query_weight.shape[0]

    kv_head = me // sharing
    qkv_shard = jnp.concatenate(
        [
            own_columns(query_weight, me, heads * HEAD_SIZE),
            own_columns(key_matrix, kv_head, HEAD_SIZE),
            own_columns(value_matrix, kv_head, HEAD_SIZE),
        ],
        axis=1,
    )
    w_qkv = lax.all_gather(qkv_shard, "fsdp", axis=0, tiled=True)
    gains = lax.all_gather(jnp.stack([attn_gain, mlp_gain]), "fsdp", axis=1, tiled=True).astype(F32)
    w_out = lax.all_gather(own_columns(out_weight, me, own_width), "fsdp", axis=0, tiled=True)

    def ff_columns(array):
        picked = lax.dynamic_index_in_dim(
            array.reshape(rows_shard, n_fsdp, n_ctx, slab), me, 2, keepdims=False
        )
        return picked.reshape(rows_shard, own_ff)

    w_gate = lax.all_gather(ff_columns(gate_weight), "fsdp", axis=0, tiled=True)
    w_up = lax.all_gather(ff_columns(up_weight), "fsdp", axis=0, tiled=True)
    w_down = lax.all_gather(
        lax.dynamic_slice_in_dim(down_weight, me * slab, slab, axis=0), "fsdp", axis=0, tiled=True
    )

    first_len = lengths[0, 0]
    given = jnp.arange(total, dtype=jnp.int32)
    position = given - jnp.where(given >= first_len, first_len, 0)
    freq_index = jnp.arange(HEAD_SIZE // 2, dtype=F32)
    inverse = ROPE_BASE ** (-2.0 * freq_index / HEAD_SIZE)
    angles = position.astype(F32)[:, None] * inverse[None, :]
    cos, sin = jnp.cos(angles), jnp.sin(angles)
    cos_table = jnp.concatenate([cos, cos, cos, cos], axis=1)
    sin_table = jnp.concatenate([-sin, sin, -sin, sin], axis=1)

    deal_rows = deal[0]
    slot_ids = jnp.arange(n_ctx, dtype=jnp.int32)
    dealt_of_given = (deal_rows * n_ctx + slot_ids[:, None]).reshape(-1)
    matched = deal_rows[:, :, None] == slot_ids[None, None, :]
    source_slot = jnp.sum(jnp.where(matched, slot_ids[None, :, None], 0), axis=1)
    given_of_dealt = (slot_ids[:, None] * n_ctx + source_slot).T.reshape(-1)

    def reorder(array, table):
        blocks = array.reshape(n_ctx * n_ctx, block_rows, array.shape[1])
        return jnp.take(blocks, table, axis=0).reshape(array.shape)

    x = lax.all_gather(tokens[0], "ctx", axis=0, tiled=True).astype(F32)
    grad_result = reorder(lax.all_gather(cotangent[0], "ctx", axis=0, tiled=True), dealt_of_given)
    r1 = lax.rsqrt(jnp.mean(x * x, axis=-1, keepdims=True) + EPSILON)
    normed = (x * r1 * gains[0]).astype(BF16)
    qkv = dot_nn(normed, w_qkv)
    attended, q_rot, k_rot, v_rows, lse = attention_forward(qkv, cos_table, sin_table, lengths[0], heads)
    attended_all = lax.all_gather(attended, "ctx", axis=1, tiled=True)
    hidden_own = own_columns(x, me, own_width) + RESIDUAL_SCALE * dot_nn(attended_all, w_out)
    hidden = lax.all_gather(hidden_own.astype(BF16), "ctx", axis=1, tiled=True).astype(F32)
    r2 = lax.rsqrt(jnp.mean(hidden * hidden, axis=-1, keepdims=True) + EPSILON)
    normed2 = (hidden * r2 * gains[1]).astype(BF16)
    gate = dot_nn(normed2, w_gate)
    up = dot_nn(normed2, w_up)
    sig = jax.nn.sigmoid(gate)
    mixed = (gate * sig * up).astype(BF16)

    mlp_grad = (RESIDUAL_SCALE * grad_result.astype(F32)).astype(BF16)

    def settle(left, right):
        return lax.psum_scatter(dot_tn(left, right).astype(BF16), "fsdp", scatter_dimension=0, tiled=True)

    down_part = settle(mixed, mlp_grad)
    mixed_grad = dot_nt(mlp_grad, w_down)
    gate_rows_grad = (mixed_grad * up * sig * (1.0 + gate * (1.0 - sig))).astype(BF16)
    up_rows_grad = (mixed_grad * gate * sig).astype(BF16)
    gate_part = settle(normed2, gate_rows_grad)
    up_part = settle(normed2, up_rows_grad)
    normed2_grad = dot_nt(gate_rows_grad, w_gate) + dot_nt(up_rows_grad, w_up)
    weighted2 = normed2_grad * gains[1]
    mlp_gain_part = jnp.sum(normed2_grad * hidden * r2, axis=0)
    hidden_part = r2 * weighted2 - hidden * r2**3 * jnp.mean(weighted2 * hidden, axis=-1, keepdims=True)
    hidden_grad = lax.psum_scatter(
        hidden_part.astype(BF16), "ctx", scatter_dimension=1, tiled=True
    ).astype(F32) + own_columns(grad_result, me, own_width).astype(F32)
    branch_grad = (RESIDUAL_SCALE * hidden_grad).astype(BF16)
    out_part = settle(attended_all, branch_grad)
    attended_grad = lax.psum_scatter(
        dot_nt(branch_grad, w_out).astype(BF16), "ctx", scatter_dimension=1, tiled=True
    )
    dq, dkv = attention_backward(attended_grad, q_rot, k_rot, v_rows, lse, cos_table, sin_table, lengths[0])
    dqkv = jnp.concatenate([dq, dkv], axis=1)
    qkv_part = settle(normed, dqkv)
    normed_grad = dot_nt(dqkv, w_qkv)
    weighted1 = normed_grad * gains[0]
    attn_gain_part = jnp.sum(normed_grad * x * r1, axis=0)
    token_part = r1 * weighted1 - x * r1**3 * jnp.mean(weighted1 * x, axis=-1, keepdims=True)
    spread = jnp.zeros((total, width), F32)
    spread = lax.dynamic_update_slice_in_dim(spread, hidden_grad, me * own_width, axis=1)
    token_grad = lax.psum_scatter(
        (token_part + spread).astype(BF16), "ctx", scatter_dimension=0, tiled=True
    ).astype(F32)[None]

    mixed_dealt = reorder(mixed, given_of_dealt)
    hidden_spread = jnp.zeros((total, width), F32)
    hidden_spread = lax.dynamic_update_slice_in_dim(
        hidden_spread, reorder(hidden_own, given_of_dealt), me * own_width, axis=1
    )
    result_part = hidden_spread + RESIDUAL_SCALE * dot_nn(mixed_dealt, w_down)
    activations = lax.psum_scatter(result_part.astype(BF16), "ctx", scatter_dimension=0, tiled=True)[None]

    def whole(part):
        return lax.all_gather(part, "ctx", axis=0, tiled=False)

    qkv_all = whole(qkv_part).astype(F32)
    split = heads * HEAD_SIZE
    query_grad = qkv_all[:, :, :split].transpose(1, 0, 2).reshape(rows_shard, width)

    def shared_heads(pieces):
        pieces = pieces.reshape(KEY_VALUE_HEADS, sharing, rows_shard, HEAD_SIZE).sum(axis=1)
        return pieces.transpose(1, 0, 2).reshape(rows_shard, KEY_VALUE_HEADS * HEAD_SIZE)

    key_grad = shared_heads(qkv_all[:, :, split : split + HEAD_SIZE])
    value_grad = shared_heads(qkv_all[:, :, split + HEAD_SIZE :])
    out_grad = whole(out_part).transpose(1, 0, 2).reshape(rows_shard, width).astype(F32)

    def ff_whole(part):
        pieces = whole(part).reshape(n_ctx, rows_shard, n_fsdp, slab)
        return pieces.transpose(1, 2, 0, 3).reshape(rows_shard, ff).astype(F32)

    gate_grad = ff_whole(gate_part)
    up_grad = ff_whole(up_part)
    down_grad = whole(down_part).reshape(n_ctx * slab, width).astype(F32)
    gain_totals = lax.psum(jnp.stack([attn_gain_part, mlp_gain_part]), ("ctx", "fsdp"))
    own_gains = lax.dynamic_slice_in_dim(gain_totals, plane * rows_shard, rows_shard, axis=1)
    return (
        activations,
        token_grad,
        own_gains[0],
        query_grad,
        key_grad,
        value_grad,
        out_grad,
        own_gains[1],
        gate_grad,
        up_grad,
        down_grad,
    )


def solution(mesh):
    rows = P("fsdp", None)
    block = P("fsdp", "ctx", None)
    gain = P("fsdp")
    return jax.shard_map(
        local,
        mesh=mesh,
        in_specs=(block, rows, P("fsdp", None, None), gain, rows, rows, rows, rows, gain, rows, rows, rows, block),
        out_specs=(block, block, gain, rows, rows, rows, rows, gain, rows, rows, rows),
        check_vma=False,
    )
```

time: 4880 us -> 1390 us (0.28)
  waiting for transfers between devices: 4280 us -> 842 us
  matrix products: 320 us -> 157 us
  local copies, waits for them, and re-layouts: 95 us -> 170 us
    unnamed x24 -> x23, waiting for transfers between devices: 1740 us -> 2.05 us
    all_gather x9 -> x14, waiting for transfers between devices: 1920 us -> 377 us  [the longest x1 75.9 us: local(): w_gate = lax.all_gather(ff_columns(gate_weight), 'fsdp', axis=0, tiled=True)]
    psum x1 -> x0, waiting for transfers between devices: 303 us -> none  [settle(): return lax.psum(partial_value, 'ctx').astype(jnp.float32)]
    dot_general x42 -> x15, matrix products: 320 us -> 157 us  [the longest x5 60.1 us: dot_nt(): lax.dot_general(a, b, (((1,), (1,)), ((), ())), preferred_element_type=F32)]
    reduce_scatter x4 -> x9, waiting for transfers between devices: 317 us -> 463 us  [the longest x5 267 us: settle(): lax.psum_scatter(dot_tn(left, right).astype(BF16), 'fsdp', scatter_dimens...]
    convert_element_type x2 -> x5, local copies, waits for them, and re-layouts: 2.1 us -> 67.1 us  [the longest x4 64.5 us: ff_whole(): return pieces.transpose(1, 2, 0, 3).reshape(rows_shard, ff).astype(F32)]
  transfers between devices with their start and end apart: 21 -> 23, of which waited for: 18 -> 17; matrix products, arithmetic and copies ran while one was open for 6% -> 26% of each run, Pallas kernels for 0% -> 3%
where the time goes in v1:
time: 1390 us; the launch traced here: 1380 us
  waiting for transfers between devices  842 us (61%)
  local copies, waits for them, and re-layouts  170 us (12%)
  matrix products  157 us (11%)
  other arithmetic  93.5 us (7%)
  blocking collectives  52.7 us (4%)
  Pallas kernels  46.4 us (3%)
  between operations  15 us (1%)
    reduce_scatter x5, waiting for transfers between devices, settle(): lax.psum_scatter(dot_tn(left, right).astype(BF16), 'fsdp', scatter_dimens...  267 us
    all_gather x1, waiting for transfers between devices, local(): w_gate = lax.all_gather(ff_columns(gate_weight), 'fsdp', axis=0, tiled=True)  75.9 us
    unnamed x48, local copies, waits for them, and re-layouts  71.8 us
    all_gather x1, waiting for transfers between devices, local(): lax.all_gather(lax.dynamic_slice_in_dim(down_weight, me * slab, slab, axi...  69.5 us
    all_gather x1, waiting for transfers between devices, local(): w_up = lax.all_gather(ff_columns(up_weight), 'fsdp', axis=0, tiled=True)  69.5 us
    convert_element_type x4, local copies, waits for them, and re-layouts, ff_whole(): return pieces.transpose(1, 2, 0, 3).reshape(rows_shard, ff).astype(F32)  64.5 us
    reduce_scatter x1, waiting for transfers between devices, local(): lax.psum_scatter(result_part.astype(BF16), 'ctx', scatter_dimension=0, ti...  63.6 us
    reduce_scatter x1, waiting for transfers between devices, local(): lax.psum_scatter(hidden_part.astype(BF16), 'ctx', scatter_dimension=1, ti...  62.9 us
  transfers between devices with their start and end apart: 23, of which 17 were waited for; matrix products, arithmetic and copies ran while one was open for 26% of the time, Pallas kernels for 3%

profile of v1, /device:TPU:9, one launch (start us, length us, event | category | flops | bytes accessed | tf_op | source)
XLA Modules:
  0.0 1378.4 jit_solution(1266848024063394680)
XLA Ops:
  29.8 27.3 %all-gather.36.cloned.1.call-done = bf16[1,1536,2048]{2,1,0:T(8,128)(2,1)} async-done(((bf16[1,192,2048]{2,1,0:T(8,128)(2,1)}), bf16[1,1536,2048]{2,1,0:T(8,128)(2,1)}) %all-gather.36.cloned.1.call-update) | async-done | bytes 6291472 | tf_op jit(solution)/shard_map/all_gather | solution.py:283
  61.8 32.9 %all-gather.22.cloned.1.call-done = bf16[2048,384]{1,0:T(8,128)(2,1)} async-done(((bf16[512,384]{1,0:T(8,128)(2,1)}), bf16[2048,384]{1,0:T(8,128)(2,1)}) %all-gather.22.cloned.1.call-update) | async-done | bytes 1572880 | tf_op jit(solution)/shard_map/all_gather | solution.py:246
  102.8 19.5 %attend.1 = (bf16[1536,256]{1,0:T(8,128)(2,1)}, bf16[1536,256]{1,0:T(8,128)(2,1)}, bf16[1536,128]{1,0:T(8,128)(2,1)}, bf16[1536,128]{1,0:T(8,128)(2,1)}, f32[2,1536,128]{2,1,0:T(8,128)}) custom-call(s32[2]{0:T(128)} %bitcast.145, f32[1536,384]{1,0:T(8,128)} %fusion.22.q_ref.kv_ref, f32[1536,384]{1,0:T(8,128)} %fusion.22.q_ref.kv_ref, ...), custom_call_target="tpu_custom_call" | custom-call | flops 2415919104 | bytes 4718592 | tf_op jit(solution)/shard_map/attend/pallas_call | solution.py:92
  132.1 41.8 %all-gather.24.cloned.1.call-done = bf16[1536,2048]{1,0:T(8,128)(2,1)} async-done(((bf16[1536,256]{1,0:T(8,128)(2,1)}), bf16[1536,2048]{1,0:T(8,128)(2,1)}) %all-gather.24.cloned.1.call-update) | async-done | bytes 6291472 | tf_op jit(solution)/shard_map/all_gather | solution.py:289
  233.7 36.4 %all-gather.28.cloned.1.call-done = bf16[1536,2048]{1,0:T(8,128)(2,1)} async-done(((bf16[1536,256]{1,0:T(8,128)(2,1)}), bf16[1536,2048]{1,0:T(8,128)(2,1)}) %all-gather.28.cloned.1.call-update) | async-done | bytes 6291472 | tf_op jit(solution)/shard_map/all_gather | solution.py:291
  274.2 75.9 %all-gather.30.cloned.1.call-done = bf16[2048,1024]{0,1:T(8,128)(2,1)} async-done(((bf16[512,1024]{0,1:T(8,128)(2,1)}), bf16[2048,1024]{0,1:T(8,128)(2,1)}) %all-gather.30.cloned.1.call-update) | async-done | bytes 4194320 | tf_op jit(solution)/shard_map/all_gather | solution.py:256
  362.1 69.5 %all-gather.32.cloned.1.call-done = bf16[2048,1024]{0,1:T(8,128)(2,1)} async-done(((bf16[512,1024]{0,1:T(8,128)(2,1)}), bf16[2048,1024]{0,1:T(8,128)(2,1)}) %all-gather.32.cloned.1.call-update) | async-done | bytes 4194320 | tf_op jit(solution)/shard_map/all_gather | solution.py:257
  443.5 69.5 %all-gather.34.cloned.1.call-done = bf16[1024,2048]{1,0:T(8,128)(2,1)} async-done(((bf16[256,2048]{1,0:T(8,128)(2,1)}), bf16[1024,2048]{1,0:T(8,128)(2,1)}) %all-gather.34.cloned.1.call-update) | async-done | bytes 4194320 | tf_op jit(solution)/shard_map/all_gather | solution.py:258
  513.1 17.7 %multiply_convert_fusion.1 = (bf16[1536,1024]{1,0:T(8,128)(2,1)S(1)}, bf16[1536,1024]{1,0:T(8,128)(2,1)}, bf16[1536,1024]{1,0:T(8,128)(2,1)}) fusion(f32[1536,1024]{1,0:T(8,128)} %fusion.38, f32[1536,1024]{1,0:T(8,128)} %fusion.36, bf16[1024,2048]{1,0:T(8,128)(2,1)} %all-gather.34.cloned.1.call-done, bf16[1536,2048]{1,0:T(8,128)(2,1)} %bitcast_select_fusion), kind=kOutput, calls=%fused_computation.35 | convolution fusion | flops 6477053952 | bytes 32505856 | tf_op jit(solution)/shard_map/dot_general | solution.py:28
  543.8 16.3 %fusion.8 = (f32[2048]{0:T(1024)S(1)}, f32[1536]{0:T(1024)S(1)}, f32[1536,2048]{1,0:T(8,128)}) fusion(bf16[1536,2048]{1,0:T(8,128)(2,1)} %all-gather.28.cloned.1.call-done, f32[1536]{0:T(1024)S(1)} %get-tuple-element.86, f32[2048]{0:T(1024)S(1)} %bitcast.135, f32[1536,2048]{1,0:T(8,128)} %fusion.44, bf16[1536,1024]{1,0:T(8,128)(2,1)S(1)} %get-tuple-element.73, ...), kind=kOutput, calls=%fused_computation.16 | convolution fusion | flops 6467613184 | bytes 38825984 | tf_op jit(solution)/shard_map/dot_general | solution.py:28
  569.5 62.9 %reduce-scatter.12.cloned.1.call-done = bf16[1536,256]{1,0:T(8,128)(2,1)} async-done(((bf16[1536,2048]{1,0:T(8,128)(2,1)}), bf16[1536,256]{1,0:T(8,128)(2,1)}) %reduce-scatter.12.cloned.1.call-update) | async-done | bytes 786448 | tf_op jit(solution)/shard_map/reduce_scatter | solution.py:314
  680.2 20.2 %reduce-scatter.14.cloned.1.call-done.g_ref = bf16[1536,256]{1,0:T(8,128)(2,1)} async-done(((bf16[1536,2048]{1,0:T(8,128)(2,1)}), bf16[1536,256]{1,0:T(8,128)(2,1)}) %reduce-scatter.14.cloned.1.call-update) | async-done | bytes 786448 | tf_op jit(solution)/shard_map/reduce_scatter | solution.py:319
  700.4 26.9 %attend_back.1 = (bf16[1536,256]{1,0:T(8,128)(2,1)}, bf16[1536,128]{1,0:T(8,128)(2,1)}) custom-call(s32[2]{0:T(128)} %bitcast.146, bf16[1536,256]{1,0:T(8,128)(2,1)} %reduce-scatter.14.cloned.1.call-done.g_ref, bf16[1536,256]{1,0:T(8,128)(2,1)} %get-tuple-element.19.q_ref, bf16[1536,128]{1,0:T(8,128)(2,1)} %get-tuple-element.20.k_ref, ...), custom_call_target="tpu_custom_call" | custom-call | flops 6039797760 | bytes 4718592 | tf_op jit(solution)/shard_map/attend_back/pallas_call | solution.py:174
  737.9 70.8 %reduce-scatter.22.cloned.1.call-done = bf16[512,1024]{1,0:T(8,128)(2,1)} async-done(((bf16[2048,1024]{1,0:T(8,128)(2,1)}), bf16[512,1024]{1,0:T(8,128)(2,1)}) %reduce-scatter.22.cloned.1.call-update) | async-done | bytes 1048592 | tf_op jit(solution)/shard_map/reduce_scatter | solution.py:302
  808.8 80.0 %reduce-scatter.24.cloned.1.call-done = bf16[512,1024]{1,0:T(8,128)(2,1)} async-done(((bf16[2048,1024]{1,0:T(8,128)(2,1)}), bf16[512,1024]{1,0:T(8,128)(2,1)}) %reduce-scatter.24.cloned.1.call-update) | async-done | bytes 1048592 | tf_op jit(solution)/shard_map/reduce_scatter | solution.py:302
  888.8 80.0 %reduce-scatter.26.cloned.1.call-done = bf16[256,2048]{1,0:T(8,128)(2,1)} async-done(((bf16[1024,2048]{1,0:T(8,128)(2,1)}), bf16[256,2048]{1,0:T(8,128)(2,1)}) %reduce-scatter.26.cloned.1.call-update) | async-done | bytes 1048592 | tf_op jit(solution)/shard_map/reduce_scatter | solution.py:302
  968.9 36.6 %reduce-scatter.18.cloned.1.call-done = bf16[512,384]{1,0:T(8,128)(2,1)} async-done(((bf16[2048,384]{1,0:T(8,128)(2,1)}), bf16[512,384]{1,0:T(8,128)(2,1)}) %reduce-scatter.18.cloned.1.call-update) | async-done | bytes 393232 | tf_op jit(solution)/shard_map/reduce_scatter | solution.py:302
  1068.5 42.8 %psum.7 = f32[2,2048]{1,0:T(2,128)S(1)} all-reduce(f32[2,2048]{1,0:T(2,128)S(1)} %pad_maximum_fusion.3), channel_id=1, replica_groups=mesh['ctx'=8,'fsdp'=4] {'ctx','fsdp'}, use_global_device_ids=true, to_apply=%region_11.12 | all-reduce | flops 4096 | bytes 32768 | tf_op jit(solution)/shard_map/psum | solution.py:365
  1112.0 16.7 %reshape.242 = f32[8,512,4,256]{3,2,1,0:T(4,128)} reshape(bf16[4096,1024]{1,0:T(8,128)(2,1)} %all-gather.44.cloned.1.call-done) | data formatting | bytes 25165824 | tf_op jit(solution)/shard_map/convert_element_type | solution.py:360
  1143.9 18.0 %copy.77 = f32[64,8,32,256]{3,1,2,0:T(8,128)} copy(f32[64,8,32,256]{3,2,1,0:T(8,128)S(1)} %bitcast.108) | data formatting | bytes 33554432
  1161.9 16.5 %reshape.243 = f32[8,512,4,256]{3,2,1,0:T(4,128)} reshape(bf16[4096,1024]{1,0:T(8,128)(2,1)} %all-gather.46.cloned.1.call-done) | data formatting | bytes 25165824 | tf_op jit(solution)/shard_map/convert_element_type | solution.py:360
  1194.5 18.3 %copy.78 = f32[64,8,32,256]{3,1,2,0:T(8,128)} copy(f32[64,8,32,256]{3,2,1,0:T(8,128)S(1)} %bitcast.110) | data formatting | bytes 33554432
  1256.1 49.2 %reduce-scatter.16.cloned.1.call-done = bf16[192,2048]{1,0:T(8,128)(2,1)} async-done(((bf16[1536,2048]{1,0:T(8,128)(2,1)}), bf16[192,2048]{1,0:T(8,128)(2,1)}) %reduce-scatter.16.cloned.1.call-update) | async-done | bytes 786448 | tf_op jit(solution)/shard_map/reduce_scatter | solution.py:331
  1307.7 63.6 %reduce-scatter.10.cloned.1.call-done = bf16[192,2048]{1,0:T(8,128)(2,1)} async-done(((bf16[1536,2048]{1,0:T(8,128)(2,1)}), bf16[192,2048]{1,0:T(8,128)(2,1)}) %reduce-scatter.10.cloned.1.call-update) | async-done | bytes 786448 | tf_op jit(solution)/shard_map/reduce_scatter | solution.py:341
  (182 shorter events, 354.1 us)
Async XLA Ops:
  7.2 49.9 %all-gather.36.cloned.1.call-start = ((), (), s32[]{:S(2)}) async-start(), calls=%async_computation.25 | async-start | bytes 7077888 | tf_op jit(solution)/shard_map/all_gather | solution.py:283
  7.9 86.7 %all-gather.22.cloned.1.call-start = ((), (), s32[]{:S(2)}) async-start(), calls=%async_computation.9 | async-start | bytes 1966080 | tf_op jit(solution)/shard_map/all_gather | solution.py:246
  10.8 121.2 %all-gather.26.cloned.1.call-start = ((), (), s32[]{:S(2)}) async-start(), calls=%async_computation.11 | async-start | bytes 1310720 | tf_op jit(solution)/shard_map/all_gather | solution.py:248
  12.6 161.2 %all-gather.24.cloned.1.call-start = ((), (), s32[]{:S(2)}) async-start(), calls=%async_computation.10 | async-start | bytes 7077888 | tf_op jit(solution)/shard_map/all_gather | solution.py:289
  122.3 98.8 %all-gather.38.cloned.1.call-start = ((), (), s32[]{:S(2)}) async-start(), calls=%async_computation.26 | async-start | bytes 7077888 | tf_op jit(solution)/shard_map/all_gather | solution.py:284
  122.9 147.2 %all-gather.28.cloned.1.call-start = ((), (), s32[]{:S(2)}) async-start(), calls=%async_computation.12 | async-start | bytes 7077888 | tf_op jit(solution)/shard_map/all_gather | solution.py:291
  180.6 169.5 %all-gather.30.cloned.1.call-start = ((), (), s32[]{:S(2)}) async-start(), calls=%async_computation.13 | async-start | bytes 5242880 | tf_op jit(solution)/shard_map/all_gather | solution.py:256
  194.9 236.6 %all-gather.32.cloned.1.call-start = ((), (), s32[]{:S(2)}) async-start(), calls=%async_computation.14 | async-start | bytes 5242880 | tf_op jit(solution)/shard_map/all_gather | solution.py:257
  209.3 303.7 %all-gather.34.cloned.1.call-start = ((), (), s32[]{:S(2)}) async-start(), calls=%async_computation.15 | async-start | bytes 5242880 | tf_op jit(solution)/shard_map/all_gather | solution.py:258
  211.7 420.8 %reduce-scatter.12.cloned.1.call-start = ((), (), s32[]{:S(2)}) async-start(), calls=%async_computation.17 | async-start | bytes 7077888 | tf_op jit(solution)/shard_map/reduce_scatter | solution.py:314
  569.5 130.9 %reduce-scatter.14.cloned.1.call-start = ((), (), s32[]{:S(2)}) async-start(), calls=%async_computation.18 | async-start | bytes 7077888 | tf_op jit(solution)/shard_map/reduce_scatter | solution.py:319
  638.5 98.8 %reduce-scatter.20.cloned.1.call-start = ((), (), s32[]{:S(2)}) async-start(), calls=%async_computation.21 | async-start | bytes 1310720 | tf_op jit(solution)/shard_map/reduce_scatter | solution.py:302
  644.4 164.3 %reduce-scatter.22.cloned.1.call-start = ((), (), s32[]{:S(2)}) async-start(), calls=%async_computation.22 | async-start | bytes 5242880 | tf_op jit(solution)/shard_map/reduce_scatter | solution.py:302
  656.9 231.8 %reduce-scatter.24.cloned.1.call-start = ((), (), s32[]{:S(2)}) async-start(), calls=%async_computation.23 | async-start | bytes 5242880 | tf_op jit(solution)/shard_map/reduce_scatter | solution.py:302
  668.7 300.1 %reduce-scatter.26.cloned.1.call-start = ((), (), s32[]{:S(2)}) async-start(), calls=%async_computation.24 | async-start | bytes 5242880 | tf_op jit(solution)/shard_map/reduce_scatter | solution.py:302
  680.1 325.3 %reduce-scatter.18.cloned.1.call-start = ((), (), s32[]{:S(2)}) async-start(), calls=%async_computation.20 | async-start | bytes 1966080 | tf_op jit(solution)/shard_map/reduce_scatter | solution.py:302
  737.3 326.6 %all-gather.42.cloned.1.call-start = ((), (), s32[]{:S(2)}) async-start(), calls=%async_computation.28 | async-start | bytes 2359296 | tf_op jit(solution)/shard_map/all_gather | solution.py:344
  737.8 374.1 %all-gather.44.cloned.1.call-start = ((), (), s32[]{:S(2)}) async-start(), calls=%async_computation.29 | async-start | bytes 9437184 | tf_op jit(solution)/shard_map/all_gather | solution.py:344
  808.7 353.2 %all-gather.46.cloned.1.call-start = ((), (), s32[]{:S(2)}) async-start(), calls=%async_computation.30 | async-start | bytes 9437184 | tf_op jit(solution)/shard_map/all_gather | solution.py:344
  888.8 324.0 %all-gather.48.cloned.1.call-start = ((), (), s32[]{:S(2)}) async-start(), calls=%async_computation.31 | async-start | bytes 9437184 | tf_op jit(solution)/shard_map/all_gather | solution.py:344
  968.9 271.7 %all-gather.40.cloned.1.call-start = ((), (), s32[]{:S(2)}) async-start(), calls=%async_computation.27 | async-start | bytes 3538944 | tf_op jit(solution)/shard_map/all_gather | solution.py:344
  1005.5 299.8 %reduce-scatter.16.cloned.1.call-start = ((), (), s32[]{:S(2)}) async-start(), calls=%async_computation.19 | async-start | bytes 7077888 | tf_op jit(solution)/shard_map/reduce_scatter | solution.py:331
  1033.1 338.3 %reduce-scatter.10.cloned.1.call-start = ((), (), s32[]{:S(2)}) async-start(), calls=%async_computation.16 | async-start | bytes 7077888 | tf_op jit(solution)/shard_map/reduce_scatter | solution.py:341
  1248.3 123.1 %copy-start.1 = (bf16[512,2048]{1,0:T(8,128)(2,1)S(1)}, bf16[512,2048]{1,0:T(8,128)(2,1)}, u32[]{:S(2)}) copy-start(bf16[512,2048]{1,0:T(8,128)(2,1)} %param.17) | copy-start | bytes 6291460
  (18 other events, 351.5 us)
Sparse Core Ops, SparseCore 0:
  9.9 47.0 all-gather.35
  59.2 35.4 all-gather.21
  96.8 27.7 all-gather.25
  126.9 46.8 all-gather.23
  175.5 45.5 all-gather.37
  223.4 46.6 all-gather.27
  272.2 77.8 all-gather.29
  352.2 79.2 all-gather.31
  433.7 79.2 all-gather.33
  569.6 62.7 reduce-scatter.11
  638.6 61.7 reduce-scatter.13
  703.1 25.1 reduce-scatter.19
  731.2 77.4 reduce-scatter.21
  811.4 77.2 reduce-scatter.23
  891.5 77.2 reduce-scatter.25
  971.6 33.8 reduce-scatter.17
  1007.2 29.2 all-gather.41
  1038.2 55.0 all-gather.43
  1095.2 54.9 all-gather.45
  1151.9 54.3 all-gather.47
  1208.2 32.3 all-gather.39
  1243.9 61.3 reduce-scatter.15
  1309.6 61.7 reduce-scatter.9

commit v2 on v1

--- a/solution.py
+++ b/solution.py
@@ -200,8 +200,311 @@
     )(lengths, grads, q_rot, k_rot, v_rows, lse, cos, sin)
 
 
+def row_block(width):
+    return pl.BlockSpec((ROWS, width), lambda i: (i, 0))
+
+
+def fixed(*shape):
+    return pl.BlockSpec(shape, lambda i: (0,) * len(shape))
+
+
+def params():
+    return pltpu.CompilerParams(vmem_limit_bytes=VMEM_LIMIT)
+
+
+def cost(flops, *arrays):
+    moved = sum(a.size * a.dtype.itemsize for a in arrays)
+    return pl.CostEstimate(flops=flops, bytes_accessed=moved, transcendentals=0)
+
+
+def project_kernel(x_ref, gain_ref, w_ref, normed_ref, qkv_ref):
+    x = x_ref[...].astype(F32)
+    r1 = lax.rsqrt(jnp.mean(x * x, axis=-1, keepdims=True) + EPSILON)
+    normed = (x * r1 * gain_ref[...]).astype(BF16)
+    normed_ref[...] = normed
+    qkv_ref[...] = dot_nn(normed, w_ref[...])
+
+
+def project(x, gain, w_qkv):
+    total, width = x.shape
+    columns = w_qkv.shape[1]
+    out_shape = [jax.ShapeDtypeStruct((total, width), BF16), jax.ShapeDtypeStruct((total, columns), F32)]
+    return pl.pallas_call(
+        project_kernel,
+        grid=(total // ROWS,),
+        in_specs=[row_block(width), fixed(1, width), fixed(width, columns)],
+        out_specs=[row_block(width), row_block(columns)],
+        out_shape=out_shape,
+        compiler_params=params(),
+        cost_estimate=cost(2 * total * width * columns, x, w_qkv, *out_shape),
+        name="project",
+    )(x, gain, w_qkv)
+
+
+def out_kernel(me_ref, x_ref, att_ref, w_ref, hidden_ref):
+    own_width = hidden_ref.shape[1]
+    acc = jnp.zeros(hidden_ref.shape, F32)
+    for c in range(att_ref.shape[0]):
+        acc += dot_nn(att_ref[c], w_ref[c])
+    start = pl.multiple_of(me_ref[0] * own_width, LANES)
+    x = x_ref[:, pl.ds(start, own_width)].astype(F32)
+    hidden_ref[...] = (x + RESIDUAL_SCALE * acc).astype(BF16)
+
+
+def out_projection(me, x, att_all, w_out):
+    n, total, own = att_all.shape
+    width = x.shape[1]
+    own_width = w_out.shape[1]
+    w_heads = w_out.reshape(n, own, own_width)
+    out_shape = jax.ShapeDtypeStruct((total, own_width), BF16)
+    return pl.pallas_call(
+        out_kernel,
+        grid=(total // ROWS,),
+        in_specs=[
+            pl.BlockSpec(memory_space=pltpu.SMEM),
+            row_block(width),
+            pl.BlockSpec((n, ROWS, own), lambda i: (0, i, 0)),
+            fixed(n, own, own_width),
+        ],
+        out_specs=row_block(own_width),
+        out_shape=out_shape,
+        compiler_params=params(),
+        cost_estimate=cost(2 * total * width * own_width, x, att_all, w_out, out_shape),
+        name="out_projection",
+    )(me, x, att_all, w_heads)
+
+
+def join(ref):
+    return jnp.concatenate([ref[c].astype(F32) for c in range(ref.shape[0])], axis=1)
+
+
+def mlp_kernel(hidden_ref, gain_ref, gate_ref, up_ref, normed_ref, a_ref, b_ref, mixed_ref):
+    hidden = join(hidden_ref)
+    r2 = lax.rsqrt(jnp.mean(hidden * hidden, axis=-1, keepdims=True) + EPSILON)
+    normed = (hidden * r2 * gain_ref[...]).astype(BF16)
+    normed_ref[...] = normed
+    gate = dot_nn(normed, gate_ref[...])
+    up = dot_nn(normed, up_ref[...])
+    sig = jax.nn.sigmoid(gate)
+    silu = gate * sig
+    mixed_ref[...] = (silu * up).astype(BF16)
+    b_ref[...] = silu.astype(BF16)
+    a_ref[...] = (up * sig * (1.0 + gate * (1.0 - sig))).astype(BF16)
+
+
+def mlp_forward(hidden_all, gain, w_gate, w_up):
+    n, total, own = hidden_all.shape
+    width, own_ff = w_gate.shape
+    wide = jax.ShapeDtypeStruct((total, width), BF16)
+    narrow = jax.ShapeDtypeStruct((total, own_ff), BF16)
+    return pl.pallas_call(
+        mlp_kernel,
+        grid=(total // ROWS,),
+        in_specs=[
+            pl.BlockSpec((n, ROWS, own), lambda i: (0, i, 0)),
+            fixed(1, width),
+            fixed(width, own_ff),
+            fixed(width, own_ff),
+        ],
+        out_specs=[row_block(width), row_block(own_ff), row_block(own_ff), row_block(own_ff)],
+        out_shape=[wide, narrow, narrow, narrow],
+        compiler_params=params(),
+        cost_estimate=cost(4 * total * width * own_ff, hidden_all, w_gate, w_up, wide, narrow, narrow, narrow),
+        name="mlp_forward",
+    )(hidden_all, gain, w_gate, w_up)
+
+
+def mlp_back_kernel(
+    grad_ref, a_ref, b_ref, hidden_ref, gain_ref, gate_ref, up_ref, down_ref, ggrad_ref, ugrad_ref, part_ref, gain_out
+):
+    mixed_grad = dot_nt(grad_ref[...], down_ref[...])
+    ggrad = (mixed_grad * a_ref[...].astype(F32)).astype(BF16)
+    ugrad = (mixed_grad * b_ref[...].astype(F32)).astype(BF16)
+    ggrad_ref[...] = ggrad
+    ugrad_ref[...] = ugrad
+    normed_grad = dot_nt(ggrad, gate_ref[...]) + dot_nt(ugrad, up_ref[...])
+    hidden = join(hidden_ref)
+    r2 = lax.rsqrt(jnp.mean(hidden * hidden, axis=-1, keepdims=True) + EPSILON)
+    gain_part = jnp.sum(normed_grad * (hidden * r2), axis=0, keepdims=True)
+
+    @pl.when(pl.program_id(0) == 0)
+    def _():
+        gain_out[...] = jnp.zeros_like(gain_out)
+
+    gain_out[...] += gain_part
+    weighted = normed_grad * gain_ref[...]
+    mean = jnp.mean(weighted * hidden, axis=-1, keepdims=True)
+    part = r2 * weighted - hidden * (r2 * r2 * r2 * mean)
+    own = part_ref.shape[2]
+    for c in range(part_ref.shape[0]):
+        part_ref[c] = part[:, c * own : (c + 1) * own].astype(BF16)
+
+
+def mlp_backward(mlp_grad, a, b, hidden_all, gain, w_gate, w_up, w_down):
+    n, total, own = hidden_all.shape
+    width, own_ff = w_gate.shape
+    narrow = jax.ShapeDtypeStruct((total, own_ff), BF16)
+    planes = pl.BlockSpec((n, ROWS, own), lambda i: (0, i, 0))
+    return pl.pallas_call(
+        mlp_back_kernel,
+        grid=(total // ROWS,),
+        in_specs=[
+            row_block(width),
+            row_block(own_ff),
+            row_block(own_ff),
+            planes,
+            fixed(1, width),
+            fixed(width, own_ff),
+            fixed(width, own_ff),
+            fixed(own_ff, width),
+        ],
+        out_specs=[row_block(own_ff), row_block(own_ff), planes, fixed(1, width)],
+        out_shape=[narrow, narrow, jax.ShapeDtypeStruct((n, total, own), BF16), jax.ShapeDtypeStruct((1, width), F32)],
+        compiler_params=params(),
+        cost_estimate=cost(6 * total * width * own_ff, mlp_grad, hidden_all, hidden_all, w_gate, w_up, w_down, a, b, a, b),
+        name="mlp_backward",
+    )(mlp_grad, a, b, hidden_all, gain, w_gate, w_up, w_down)
+
+
+def branch_kernel(part_ref, grad_ref, w_ref, hidden_ref, branch_ref, out_ref):
+    hidden_grad = part_ref[...].astype(F32) + grad_ref[...].astype(F32)
+    hidden_ref[...] = hidden_grad
+    branch = (RESIDUAL_SCALE * hidden_grad).astype(BF16)
+    branch_ref[...] = branch
+    own = out_ref.shape[2]
+    for c in range(out_ref.shape[0]):
+        out_ref[c] = dot_nt(branch, w_ref[c]).astype(BF16)
+
+
+def branch_backward(hidden_part, grad_own, w_out, n):
+    total, own_width = hidden_part.shape
+    own = w_out.shape[0] // n
+    w_heads = w_out.reshape(n, own, own_width)
+    return pl.pallas_call(
+        branch_kernel,
+        grid=(total // ROWS,),
+        in_specs=[row_block(own_width), row_block(own_width), fixed(n, own, own_width)],
+        out_specs=[row_block(own_width), row_block(own_width), pl.BlockSpec((n, ROWS, own), lambda i: (0, i, 0))],
+        out_shape=[
+            jax.ShapeDtypeStruct((total, own_width), F32),
+            jax.ShapeDtypeStruct((total, own_width), BF16),
+            jax.ShapeDtypeStruct((n, total, own), BF16),
+        ],
+        compiler_params=params(),
+        cost_estimate=cost(2 * total * own_width * own * n, hidden_part, hidden_part, hidden_part, w_out),
+        name="branch_backward",
+    )(hidden_part, grad_own, w_heads)
+
+
+def token_kernel(me_ref, dq_ref, dkv_ref, w_ref, x_ref, gain_ref, hidden_ref, part_ref, gain_out):
+    split = dq_ref.shape[1]
+    normed_grad = dot_nt(dq_ref[...], w_ref[:, :split]) + dot_nt(dkv_ref[...], w_ref[:, split:])
+    x = x_ref[...].astype(F32)
+    r1 = lax.rsqrt(jnp.mean(x * x, axis=-1, keepdims=True) + EPSILON)
+
+    @pl.when(pl.program_id(0) == 0)
+    def _():
+        gain_out[...] = jnp.zeros_like(gain_out)
+
+    gain_out[...] += jnp.sum(normed_grad * (x * r1), axis=0, keepdims=True)
+    weighted = normed_grad * gain_ref[...]
+    mean = jnp.mean(weighted * x, axis=-1, keepdims=True)
+    part = r1 * weighted - x * (r1 * r1 * r1 * mean)
+    own_width = hidden_ref.shape[1]
+    for c in range(part.shape[1] // own_width):
+        piece = part[:, c * own_width : (c + 1) * own_width]
+        piece = piece + jnp.where(me_ref[0] == c, hidden_ref[...], 0.0)
+        part_ref[:, c * own_width : (c + 1) * own_width] = piece.astype(BF16)
+
+
+def token_backward(me, dq, dkv, w_qkv, x, gain, hidden_grad):
+    total, width = x.shape
+    own_width = hidden_grad.shape[1]
+    return pl.pallas_call(
+        token_kernel,
+        grid=(total // ROWS,),
+        in_specs=[
+            pl.BlockSpec(memory_space=pltpu.SMEM),
+            row_block(dq.shape[1]),
+            row_block(dkv.shape[1]),
+            fixed(*w_qkv.shape),
+            row_block(width),
+            fixed(1, width),
+            row_block(own_width),
+        ],
+        out_specs=[row_block(width), fixed(1, width)],
+        out_shape=[jax.ShapeDtypeStruct((total, width), BF16), jax.ShapeDtypeStruct((1, width), F32)],
+        compiler_params=params(),
+        cost_estimate=cost(2 * total * width * w_qkv.shape[1], x, x, w_qkv, dq, dkv, hidden_grad),
+        name="token_backward",
+    )(me, dq, dkv, w_qkv, x, gain, hidden_grad)
+
+
+def spread_kernel(in_ref, out_ref):
+    out_ref[...] = in_ref[0].astype(F32)
+
+
+def spread_columns(pieces, slab, groups):
+    n, rows, _ = pieces.shape
+    out_shape = jax.ShapeDtypeStruct((rows, groups * n * slab), F32)
+    return pl.pallas_call(
+        spread_kernel,
+        grid=(groups, n),
+        in_specs=[pl.BlockSpec((1, rows, slab), lambda f, c: (c, 0, f))],
+        out_specs=pl.BlockSpec((rows, slab), lambda f, c: (0, f * n + c)),
+        out_shape=out_shape,
+        compiler_params=params(),
+        cost_estimate=cost(0, pieces, out_shape),
+        name="spread_columns",
+    )(pieces)
+
+
+def gather_planes(shards):
+    n_planes = lax.axis_size("fsdp")
+    plane = lax.axis_index("fsdp")
+    ups, downs = [], []
+    up = down = shards
+    for step in range(n_planes - 1):
+        up = lax.ppermute(up, "fsdp", [(q, q + 1) for q in range(step, n_planes - 1)])
+        down = lax.ppermute(down, "fsdp", [(q + 1, q) for q in range(n_planes - 1 - step)])
+        ups.append(up)
+        downs.append(down)
+
+    def order(p):
+        return lambda own, ups, downs: jnp.concatenate([ups[p - 1 - j] if j < p else own if j == p else downs[j - p - 1] for j in range(n_planes)], axis=0)
+
+    return lax.switch(plane, [order(p) for p in range(n_planes)], shards, ups, downs), ups
+
+
+def settle_planes(part):
+    n_planes = lax.axis_size("fsdp")
+    plane = lax.axis_index("fsdp")
+    rows = part.shape[0] // n_planes
+
+    def block(index):
+        return lax.dynamic_slice_in_dim(part, jnp.clip(index, 0, n_planes - 1) * rows, rows, axis=0)
+
+    def chain(index_of, pair):
+        got = None
+        for step in range(n_planes - 1):
+            value = block(index_of(step))
+            if got is not None:
+                value = value + got
+            got = lax.ppermute(value, "fsdp", [pair(q) for q in range(step + 1)])
+        return got
+
+    last = n_planes - 1
+    from_below = chain(lambda s: last - s + plane, lambda q: (q, q + 1))
+    from_above = chain(lambda s: s - last + plane, lambda q: (last - q, last - q - 1))
+    return (block(plane).astype(F32) + from_below.astype(F32) + from_above.astype(F32)).astype(part.dtype)
+
+
 def own_columns(array, index, width):
     return lax.dynamic_slice_in_dim(array, index * width, width, axis=1)
+
+
+def after(value, *others):
+    return lax.optimization_barrier((value, *others))[0]
 
 
 def local(
@@ -222,7 +525,7 @@
     n_ctx = lax.axis_size("ctx")
     n_fsdp = lax.axis_size("fsdp")
     me = lax.axis_index("ctx")
-    plane = lax.axis_index("fsdp")
+    me_array = me.astype(jnp.int32).reshape(1)
     per_device, width = tokens.shape[1], tokens.shape[2]
     total = per_device * n_ctx
     block_rows = per_device // n_ctx
@@ -231,32 +534,32 @@
     own_width = width // n_ctx
     ff = gate_weight.shape[1]
     slab = ff // (n_fsdp * n_ctx)
-    own_ff = slab * n_fsdp
     rows_shard = query_weight.shape[0]
 
     kv_head = me // sharing
-    qkv_shard = jnp.concatenate(
+    split = heads * HEAD_SIZE
+    attn_shard = jnp.concatenate(
         [
-            own_columns(query_weight, me, heads * HEAD_SIZE),
+            own_columns(query_weight, me, split),
             own_columns(key_matrix, kv_head, HEAD_SIZE),
             own_columns(value_matrix, kv_head, HEAD_SIZE),
+            own_columns(out_weight, me, own_width),
         ],
         axis=1,
     )
-    w_qkv = lax.all_gather(qkv_shard, "fsdp", axis=0, tiled=True)
-    gains = lax.all_gather(jnp.stack([attn_gain, mlp_gain]), "fsdp", axis=1, tiled=True).astype(F32)
-    w_out = lax.all_gather(own_columns(out_weight, me, own_width), "fsdp", axis=0, tiled=True)
 
     def ff_columns(array):
-        picked = lax.dynamic_index_in_dim(
-            array.reshape(rows_shard, n_fsdp, n_ctx, slab), me, 2, keepdims=False
-        )
-        return picked.reshape(rows_shard, own_ff)
-
-    w_gate = lax.all_gather(ff_columns(gate_weight), "fsdp", axis=0, tiled=True)
-    w_up = lax.all_gather(ff_columns(up_weight), "fsdp", axis=0, tiled=True)
-    w_down = lax.all_gather(
-        lax.dynamic_slice_in_dim(down_weight, me * slab, slab, axis=0), "fsdp", axis=0, tiled=True
+        return jnp.concatenate([own_columns(array, f * n_ctx + me, slab) for f in range(n_fsdp)], axis=1)
+
+    gain_shard = jnp.stack([attn_gain, mlp_gain]).reshape(1, 2 * rows_shard)
+    gains_all, _ = gather_planes(gain_shard)
+    gains = gains_all.reshape(n_fsdp, 2, rows_shard).transpose(1, 0, 2).reshape(2, 1, width).astype(F32)
+    w_attn, first = gather_planes(attn_shard)
+    w_qkv, w_out = w_attn[:, : split + 2 * HEAD_SIZE], w_attn[:, split + 2 * HEAD_SIZE :]
+    w_gate, second = gather_planes(after(ff_columns(gate_weight), first[0]))
+    w_up, second = gather_planes(after(ff_columns(up_weight), first[0]))
+    w_down, _ = gather_planes(
+        after(lax.dynamic_slice_in_dim(down_weight, me * slab, slab, axis=0), second[1])
     )
 
     first_len = lengths[0, 0]
@@ -278,92 +581,85 @@
 
     def reorder(array, table):
         blocks = array.reshape(n_ctx * n_ctx, block_rows, array.shape[1])
-        return jnp.take(blocks, table, axis=0).reshape(array.shape)
-
-    x = lax.all_gather(tokens[0], "ctx", axis=0, tiled=True).astype(F32)
-    grad_result = reorder(lax.all_gather(cotangent[0], "ctx", axis=0, tiled=True), dealt_of_given)
-    r1 = lax.rsqrt(jnp.mean(x * x, axis=-1, keepdims=True) + EPSILON)
-    normed = (x * r1 * gains[0]).astype(BF16)
-    qkv = dot_nn(normed, w_qkv)
+        return jnp.take(blocks, table, axis=0, mode="clip").reshape(array.shape)
+
+    x = lax.all_gather(tokens[0], "ctx", axis=0, tiled=True)
+    normed, qkv = project(x, gains[0], w_qkv)
     attended, q_rot, k_rot, v_rows, lse = attention_forward(qkv, cos_table, sin_table, lengths[0], heads)
-    attended_all = lax.all_gather(attended, "ctx", axis=1, tiled=True)
-    hidden_own = own_columns(x, me, own_width) + RESIDUAL_SCALE * dot_nn(attended_all, w_out)
-    hidden = lax.all_gather(hidden_own.astype(BF16), "ctx", axis=1, tiled=True).astype(F32)
-    r2 = lax.rsqrt(jnp.mean(hidden * hidden, axis=-1, keepdims=True) + EPSILON)
-    normed2 = (hidden * r2 * gains[1]).astype(BF16)
-    gate = dot_nn(normed2, w_gate)
-    up = dot_nn(normed2, w_up)
-    sig = jax.nn.sigmoid(gate)
-    mixed = (gate * sig * up).astype(BF16)
+    attended_all = lax.all_gather(attended, "ctx", axis=0, tiled=False)
+    hidden_own = out_projection(me_array, x, attended_all, w_out)
+    hidden_all = lax.all_gather(hidden_own, "ctx", axis=0, tiled=False)
+    cotangent_all = lax.all_gather(after(cotangent[0], attended), "ctx", axis=0, tiled=True)
+    grad_result = reorder(cotangent_all, dealt_of_given)
+    normed2, a, b, mixed = mlp_forward(hidden_all, gains[1], w_gate, w_up)
 
     mlp_grad = (RESIDUAL_SCALE * grad_result.astype(F32)).astype(BF16)
 
     def settle(left, right):
-        return lax.psum_scatter(dot_tn(left, right).astype(BF16), "fsdp", scatter_dimension=0, tiled=True)
+        return settle_planes(dot_tn(left, right).astype(BF16))
 
     down_part = settle(mixed, mlp_grad)
-    mixed_grad = dot_nt(mlp_grad, w_down)
-    gate_rows_grad = (mixed_grad * up * sig * (1.0 + gate * (1.0 - sig))).astype(BF16)
-    up_rows_grad = (mixed_grad * gate * sig).astype(BF16)
-    gate_part = settle(normed2, gate_rows_grad)
-    up_part = settle(normed2, up_rows_grad)
-    normed2_grad = dot_nt(gate_rows_grad, w_gate) + dot_nt(up_rows_grad, w_up)
-    weighted2 = normed2_grad * gains[1]
-    mlp_gain_part = jnp.sum(normed2_grad * hidden * r2, axis=0)
-    hidden_part = r2 * weighted2 - hidden * r2**3 * jnp.mean(weighted2 * hidden, axis=-1, keepdims=True)
-    hidden_grad = lax.psum_scatter(
-        hidden_part.astype(BF16), "ctx", scatter_dimension=1, tiled=True
-    ).astype(F32) + own_columns(grad_result, me, own_width).astype(F32)
-    branch_grad = (RESIDUAL_SCALE * hidden_grad).astype(BF16)
-    out_part = settle(attended_all, branch_grad)
-    attended_grad = lax.psum_scatter(
-        dot_nt(branch_grad, w_out).astype(BF16), "ctx", scatter_dimension=1, tiled=True
+    ggrad, ugrad, hidden_part, mlp_gain_part = mlp_backward(
+        mlp_grad, a, b, hidden_all, gains[1], w_gate, w_up, w_down
+    )
+    hidden_sum = lax.psum_scatter(hidden_part, "ctx", scatter_dimension=0, tiled=False)
+    gate_part = settle(normed2, ggrad)
+    up_part = settle(normed2, ugrad)
+    hidden_grad, branch_grad, attended_part = branch_backward(
+        hidden_sum, own_columns(grad_result, me, own_width), w_out, n_ctx
+    )
+    attended_grad = lax.psum_scatter(attended_part, "ctx", scatter_dimension=0, tiled=False)
+    out_part = settle_planes(
+        jnp.einsum("ctk,to->cko", attended_all, branch_grad, preferred_element_type=F32)
+        .astype(BF16)
+        .reshape(width, own_width)
     )
     dq, dkv = attention_backward(attended_grad, q_rot, k_rot, v_rows, lse, cos_table, sin_table, lengths[0])
-    dqkv = jnp.concatenate([dq, dkv], axis=1)
-    qkv_part = settle(normed, dqkv)
-    normed_grad = dot_nt(dqkv, w_qkv)
-    weighted1 = normed_grad * gains[0]
-    attn_gain_part = jnp.sum(normed_grad * x * r1, axis=0)
-    token_part = r1 * weighted1 - x * r1**3 * jnp.mean(weighted1 * x, axis=-1, keepdims=True)
-    spread = jnp.zeros((total, width), F32)
-    spread = lax.dynamic_update_slice_in_dim(spread, hidden_grad, me * own_width, axis=1)
-    token_grad = lax.psum_scatter(
-        (token_part + spread).astype(BF16), "ctx", scatter_dimension=0, tiled=True
-    ).astype(F32)[None]
-
-    mixed_dealt = reorder(mixed, given_of_dealt)
-    hidden_spread = jnp.zeros((total, width), F32)
-    hidden_spread = lax.dynamic_update_slice_in_dim(
-        hidden_spread, reorder(hidden_own, given_of_dealt), me * own_width, axis=1
-    )
-    result_part = hidden_spread + RESIDUAL_SCALE * dot_nn(mixed_dealt, w_down)
-    activations = lax.psum_scatter(result_part.astype(BF16), "ctx", scatter_dimension=0, tiled=True)[None]
+    qkv_part = settle(normed, jnp.concatenate([dq, dkv], axis=1))
+    token_part, attn_gain_part = token_backward(me_array, dq, dkv, w_qkv, x, gains[0], hidden_grad)
+    token_grad = lax.psum_scatter(token_part, "ctx", scatter_dimension=0, tiled=True).astype(F32)[None]
+
+    both = jnp.concatenate([mixed, (hidden_own.astype(F32) * (1.0 / RESIDUAL_SCALE)).astype(BF16)], axis=1)
+    column = lax.broadcasted_iota(jnp.int32, (own_width, width), 1) - me * own_width
+    place = (column == lax.broadcasted_iota(jnp.int32, (own_width, width), 0)).astype(BF16)
+    result_part = RESIDUAL_SCALE * dot_nn(reorder(both, given_of_dealt), jnp.concatenate([w_down, place], axis=0))
+    activations = lax.psum_scatter(
+        after(result_part.astype(BF16), attended_grad), "ctx", scatter_dimension=0, tiled=True
+    )[None]
 
     def whole(part):
         return lax.all_gather(part, "ctx", axis=0, tiled=False)
 
-    qkv_all = whole(qkv_part).astype(F32)
-    split = heads * HEAD_SIZE
-    query_grad = qkv_all[:, :, :split].transpose(1, 0, 2).reshape(rows_shard, width)
+    down_grad = whole(down_part).reshape(n_ctx * slab, width).astype(F32)
+    if slab % LANES == 0:
+        gate_grad = spread_columns(whole(gate_part), slab, n_fsdp)
+        up_grad = spread_columns(whole(up_part), slab, n_fsdp)
+    else:
+
+        def ff_whole(part):
+            pieces = whole(part).reshape(n_ctx, rows_shard, n_fsdp, slab)
+            return pieces.transpose(1, 2, 0, 3).reshape(rows_shard, ff).astype(F32)
+
+        gate_grad = ff_whole(gate_part)
+        up_grad = ff_whole(up_part)
+    out_grad = spread_columns(whole(out_part), own_width, 1)
+    qkv_all = whole(qkv_part)
+    query_grad = spread_columns(qkv_all, split, 1)
 
     def shared_heads(pieces):
-        pieces = pieces.reshape(KEY_VALUE_HEADS, sharing, rows_shard, HEAD_SIZE).sum(axis=1)
+        pieces = pieces.astype(F32).reshape(KEY_VALUE_HEADS, sharing, rows_shard, HEAD_SIZE).sum(axis=1)
         return pieces.transpose(1, 0, 2).reshape(rows_shard, KEY_VALUE_HEADS * HEAD_SIZE)
 
     key_grad = shared_heads(qkv_all[:, :, split : split + HEAD_SIZE])
     value_grad = shared_heads(qkv_all[:, :, split + HEAD_SIZE :])
-    out_grad = whole(out_part).transpose(1, 0, 2).reshape(rows_shard, width).astype(F32)
-
-    def ff_whole(part):
-        pieces = whole(part).reshape(n_ctx, rows_shard, n_fsdp, slab)
-        return pieces.transpose(1, 2, 0, 3).reshape(rows_shard, ff).astype(F32)
-
-    gate_grad = ff_whole(gate_part)
-    up_grad = ff_whole(up_part)
-    down_grad = whole(down_part).reshape(n_ctx * slab, width).astype(F32)
-    gain_totals = lax.psum(jnp.stack([attn_gain_part, mlp_gain_part]), ("ctx", "fsdp"))
-    own_gains = lax.dynamic_slice_in_dim(gain_totals, plane * rows_shard, rows_shard, axis=1)
+
+    gain_parts = jnp.concatenate([attn_gain_part, mlp_gain_part], axis=0)
+    step = 1
+    while step < n_ctx:
+        gain_parts = gain_parts + lax.ppermute(gain_parts, "ctx", [(c, c ^ step) for c in range(n_ctx)])
+        step *= 2
+    gain_rows = gain_parts.reshape(2, n_fsdp, rows_shard).transpose(1, 0, 2).reshape(n_fsdp, 2 * rows_shard)
+    own_gains = settle_planes(gain_rows).reshape(2, rows_shard)
     return (
         activations,
         token_grad,

time: 1390 us -> 1210 us (0.87)
  waiting for transfers between devices: 842 us -> 581 us
  starting transfers between devices: 1.34 us -> 241 us
  Pallas kernels: 46.4 us -> 192 us
  local copies, waits for them, and re-layouts: 170 us -> 35 us
  matrix products: 157 us -> 50.6 us
  blocking collectives: 52.7 us -> 0 us
    ppermute x0 -> x69, waiting for transfers between devices: none -> 452 us  [the longest x36 255 us: chain(): got = lax.ppermute(value, 'fsdp', [pair(q) for q in range(step + 1)])]
    reduce_scatter x9 -> x4, waiting for transfers between devices: 463 us -> 78.9 us  [the longest x1 58.9 us: local(): lax.psum_scatter(hidden_part, 'ctx', scatter_dimension=0, tiled=False)]
    all_gather x9 -> x4, waiting for transfers between devices: 361 us -> 49.2 us  [the longest x1 49.2 us: local(): attended_all = lax.all_gather(attended, 'ctx', axis=0, tiled=False)]
    ppermute x0 -> x69, starting transfers between devices: none -> 240 us  [the longest x36 131 us: chain(): got = lax.ppermute(value, 'fsdp', [pair(q) for q in range(step + 1)])]
    pallas_call x0 -> x10, Pallas kernels: none -> 147 us  [the longest x4 53.4 us: spread_columns(): pl.pallas_call(spread_kernel, grid=(groups, n), in_specs=[pl.BlockSpec((1...]
    convert_element_type x5 -> x0, local copies, waits for them, and re-layouts: 67.1 us -> none  [the longest x4 64.5 us: ff_whole(): return pieces.transpose(1, 2, 0, 3).reshape(rows_shard, ff).astype(F32)]
    unnamed x48 -> x56, local copies, waits for them, and re-layouts: 71.8 us -> 7.22 us
    dot_general x5 -> x1, matrix products: 60.1 us -> 1.85 us  [local(): jnp.einsum('ctk,to->cko', attended_all, branch_grad, preferred_element_ty...]
  transfers between devices with their start and end apart: 23 -> 82, of which waited for: 17 -> 42; matrix products, arithmetic and copies ran while one was open for 26% -> 14% of each run, Pallas kernels for 3% -> 9%
where the time goes in v2:
time: 1210 us; the launch traced here: 1200 us
  waiting for transfers between devices  581 us (48%)
  starting transfers between devices  241 us (20%)
  Pallas kernels  192 us (16%)
  other arithmetic  83.7 us (7%)
  matrix products  50.6 us (4%)
  local copies, waits for them, and re-layouts  35 us (3%)
  between operations  15.4 us (1%)
    ppermute x36, waiting for transfers between devices, chain(): got = lax.ppermute(value, 'fsdp', [pair(q) for q in range(step + 1)])  255 us
    ppermute x36, starting transfers between devices, chain(): got = lax.ppermute(value, 'fsdp', [pair(q) for q in range(step + 1)])  131 us
    ppermute x15, waiting for transfers between devices, gather_planes(): lax.ppermute(down, 'fsdp', [(q + 1, q) for q in range(n_planes - 1 - step)])  101 us
    ppermute x15, waiting for transfers between devices, gather_planes(): lax.ppermute(up, 'fsdp', [(q, q + 1) for q in range(step, n_planes - 1)])  91.5 us
    reduce_scatter x1, waiting for transfers between devices, local(): lax.psum_scatter(hidden_part, 'ctx', scatter_dimension=0, tiled=False)  58.9 us
    pallas_call x4, Pallas kernels, spread_columns(): pl.pallas_call(spread_kernel, grid=(groups, n), in_specs=[pl.BlockSpec((1...  53.4 us
    all_gather x1, waiting for transfers between devices, local(): attended_all = lax.all_gather(attended, 'ctx', axis=0, tiled=False)  49.2 us
    ppermute x15, starting transfers between devices, gather_planes(): lax.ppermute(up, 'fsdp', [(q, q + 1) for q in range(step, n_planes - 1)])  44.2 us
  transfers between devices with their start and end apart: 82, of which 42 were waited for; matrix products, arithmetic and copies ran while one was open for 14% of the time, Pallas kernels for 9%

profile of v2, /device:TPU:9, one launch (start us, length us, event | category | flops | bytes accessed | tf_op | source)
XLA Modules:
  0.0 1199.2 jit_solution(17390707711183904375)
XLA Ops:
  78.2 19.2 %attend.1 = (bf16[1536,256]{1,0:T(8,128)(2,1)}, bf16[1536,256]{1,0:T(8,128)(2,1)}, bf16[1536,128]{1,0:T(8,128)(2,1)}, bf16[1536,128]{1,0:T(8,128)(2,1)}, f32[2,1536,128]{2,1,0:T(8,128)}) custom-call(s32[2]{0:T(128)} %bitcast.116, f32[1536,384]{1,0:T(8,128)} %get-tuple-element.328.q_ref.kv_ref, f32[1536,384]{1,0:T(8,128)} %get-tuple-element.328.q_ref.kv_ref, ...), custom_call_target="tpu_custom_call" | custom-call | flops 2415919104 | bytes 4718592 | tf_op jit(solution)/shard_map/attend/pallas_call | solution.py:92
  98.2 49.2 %all-gather.22.cloned.1.call-done = bf16[12288,256]{1,0:T(8,128)(2,1)} async-done(((bf16[1536,256]{1,0:T(8,128)(2,1)}), bf16[12288,256]{1,0:T(8,128)(2,1)}) %all-gather.22.cloned.1.call-update) | async-done | bytes 6291472 | tf_op jit(solution)/shard_map/all_gather | solution.py:589
  163.9 20.1 %collective-permute-done.21 = bf16[512,1024]{1,0:T(8,128)(2,1)S(1)} collective-permute-done((bf16[512,1024]{1,0:T(8,128)(2,1)S(1)}, bf16[512,1024]{1,0:T(8,128)(2,1)S(1)}, u32[]{:S(2)}, u32[]{:S(2)}) %collective-permute-start.21) | collective-permute-done | bytes 1048608 | tf_op jit(solution)/shard_map/ppermute | solution.py:468
  251.1 21.7 %collective-permute-done.27 = bf16[256,2048]{1,0:T(8,128)(2,1)S(1)} collective-permute-done((bf16[256,2048]{1,0:T(8,128)(2,1)S(1)}, bf16[256,2048]{1,0:T(8,128)(2,1)S(1)}, u32[]{:S(2)}, u32[]{:S(2)}) %collective-permute-start.27) | collective-permute-done | bytes 1048608 | tf_op jit(solution)/shard_map/ppermute | solution.py:468
  284.4 19.2 %collective-permute-done.19 = bf16[512,1024]{1,0:T(8,128)(2,1)} collective-permute-done((bf16[512,1024]{1,0:T(8,128)(2,1)S(1)}, bf16[512,1024]{1,0:T(8,128)(2,1)}, u32[]{:S(2)}, u32[]{:S(2)}) %collective-permute-start.19) | collective-permute-done | bytes 1048608 | tf_op jit(solution)/shard_map/ppermute | solution.py:469
  350.2 18.9 %collective-permute-done.20 = bf16[512,1024]{1,0:T(8,128)(2,1)} collective-permute-done((bf16[512,1024]{1,0:T(8,128)(2,1)}, bf16[512,1024]{1,0:T(8,128)(2,1)}, u32[]{:S(2)}, u32[]{:S(2)}) %collective-permute-start.20) | collective-permute-done | bytes 1048608 | tf_op jit(solution)/shard_map/ppermute | solution.py:469
  372.8 18.8 %collective-permute-done.26 = bf16[256,2048]{1,0:T(8,128)(2,1)} collective-permute-done((bf16[256,2048]{1,0:T(8,128)(2,1)}, bf16[256,2048]{1,0:T(8,128)(2,1)}, u32[]{:S(2)}, u32[]{:S(2)}) %collective-permute-start.26) | collective-permute-done | bytes 1048608 | tf_op jit(solution)/shard_map/ppermute | solution.py:469
  412.6 21.4 %mlp_forward.1 = (bf16[1536,2048]{1,0:T(8,128)(2,1)}, bf16[1536,1024]{1,0:T(8,128)(2,1)}, bf16[1536,1024]{1,0:T(8,128)(2,1)}, bf16[1536,1024]{1,0:T(8,128)(2,1)}) custom-call(bf16[8,1536,256]{2,1,0:T(8,128)(2,1)} %bitcast.118, f32[1,2048]{1,0:T(1,128)} %bitcast.111, bf16[2048,1024]{1,0:T(8,128)(2,1)} %get-tuple-element.437.gate_ref, ...), custom_call_target="tpu_custom_call" | custom-call | flops 12884901888 | bytes 30408704 | tf_op jit(solution)/shard_map/mlp_forward/pallas_call | solution.py:300
  434.0 30.9 %mlp_backward.1 = (bf16[1536,1024]{1,0:T(8,128)(2,1)}, bf16[1536,1024]{1,0:T(8,128)(2,1)}, bf16[8,1536,256]{2,1,0:T(8,128)(2,1)}, f32[1,2048]{1,0:T(1,128)}) custom-call(bf16[1536,2048]{1,0:T(8,128)(2,1)} %multiply_convert_fusion.grad_ref, bf16[1536,1024]{1,0:T(8,128)(2,1)} %get-tuple-element.336.a_ref, bf16[1536,1024]{1,0:T(8,128)(2,1)} %get-tuple-element.337.b_ref, ...), custom_call_target="tpu_custom_call" | custom-call | flops 19327352832 | bytes 44040192 | tf_op jit(solution)/shard_map/mlp_backward/pallas_call | solution.py:348
  467.0 58.9 %reduce-scatter.5.cloned.1.call-done = bf16[1,1536,256]{2,1,0:T(8,128)(2,1)} async-done(((bf16[8,1536,256]{2,1,0:T(8,128)(2,1)}), bf16[1,1536,256]{2,1,0:T(8,128)(2,1)}) %reduce-scatter.5.cloned.1.call-update) | async-done | bytes 786448 | tf_op jit(solution)/shard_map/reduce_scatter | solution.py:605
  549.2 27.2 %collective-permute-done.45 = bf16[512,256]{1,0:T(8,128)(2,1)S(1)} collective-permute-done((bf16[512,256]{1,0:T(8,128)(2,1)S(1)}, bf16[512,256]{1,0:T(8,128)(2,1)S(1)}, u32[]{:S(2)}, u32[]{:S(2)}) %collective-permute-start.45) | collective-permute-done | bytes 262176 | tf_op jit(solution)/shard_map/ppermute | solution.py:493
  618.1 25.3 %collective-permute-start.59 = (bf16[512,1024]{1,0:T(8,128)(2,1)S(1)}, bf16[512,1024]{1,0:T(8,128)(2,1)S(1)}, u32[]{:S(2)}, u32[]{:S(2)}) collective-permute-start(bf16[512,1024]{1,0:T(8,128)(2,1)S(1)} %copy-done.16), channel_id=1, source_target_pairs={{0,1},{1,2},{2,3},{4,5},{5,6},{6,7},{8,9},{9,10},{10,11},{12,13},{... | collective-permute-start | bytes 3145736 | tf_op jit(solution)/shard_map/ppermute | solution.py:493
  665.4 20.8 %collective-permute-done.62 = bf16[512,1024]{1,0:T(8,128)(2,1)S(1)} collective-permute-done((bf16[512,1024]{1,0:T(8,128)(2,1)S(1)}, bf16[512,1024]{1,0:T(8,128)(2,1)S(1)}, u32[]{:S(2)}, u32[]{:S(2)}) %collective-permute-start.62) | collective-permute-done | bytes 1048608 | tf_op jit(solution)/shard_map/ppermute | solution.py:493
  700.5 20.6 %collective-permute-done.51 = bf16[512,1024]{1,0:T(8,128)(2,1)S(1)} collective-permute-done((bf16[512,1024]{1,0:T(8,128)(2,1)S(1)}, bf16[512,1024]{1,0:T(8,128)(2,1)S(1)}, u32[]{:S(2)}, u32[]{:S(2)}) %collective-permute-start.51) | collective-permute-done | bytes 1048608 | tf_op jit(solution)/shard_map/ppermute | solution.py:493
  723.4 19.4 %collective-permute-done.52 = bf16[512,1024]{1,0:T(8,128)(2,1)S(1)} collective-permute-done((bf16[512,1024]{1,0:T(8,128)(2,1)S(1)}, bf16[512,1024]{1,0:T(8,128)(2,1)S(1)}, u32[]{:S(2)}, u32[]{:S(2)}) %collective-permute-start.52) | collective-permute-done | bytes 1048608 | tf_op jit(solution)/shard_map/ppermute | solution.py:493
  745.8 22.2 %collective-permute-start.53 = (bf16[512,1024]{1,0:T(8,128)(2,1)S(1)}, bf16[512,1024]{1,0:T(8,128)(2,1)S(1)}, u32[]{:S(2)}, u32[]{:S(2)}) collective-permute-start(bf16[512,1024]{1,0:T(8,128)(2,1)S(1)} %get-tuple-element.401), channel_id=1, source_target_pairs={{0,1},{1,2},{2,3},{4,5},{5,6},{6,7},{8,9},{9,10},{10,11},{12,13},{... | collective-permute-start | bytes 3145736 | tf_op jit(solution)/shard_map/ppermute | solution.py:493
  782.6 19.3 %collective-permute-done.56 = bf16[512,1024]{1,0:T(8,128)(2,1)S(1)} collective-permute-done((bf16[512,1024]{1,0:T(8,128)(2,1)S(1)}, bf16[512,1024]{1,0:T(8,128)(2,1)S(1)}, u32[]{:S(2)}, u32[]{:S(2)}) %collective-permute-start.56) | collective-permute-done | bytes 1048608 | tf_op jit(solution)/shard_map/ppermute | solution.py:493
  834.4 18.7 %collective-permute-done.64 = bf16[256,2048]{1,0:T(8,128)(2,1)S(1)} collective-permute-done((bf16[256,2048]{1,0:T(8,128)(2,1)S(1)}, bf16[256,2048]{1,0:T(8,128)(2,1)S(1)}, u32[]{:S(2)}, u32[]{:S(2)}) %collective-permute-start.64) | collective-permute-done | bytes 1048608 | tf_op jit(solution)/shard_map/ppermute | solution.py:493
  887.3 34.8 %collective-permute-done.68 = bf16[256,2048]{1,0:T(8,128)(2,1)S(1)} collective-permute-done((bf16[256,2048]{1,0:T(8,128)(2,1)S(1)}, bf16[256,2048]{1,0:T(8,128)(2,1)S(1)}, u32[]{:S(2)}, u32[]{:S(2)}) %collective-permute-start.68) | collective-permute-done | bytes 1048608 | tf_op jit(solution)/shard_map/ppermute | solution.py:493
  924.9 26.5 %attend_back.1 = (bf16[1536,256]{1,0:T(8,128)(2,1)}, bf16[1536,128]{1,0:T(8,128)(2,1)}) custom-call(s32[2]{0:T(128)} %bitcast.117, bf16[1536,256]{1,0:T(8,128)(2,1)} %bitcast.120, bf16[1536,256]{1,0:T(8,128)(2,1)} %get-tuple-element.341.q_ref, bf16[1536,128]{1,0:T(8,128)(2,1)} %get-tuple-element.342.k_ref, bf16[1536,128]{1,0:T(8,128)(2,1)} %get-tuple-element.343.v_ref, ...), custom_call_target="tpu_custom_call" | custom-call | flops 6039797760 | bytes 4718592 | tf_op jit(solution)/shard_map/attend_back/pallas_call | solution.py:174
  1043.1 27.6 %collective-permute-start.30 = (f32[2,2048]{1,0:T(2,128)S(1)}, f32[2,2048]{1,0:T(2,128)S(1)}, u32[]{:S(2)}, u32[]{:S(2)}) collective-permute-start(f32[2,2048]{1,0:T(2,128)S(1)} %pad_maximum_fusion.22), channel_id=1, source_target_pairs={{0,4},{4,0},{8,12},{12,8},{16,20},{20,16},{24,28},{28,24},{1,5},{5... | collective-permute-start | bytes 49160 | tf_op jit(solution)/shard_map/ppermute | solution.py:659
  1102.8 20.6 %spread_columns.7 = f32[512,8192]{1,0:T(8,128)} custom-call(bf16[8,512,1024]{2,1,0:T(8,128)(2,1)} %bitcast.77), custom_call_target="tpu_custom_call" | custom-call | bytes 25165824 | tf_op jit(solution)/shard_map/spread_columns/pallas_call | solution.py:450
  1123.3 20.7 %spread_columns.6 = f32[512,8192]{1,0:T(8,128)} custom-call(bf16[8,512,1024]{2,1,0:T(8,128)(2,1)} %bitcast.78), custom_call_target="tpu_custom_call" | custom-call | bytes 25165824 | tf_op jit(solution)/shard_map/spread_columns/pallas_call | solution.py:450
  1172.5 19.9 %reduce-scatter.9.cloned.1.call-done = bf16[192,2048]{1,0:T(8,128)(2,1)} async-done(((bf16[1536,2048]{1,0:T(8,128)(2,1)}), bf16[192,2048]{1,0:T(8,128)(2,1)}) %reduce-scatter.9.cloned.1.call-update) | async-done | bytes 786448 | tf_op jit(solution)/shard_map/reduce_scatter | solution.py:626
  (325 shorter events, 599.2 us)
Async XLA Ops:
  7.2 61.7 %all-gather.20.cloned.1.call-start = ((), (), s32[]{:S(2)}) async-start(), calls=%async_computation.9 | async-start | bytes 7077888 | tf_op jit(solution)/shard_map/all_gather | solution.py:586
  7.9 139.5 %all-gather.22.cloned.1.call-start = ((), (), s32[]{:S(2)}) async-start(), calls=%async_computation.10 | async-start | bytes 7077888 | tf_op jit(solution)/shard_map/all_gather | solution.py:589
  97.4 301.0 %all-gather.18.cloned.1.call-start = ((), (), s32[]{:S(2)}) async-start(), calls=%async_computation.4 | async-start | bytes 7077888 | tf_op jit(solution)/shard_map/all_gather | solution.py:592
  98.2 314.4 %all-gather.24.cloned.1.call-start = ((), (), s32[]{:S(2)}) async-start(), calls=%async_computation.11 | async-start | bytes 7077888 | tf_op jit(solution)/shard_map/all_gather | solution.py:591
  155.4 370.5 %reduce-scatter.5.cloned.1.call-start = ((), (), s32[]{:S(2)}) async-start(), calls=%async_computation.5 | async-start | bytes 7077888 | tf_op jit(solution)/shard_map/reduce_scatter | solution.py:605
  188.1 45.9 %collective-permute-start.12 = (bf16[512,1024]{1,0:T(8,128)(2,1)S(1)}, bf16[512,1024]{1,0:T(8,128)(2,1)S(1)}, u32[]{:S(2)}, u32[]{:S(2)}) collective-permute-start(bf16[512,1024]{1,0:T(8,128)(2,1)S(1)} %pad_maximum_fusion.17), channel_id=1, source_target_pairs={{1,0},{2,1},{3,2},{5,4},{6,5},{7,6},{9,8},{10,9},{11,10},{13,12},{... | collective-permute-start | bytes 3145736 | tf_op jit(solution)/shard_map/ppermute | solution.py:469
  234.1 47.1 %collective-permute-start.13 = (bf16[512,1024]{1,0:T(8,128)(2,1)S(1)}, bf16[512,1024]{1,0:T(8,128)(2,1)}, u32[]{:S(2)}, u32[]{:S(2)}) collective-permute-start(bf16[512,1024]{1,0:T(8,128)(2,1)S(1)} %collective-permute-done.12), channel_id=1, source_target_pairs={{1,0},{2,1},{5,4},{6,5},{9,8},{10,9},{13,12},{14,13},{17,16},{18,1... | collective-permute-start | bytes 3145736 | tf_op jit(solution)/shard_map/ppermute | solution.py:469
  236.0 67.6 %collective-permute-start.19 = (bf16[512,1024]{1,0:T(8,128)(2,1)S(1)}, bf16[512,1024]{1,0:T(8,128)(2,1)}, u32[]{:S(2)}, u32[]{:S(2)}) collective-permute-start(bf16[512,1024]{1,0:T(8,128)(2,1)S(1)} %collective-permute-done.18), channel_id=1, source_target_pairs={{1,0},{2,1},{5,4},{6,5},{9,8},{10,9},{13,12},{14,13},{17,16},{18,1... | collective-permute-start | bytes 3145736 | tf_op jit(solution)/shard_map/ppermute | solution.py:469
  250.4 54.9 %collective-permute-start.17 = (bf16[512,1024]{1,0:T(8,128)(2,1)S(1)}, bf16[512,1024]{1,0:T(8,128)(2,1)S(1)}, u32[]{:S(2)}, u32[]{:S(2)}) collective-permute-start(bf16[512,1024]{1,0:T(8,128)(2,1)S(1)} %collective-permute-done.16), channel_id=1, source_target_pairs={{2,3},{6,7},{10,11},{14,15},{18,19},{22,23},{26,27},{30,31}} | collective-permute-start | bytes 3145736 | tf_op jit(solution)/shard_map/ppermute | solution.py:468
  277.9 48.2 %collective-permute-start.25 = (bf16[256,2048]{1,0:T(8,128)(2,1)S(1)}, bf16[256,2048]{1,0:T(8,128)(2,1)}, u32[]{:S(2)}, u32[]{:S(2)}) collective-permute-start(bf16[256,2048]{1,0:T(8,128)(2,1)S(1)} %collective-permute-done.24), channel_id=1, source_target_pairs={{1,0},{2,1},{5,4},{6,5},{9,8},{10,9},{13,12},{14,13},{17,16},{18,1... | collective-permute-start | bytes 3145736 | tf_op jit(solution)/shard_map/ppermute | solution.py:469
  281.2 65.5 %collective-permute-start.14 = (bf16[512,1024]{1,0:T(8,128)(2,1)}, bf16[512,1024]{1,0:T(8,128)(2,1)}, u32[]{:S(2)}, u32[]{:S(2)}) collective-permute-start(bf16[512,1024]{1,0:T(8,128)(2,1)} %collective-permute-done.13), channel_id=1, source_target_pairs={{1,0},{5,4},{9,8},{13,12},{17,16},{21,20},{25,24},{29,28}} | collective-permute-start | bytes 3145736 | tf_op jit(solution)/shard_map/ppermute | solution.py:469
  303.6 46.6 %collective-permute-start.23 = (bf16[512,1024]{1,0:T(8,128)(2,1)}, bf16[512,1024]{1,0:T(8,128)(2,1)}, u32[]{:S(2)}, u32[]{:S(2)}) collective-permute-start(bf16[512,1024]{1,0:T(8,128)(2,1)} %collective-permute-done.22), channel_id=1, source_target_pairs={{2,3},{6,7},{10,11},{14,15},{18,19},{22,23},{26,27},{30,31}} | collective-permute-start | bytes 3145736 | tf_op jit(solution)/shard_map/ppermute | solution.py:468
  305.3 63.9 %collective-permute-start.20 = (bf16[512,1024]{1,0:T(8,128)(2,1)}, bf16[512,1024]{1,0:T(8,128)(2,1)}, u32[]{:S(2)}, u32[]{:S(2)}) collective-permute-start(bf16[512,1024]{1,0:T(8,128)(2,1)} %collective-permute-done.19), channel_id=1, source_target_pairs={{1,0},{5,4},{9,8},{13,12},{17,16},{21,20},{25,24},{29,28}} | collective-permute-start | bytes 3145736 | tf_op jit(solution)/shard_map/ppermute | solution.py:469
  308.4 64.4 %collective-permute-start.29 = (bf16[256,2048]{1,0:T(8,128)(2,1)}, bf16[256,2048]{1,0:T(8,128)(2,1)}, u32[]{:S(2)}, u32[]{:S(2)}) collective-permute-start(bf16[256,2048]{1,0:T(8,128)(2,1)} %collective-permute-done.28), channel_id=1, source_target_pairs={{2,3},{6,7},{10,11},{14,15},{18,19},{22,23},{26,27},{30,31}} | collective-permute-start | bytes 3145736 | tf_op jit(solution)/shard_map/ppermute | solution.py:468
  326.1 65.5 %collective-permute-start.26 = (bf16[256,2048]{1,0:T(8,128)(2,1)}, bf16[256,2048]{1,0:T(8,128)(2,1)}, u32[]{:S(2)}, u32[]{:S(2)}) collective-permute-start(bf16[256,2048]{1,0:T(8,128)(2,1)} %collective-permute-done.25), channel_id=1, source_target_pairs={{1,0},{5,4},{9,8},{13,12},{17,16},{21,20},{25,24},{29,28}} | collective-permute-start | bytes 3145736 | tf_op jit(solution)/shard_map/ppermute | solution.py:469
  464.9 460.0 %reduce-scatter.7.cloned.1.call-start = ((), (), s32[]{:S(2)}) async-start(), calls=%async_computation.6 | async-start | bytes 7077888 | tf_op jit(solution)/shard_map/reduce_scatter | solution.py:611
  533.1 563.1 %all-gather.28.cloned.1.call-start = ((), (), s32[]{:S(2)}) async-start(), calls=%async_computation.13 | async-start | bytes 2359296 | tf_op jit(solution)/shard_map/all_gather | solution.py:631
  615.1 487.7 %all-gather.32.cloned.1.call-start = ((), (), s32[]{:S(2)}) async-start(), calls=%async_computation.15 | async-start | bytes 9437184 | tf_op jit(solution)/shard_map/all_gather | solution.py:631
  618.1 47.2 %collective-permute-start.59 = (bf16[512,1024]{1,0:T(8,128)(2,1)S(1)}, bf16[512,1024]{1,0:T(8,128)(2,1)S(1)}, u32[]{:S(2)}, u32[]{:S(2)}) collective-permute-start(bf16[512,1024]{1,0:T(8,128)(2,1)S(1)} %copy-done.16), channel_id=1, source_target_pairs={{0,1},{1,2},{2,3},{4,5},{5,6},{6,7},{8,9},{9,10},{10,11},{12,13},{... | collective-permute-start | bytes 3145736 | tf_op jit(solution)/shard_map/ppermute | solution.py:493
  689.0 434.3 %all-gather.30.cloned.1.call-start = ((), (), s32[]{:S(2)}) async-start(), calls=%async_computation.14 | async-start | bytes 9437184 | tf_op jit(solution)/shard_map/all_gather | solution.py:631
  803.5 340.5 %all-gather.34.cloned.1.call-start = ((), (), s32[]{:S(2)}) async-start(), calls=%async_computation.16 | async-start | bytes 9437184 | tf_op jit(solution)/shard_map/all_gather | solution.py:631
  924.8 231.9 %all-gather.26.cloned.1.call-start = ((), (), s32[]{:S(2)}) async-start(), calls=%async_computation.12 | async-start | bytes 3538944 | tf_op jit(solution)/shard_map/all_gather | solution.py:631
  1002.4 167.7 %reduce-scatter.11.cloned.1.call-start = ((), (), s32[]{:S(2)}) async-start(), calls=%async_computation.8 | async-start | bytes 7077888 | tf_op jit(solution)/shard_map/reduce_scatter | solution.py:620
  1019.0 173.4 %reduce-scatter.9.cloned.1.call-start = ((), (), s32[]{:S(2)}) async-start(), calls=%async_computation.7 | async-start | bytes 7077888 | tf_op jit(solution)/shard_map/reduce_scatter | solution.py:626
  (83 other events, 2081.8 us)
Sparse Core Ops, SparseCore 0:
  9.9 47.0 all-gather.19
  97.5 49.8 all-gather.21
  149.3 45.5 all-gather.17
  196.6 45.5 all-gather.23
  465.0 60.8 reduce-scatter.4
  533.2 61.7 reduce-scatter.6
  615.2 33.2 all-gather.27
  689.2 57.8 all-gather.31
  803.7 65.6 all-gather.29
  925.0 72.9 all-gather.33
  1002.5 59.2 all-gather.25
  1065.0 61.3 reduce-scatter.10
  1130.7 61.7 reduce-scatter.8

commit v3 on v2

--- a/solution.py
+++ b/solution.py
@@ -1,3 +1,5 @@
+import functools
+
 import jax
 import jax.numpy as jnp
 from jax import lax
@@ -47,80 +49,6 @@
     key = lax.broadcasted_iota(jnp.int32, (rows, cols), 1)
     start = jnp.where(query >= first_len, first_len, 0)
     return jnp.where((key <= query) & (key >= start), 0.0, NEGATIVE_BIG)
-
-
-def attention_forward_kernel(length_ref, q_ref, kv_ref, cos_ref, sin_ref, out_ref, q_out, k_out, v_out, lse_ref):
-    pair = pl.program_id(0)
-    tokens = q_ref.shape[0]
-    cos, sin = cos_ref[...], sin_ref[...]
-
-    @pl.when(pair == 0)
-    def _():
-        kv = kv_ref[...]
-        turned = pltpu.roll(kv, HEAD_SIZE, 1)
-        low = low_half(kv.shape)
-        k = jnp.where(low, kv, turned)
-        k_out[...] = (k * cos + swap_halves(k) * sin).astype(BF16)
-        v_out[...] = jnp.where(low, turned, kv).astype(BF16)
-
-    q = q_ref[...]
-    q_out[...] = ((q * cos + swap_halves(q) * sin) * SCORE_SCALE).astype(BF16)
-    first_len = length_ref[0]
-    for block in range(tokens // ROWS):
-        rows = pl.ds(block * ROWS, ROWS)
-        end = (block + 1) * ROWS
-        bias = mask_bias(first_len, block * ROWS, ROWS, end)
-        query = q_out[rows, :]
-        low = low_half(query.shape)
-        keys, values = k_out[:end, :], v_out[:end, :]
-        parts = []
-        for half in range(2):
-            chosen = low if half == 0 else jnp.logical_not(low)
-            scores = dot_nt(jnp.where(chosen, query, jnp.zeros_like(query)), keys) + bias
-            top = jnp.max(scores, axis=-1, keepdims=True)
-            weights = jnp.exp(scores - top)
-            total = jnp.sum(weights, axis=-1, keepdims=True)
-            probs = (weights * (1.0 / total)).astype(BF16)
-            parts.append(dot_nn(probs, values))
-            lse_ref[0, rows, half : half + 1] = top + jnp.log(total)
-        out_ref[rows, :] = jnp.where(low_half(parts[0].shape), parts[0], parts[1]).astype(BF16)
-
-
-def attention_forward(qkv, cos, sin, lengths, heads):
-    tokens = qkv.shape[0]
-    pairs = heads // 2
-    return pl.pallas_call(
-        attention_forward_kernel,
-        grid=(pairs,),
-        in_specs=[
-            pl.BlockSpec(memory_space=pltpu.SMEM),
-            pl.BlockSpec((tokens, LANES), lambda j: (0, j)),
-            pl.BlockSpec((tokens, LANES), lambda j: (0, pairs)),
-            pl.BlockSpec((tokens, LANES), lambda j: (0, 0)),
-            pl.BlockSpec((tokens, LANES), lambda j: (0, 0)),
-        ],
-        out_specs=[
-            pl.BlockSpec((tokens, LANES), lambda j: (0, j)),
-            pl.BlockSpec((tokens, LANES), lambda j: (0, j)),
-            pl.BlockSpec((tokens, LANES), lambda j: (0, 0)),
-            pl.BlockSpec((tokens, LANES), lambda j: (0, 0)),
-            pl.BlockSpec((1, tokens, LANES), lambda j: (j, 0, 0)),
-        ],
-        out_shape=[
-            jax.ShapeDtypeStruct((tokens, pairs * LANES), BF16),
-            jax.ShapeDtypeStruct((tokens, pairs * LANES), BF16),
-            jax.ShapeDtypeStruct((tokens, LANES), BF16),
-            jax.ShapeDtypeStruct((tokens, LANES), BF16),
-            jax.ShapeDtypeStruct((pairs, tokens, LANES), F32),
-        ],
-        compiler_params=pltpu.CompilerParams(vmem_limit_bytes=VMEM_LIMIT),
-        cost_estimate=pl.CostEstimate(
-            flops=4 * tokens * tokens * LANES * heads // 2,
-            bytes_accessed=12 * tokens * pairs * LANES,
-            transcendentals=tokens * tokens * heads // 2,
-        ),
-        name="attend",
-    )(lengths, qkv, qkv, cos, sin)
 
 
 def attention_backward_kernel(length_ref, g_ref, q_ref, k_ref, v_ref, lse_ref, cos_ref, sin_ref, dq_ref, dkv_ref, dk_sum, dv_sum):
@@ -217,103 +145,6 @@
     return pl.CostEstimate(flops=flops, bytes_accessed=moved, transcendentals=0)
 
 
-def project_kernel(x_ref, gain_ref, w_ref, normed_ref, qkv_ref):
-    x = x_ref[...].astype(F32)
-    r1 = lax.rsqrt(jnp.mean(x * x, axis=-1, keepdims=True) + EPSILON)
-    normed = (x * r1 * gain_ref[...]).astype(BF16)
-    normed_ref[...] = normed
-    qkv_ref[...] = dot_nn(normed, w_ref[...])
-
-
-def project(x, gain, w_qkv):
-    total, width = x.shape
-    columns = w_qkv.shape[1]
-    out_shape = [jax.ShapeDtypeStruct((total, width), BF16), jax.ShapeDtypeStruct((total, columns), F32)]
-    return pl.pallas_call(
-        project_kernel,
-        grid=(total // ROWS,),
-        in_specs=[row_block(width), fixed(1, width), fixed(width, columns)],
-        out_specs=[row_block(width), row_block(columns)],
-        out_shape=out_shape,
-        compiler_params=params(),
-        cost_estimate=cost(2 * total * width * columns, x, w_qkv, *out_shape),
-        name="project",
-    )(x, gain, w_qkv)
-
-
-def out_kernel(me_ref, x_ref, att_ref, w_ref, hidden_ref):
-    own_width = hidden_ref.shape[1]
-    acc = jnp.zeros(hidden_ref.shape, F32)
-    for c in range(att_ref.shape[0]):
-        acc += dot_nn(att_ref[c], w_ref[c])
-    start = pl.multiple_of(me_ref[0] * own_width, LANES)
-    x = x_ref[:, pl.ds(start, own_width)].astype(F32)
-    hidden_ref[...] = (x + RESIDUAL_SCALE * acc).astype(BF16)
-
-
-def out_projection(me, x, att_all, w_out):
-    n, total, own = att_all.shape
-    width = x.shape[1]
-    own_width = w_out.shape[1]
-    w_heads = w_out.reshape(n, own, own_width)
-    out_shape = jax.ShapeDtypeStruct((total, own_width), BF16)
-    return pl.pallas_call(
-        out_kernel,
-        grid=(total // ROWS,),
-        in_specs=[
-            pl.BlockSpec(memory_space=pltpu.SMEM),
-            row_block(width),
-            pl.BlockSpec((n, ROWS, own), lambda i: (0, i, 0)),
-            fixed(n, own, own_width),
-        ],
-        out_specs=row_block(own_width),
-        out_shape=out_shape,
-        compiler_params=params(),
-        cost_estimate=cost(2 * total * width * own_width, x, att_all, w_out, out_shape),
-        name="out_projection",
-    )(me, x, att_all, w_heads)
-
-
-def join(ref):
-    return jnp.concatenate([ref[c].astype(F32) for c in range(ref.shape[0])], axis=1)
-
-
-def mlp_kernel(hidden_ref, gain_ref, gate_ref, up_ref, normed_ref, a_ref, b_ref, mixed_ref):
-    hidden = join(hidden_ref)
-    r2 = lax.rsqrt(jnp.mean(hidden * hidden, axis=-1, keepdims=True) + EPSILON)
-    normed = (hidden * r2 * gain_ref[...]).astype(BF16)
-    normed_ref[...] = normed
-    gate = dot_nn(normed, gate_ref[...])
-    up = dot_nn(normed, up_ref[...])
-    sig = jax.nn.sigmoid(gate)
-    silu = gate * sig
-    mixed_ref[...] = (silu * up).astype(BF16)
-    b_ref[...] = silu.astype(BF16)
-    a_ref[...] = (up * sig * (1.0 + gate * (1.0 - sig))).astype(BF16)
-
-
-def mlp_forward(hidden_all, gain, w_gate, w_up):
-    n, total, own = hidden_all.shape
-    width, own_ff = w_gate.shape
-    wide = jax.ShapeDtypeStruct((total, width), BF16)
-    narrow = jax.ShapeDtypeStruct((total, own_ff), BF16)
-    return pl.pallas_call(
-        mlp_kernel,
-        grid=(total // ROWS,),
-        in_specs=[
-            pl.BlockSpec((n, ROWS, own), lambda i: (0, i, 0)),
-            fixed(1, width),
-            fixed(width, own_ff),
-            fixed(width, own_ff),
-        ],
-        out_specs=[row_block(width), row_block(own_ff), row_block(own_ff), row_block(own_ff)],
-        out_shape=[wide, narrow, narrow, narrow],
-        compiler_params=params(),
-        cost_estimate=cost(4 * total * width * own_ff, hidden_all, w_gate, w_up, wide, narrow, narrow, narrow),
-        name="mlp_forward",
-    )(hidden_all, gain, w_gate, w_up)
-
-
 def mlp_back_kernel(
     grad_ref, a_ref, b_ref, hidden_ref, gain_ref, gate_ref, up_ref, down_ref, ggrad_ref, ugrad_ref, part_ref, gain_out
 ):
@@ -323,7 +154,7 @@
     ggrad_ref[...] = ggrad
     ugrad_ref[...] = ugrad
     normed_grad = dot_nt(ggrad, gate_ref[...]) + dot_nt(ugrad, up_ref[...])
-    hidden = join(hidden_ref)
+    hidden = hidden_ref[...].astype(F32)
     r2 = lax.rsqrt(jnp.mean(hidden * hidden, axis=-1, keepdims=True) + EPSILON)
     gain_part = jnp.sum(normed_grad * (hidden * r2), axis=0, keepdims=True)
 
@@ -340,9 +171,10 @@
         part_ref[c] = part[:, c * own : (c + 1) * own].astype(BF16)
 
 
-def mlp_backward(mlp_grad, a, b, hidden_all, gain, w_gate, w_up, w_down):
-    n, total, own = hidden_all.shape
-    width, own_ff = w_gate.shape
+def mlp_backward(n, mlp_grad, a, b, hidden_all, gain, w_gate, w_up, w_down):
+    total, width = hidden_all.shape
+    own = width // n
+    own_ff = w_gate.shape[1]
     narrow = jax.ShapeDtypeStruct((total, own_ff), BF16)
     planes = pl.BlockSpec((n, ROWS, own), lambda i: (0, i, 0))
     return pl.pallas_call(
@@ -352,7 +184,7 @@
             row_block(width),
             row_block(own_ff),
             row_block(own_ff),
-            planes,
+            row_block(width),
             fixed(1, width),
             fixed(width, own_ff),
             fixed(width, own_ff),
@@ -459,44 +291,464 @@
     )(pieces)
 
 
-def gather_planes(shards):
-    n_planes = lax.axis_size("fsdp")
-    plane = lax.axis_index("fsdp")
-    ups, downs = [], []
-    up = down = shards
-    for step in range(n_planes - 1):
-        up = lax.ppermute(up, "fsdp", [(q, q + 1) for q in range(step, n_planes - 1)])
-        down = lax.ppermute(down, "fsdp", [(q + 1, q) for q in range(n_planes - 1 - step)])
-        ups.append(up)
-        downs.append(down)
-
-    def order(p):
-        return lambda own, ups, downs: jnp.concatenate([ups[p - 1 - j] if j < p else own if j == p else downs[j - p - 1] for j in range(n_planes)], axis=0)
-
-    return lax.switch(plane, [order(p) for p in range(n_planes)], shards, ups, downs), ups
-
-
-def settle_planes(part):
-    n_planes = lax.axis_size("fsdp")
-    plane = lax.axis_index("fsdp")
-    rows = part.shape[0] // n_planes
-
-    def block(index):
-        return lax.dynamic_slice_in_dim(part, jnp.clip(index, 0, n_planes - 1) * rows, rows, axis=0)
-
-    def chain(index_of, pair):
-        got = None
-        for step in range(n_planes - 1):
-            value = block(index_of(step))
-            if got is not None:
-                value = value + got
-            got = lax.ppermute(value, "fsdp", [pair(q) for q in range(step + 1)])
-        return got
-
-    last = n_planes - 1
-    from_below = chain(lambda s: last - s + plane, lambda q: (q, q + 1))
-    from_above = chain(lambda s: s - last + plane, lambda q: (last - q, last - q - 1))
-    return (block(plane).astype(F32) + from_below.astype(F32) + from_above.astype(F32)).astype(part.dtype)
+MESH = pl.DeviceIdType.MESH
+
+
+class Chain:
+    def __init__(self, slot, planes, plane, send_sem, recv_sem):
+        self.slot, self.planes, self.plane = slot, planes, plane
+        self.send_sem, self.recv_sem = send_sem, recv_sem
+
+    def copy(self, way, step, shard, to):
+        return pltpu.make_async_remote_copy(
+            src_ref=self.slot(shard),
+            dst_ref=self.slot(shard),
+            send_sem=self.send_sem.at[way, step],
+            recv_sem=self.recv_sem.at[way, step],
+            device_id={"fsdp": to},
+            device_id_type=MESH,
+        )
+
+    def moves(self, step):
+        p, last = self.plane, self.planes - 1
+        return (
+            (0, (p >= step) & (p < last), p - step, p + 1, p >= step + 1, p - 1 - step),
+            (1, (p + step <= last) & (p > 0), p + step, p - 1, p + step + 1 <= last, p + 1 + step),
+        )
+
+    def start(self, step):
+        for way, sends, shard, to, _, _ in self.moves(step):
+
+            @pl.when(sends)
+            def _(way=way, shard=shard, to=to):
+                self.copy(way, step, shard, to).start()
+
+    def arrive(self, step):
+        for way, _, _, _, receives, shard in self.moves(step):
+
+            @pl.when(receives)
+            def _(way=way, shard=shard):
+                self.copy(way, step, shard, self.plane).wait_recv()
+
+    def advance(self, step):
+        self.arrive(step - 1)
+        self.start(step)
+
+    def drain(self):
+        for step in range(self.planes - 1):
+            for way, sends, shard, to, _, _ in self.moves(step):
+
+                @pl.when(sends)
+                def _(way=way, shard=shard, to=to, step=step):
+                    self.copy(way, step, shard, to).wait_send()
+
+
+class Spread:
+    def __init__(self, src, slot, n, me, send_sem, recv_sem):
+        self.src, self.slot, self.n, self.me = src, slot, n, me
+        self.send_sem, self.recv_sem = send_sem, recv_sem
+        self.chips = n // 2
+        self.chip, self.core = me // 2, lax.rem(me, 2)
+        self.partner = me + 1 - 2 * self.core
+
+    def at(self, k):
+        return lax.rem(self.chip + k, self.chips) * 2 + self.core
+
+    def copy(self, src, owner, sem, to):
+        return pltpu.make_async_remote_copy(
+            src_ref=src,
+            dst_ref=self.slot(owner),
+            send_sem=self.send_sem.at[sem],
+            recv_sem=self.recv_sem.at[sem],
+            device_id={"ctx": to},
+            device_id_type=MESH,
+        )
+
+    def out(self, k):
+        return self.copy(self.src, self.me, k, self.at(k))
+
+    def relay(self, k):
+        owner = self.at(self.chips - k) if k else self.me
+        src = self.slot(owner) if k else self.src
+        return self.copy(src, owner, self.chips + k, self.partner)
+
+    def start(self):
+        for k in range(1, self.chips):
+            self.out(k).start()
+        self.relay(0).start()
+
+    def pass_on(self):
+        for k in range(1, self.chips):
+            self.copy(self.src, self.at(self.chips - k), k, self.me).wait_recv()
+            self.relay(k).start()
+
+    def finish(self):
+        other = 1 - 2 * self.core
+        for k in range(self.chips):
+            owner = (self.at(self.chips - k) if k else self.me) + other
+            self.copy(self.slot(owner), owner, self.chips + k, self.me).wait_recv()
+
+    def drain(self):
+        for k in range(1, self.chips):
+            self.out(k).wait_send()
+        for k in range(self.chips):
+            self.relay(k).wait_send()
+
+
+def greet(n, planes, me, plane, across):
+    barrier = pltpu.get_barrier_semaphore()
+    chips = n // 2
+    core = lax.rem(me, 2)
+    others = [lax.rem(me // 2 + k, chips) * 2 + core for k in range(1, chips)] + [me + 1 - 2 * core]
+    for other in others:
+        pl.semaphore_signal(barrier, inc=1, device_id={"ctx": other}, device_id_type=MESH)
+    if across:
+
+        @pl.when(plane > 0)
+        def _():
+            pl.semaphore_signal(barrier, inc=1, device_id={"fsdp": plane - 1}, device_id_type=MESH)
+
+        @pl.when(plane < planes - 1)
+        def _():
+            pl.semaphore_signal(barrier, inc=1, device_id={"fsdp": plane + 1}, device_id_type=MESH)
+
+    count = len(others)
+    if across:
+        count = count + (plane > 0).astype(jnp.int32) + (plane < planes - 1).astype(jnp.int32)
+    pl.semaphore_wait(barrier, count)
+
+
+def forward_kernel(
+    n,
+    planes,
+    heads,
+    length_ref,
+    tokens_ref,
+    attn_shard,
+    gate_shard,
+    up_shard,
+    down_shard,
+    gain_shard,
+    cos_ref,
+    sin_ref,
+    x_out,
+    normed_out,
+    q_out,
+    k_out,
+    v_out,
+    lse_out,
+    att_out,
+    hid_out,
+    normed2_out,
+    a_out,
+    b_out,
+    mixed_out,
+    attn_out,
+    gate_out,
+    up_out,
+    down_out,
+    gain_out,
+    w_attn,
+    w_gate,
+    w_up,
+    w_down,
+    gains,
+    x_all,
+    qkv,
+    q_rot,
+    k_rot,
+    v_rows,
+    lse,
+    own_att,
+    att_all,
+    own_hid,
+    wide,
+    narrow,
+    z_send,
+    z_recv,
+    c_send,
+    c_recv,
+    keep_sem,
+    wide_sem,
+    narrow_sem,
+):
+    me, plane = lax.axis_index("ctx"), lax.axis_index("fsdp")
+    per_device, width = tokens_ref.shape
+    total = x_all.shape[0]
+    rows_shard = attn_shard.shape[0]
+    own = own_att.shape[1]
+    own_width = own_hid.shape[1]
+    columns = qkv.shape[1]
+    blocks = total // ROWS
+    pairs = heads // 2
+
+    local_copies = []
+
+    def keep(src, dst, index):
+        copy = pltpu.make_async_copy(src, dst, keep_sem.at[index])
+        copy.start()
+        local_copies.append(copy)
+
+    def chain(index, ref, rows):
+        return Chain(lambda s: ref.at[pl.ds(s * rows, rows)], planes, plane, z_send.at[index], z_recv.at[index])
+
+    attn_chain = chain(0, w_attn, rows_shard)
+    gate_chain = chain(1, w_gate, rows_shard)
+    up_chain = chain(2, w_up, rows_shard)
+    down_chain = chain(3, w_down, down_shard.shape[0])
+    gain_chain = chain(4, gains, gain_shard.shape[0])
+    first = (attn_chain, attn_shard, 0), (gain_chain, gain_shard, 1), (gate_chain, gate_shard, 2), (up_chain, up_shard, 3), (down_chain, down_shard, 4)
+    loads = [pltpu.make_async_copy(shard, c.slot(plane), keep_sem.at[i]) for c, shard, i in first]
+    for load in loads:
+        load.start()
+    own_x = pltpu.make_async_copy(tokens_ref, x_all.at[pl.ds(me * per_device, per_device)], keep_sem.at[5])
+    own_x.start()
+    greet(n, planes, me, plane, True)
+    loads[0].wait()
+    attn_chain.start(0)
+    loads[1].wait()
+    gain_chain.start(0)
+    x_spread = Spread(
+        tokens_ref, lambda c: x_all.at[pl.ds(c * per_device, per_device)], n, me, c_send.at[0], c_recv.at[0]
+    )
+    x_spread.start()
+    for load in loads[2:]:
+        load.wait()
+    own_x.wait()
+    for step in range(1, planes - 1):
+        attn_chain.advance(step)
+        gain_chain.advance(step)
+    gate_chain.start(0)
+    up_chain.start(0)
+    x_spread.pass_on()
+    x_spread.finish()
+    x_copy = pltpu.make_async_copy(x_all, x_out, keep_sem.at[0])
+    x_copy.start()
+    attn_chain.arrive(planes - 2)
+    gain_chain.arrive(planes - 2)
+    keep(w_attn, attn_out, 1)
+    keep(gains, gain_out, 2)
+    half = gain_shard.shape[1] // 2
+    step_rows = gain_shard.shape[0]
+    attn_gain = jnp.concatenate([gains[f * step_rows : f * step_rows + 1, :half] for f in range(planes)], axis=1)
+    mlp_gain = jnp.concatenate([gains[f * step_rows : f * step_rows + 1, half:] for f in range(planes)], axis=1)
+
+    def staged(stage, sem, slot, out, rows, wait_before):
+        copy = pltpu.make_async_copy(stage.at[slot], out.at[rows], sem.at[slot])
+        return copy.wait() if wait_before else copy.start()
+
+    def project_block(i, _):
+        rows = pl.ds(pl.multiple_of(i * ROWS, ROWS), ROWS)
+        slot = lax.rem(i, 2)
+
+        @pl.when(i >= 2)
+        def _():
+            staged(wide, wide_sem, slot, normed_out, rows, True)
+
+        own_hid[rows, :] = x_all[rows, pl.ds(pl.multiple_of(me * own_width, LANES), own_width)]
+        x = x_all[rows, :].astype(F32)
+        r1 = lax.rsqrt(jnp.mean(x * x, axis=-1, keepdims=True) + EPSILON)
+        normed = (x * r1 * attn_gain).astype(BF16)
+        wide[slot] = normed
+        staged(wide, wide_sem, slot, normed_out, rows, False)
+        qkv[rows, :] = dot_nn(normed, w_attn[:, :columns])
+        return 0
+
+    lax.fori_loop(0, blocks, project_block, 0)
+    for i in range(max(blocks - 2, 0), blocks):
+        staged(wide, wide_sem, i % 2, normed_out, pl.ds(i * ROWS, ROWS), True)
+
+    split = columns - LANES
+    cos, sin = cos_ref[...], sin_ref[...]
+    kv = qkv[:, split:]
+    turned = pltpu.roll(kv, HEAD_SIZE, 1)
+    low = low_half(kv.shape)
+    k = jnp.where(low, kv, turned)
+    k_rot[...] = (k * cos + swap_halves(k) * sin).astype(BF16)
+    v_rows[...] = jnp.where(low, turned, kv).astype(BF16)
+    keep(k_rot, k_out, 3)
+    keep(v_rows, v_out, 4)
+    first_len = length_ref[0]
+
+    def attend_pair(pair, _):
+        lanes = pl.ds(pl.multiple_of(pair * LANES, LANES), LANES)
+        q = qkv[:, lanes]
+        q_rot[:, lanes] = ((q * cos_ref[...] + swap_halves(q) * sin_ref[...]) * SCORE_SCALE).astype(BF16)
+        for block in range(blocks):
+            rows = pl.ds(block * ROWS, ROWS)
+            end = (block + 1) * ROWS
+            bias = mask_bias(first_len, block * ROWS, ROWS, end)
+            query = q_rot[rows, lanes]
+            lower = low_half(query.shape)
+            keys, values = k_rot[:end, :], v_rows[:end, :]
+            parts = []
+            for side in range(2):
+                chosen = lower if side == 0 else jnp.logical_not(lower)
+                scores = dot_nt(jnp.where(chosen, query, jnp.zeros_like(query)), keys) + bias
+                top = jnp.max(scores, axis=-1, keepdims=True)
+                weights = jnp.exp(scores - top)
+                whole = jnp.sum(weights, axis=-1, keepdims=True)
+                probs = (weights * (1.0 / whole)).astype(BF16)
+                parts.append(dot_nn(probs, values))
+                lse[pair, rows, side : side + 1] = top + jnp.log(whole)
+            own_att[rows, lanes] = jnp.where(low_half(parts[0].shape), parts[0], parts[1]).astype(BF16)
+        return 0
+
+    lax.fori_loop(0, pairs, attend_pair, 0)
+    att_spread = Spread(own_att, lambda c: att_all.at[c], n, me, c_send.at[1], c_recv.at[1])
+    x_copy.wait()
+    x_spread.drain()
+    att_spread.start()
+    own_a = pltpu.make_async_copy(own_att, att_all.at[me], keep_sem.at[5])
+    own_a.start()
+    keep(q_rot, q_out, 6)
+    keep(lse, lse_out, 7)
+    if planes > 2:
+        gate_chain.advance(1)
+        up_chain.advance(1)
+    att_spread.pass_on()
+    own_a.wait()
+    att_spread.finish()
+    keep(att_all, att_out, 8)
+
+    def out_block(i, _):
+        rows = pl.ds(pl.multiple_of(i * ROWS, ROWS), ROWS)
+        acc = jnp.zeros((ROWS, own_width), F32)
+        for c in range(n):
+            acc += dot_nn(att_all[c, rows, :], w_attn[c * own : (c + 1) * own, columns:])
+        own_hid[rows, :] = (own_hid[rows, :].astype(F32) + RESIDUAL_SCALE * acc).astype(BF16)
+        return 0
+
+    lax.fori_loop(0, blocks, out_block, 0)
+    def hid_slot(c):
+        return x_all.at[:, pl.ds(pl.multiple_of(c * own_width, LANES), own_width)]
+
+    hid_spread = Spread(own_hid, hid_slot, n, me, c_send.at[2], c_recv.at[2])
+    hid_spread.start()
+    own_h = pltpu.make_async_copy(own_hid, hid_slot(me), keep_sem.at[5])
+    own_h.start()
+    for step in range(2, planes - 1):
+        gate_chain.advance(step)
+        up_chain.advance(step)
+    down_chain.start(0)
+    hid_spread.pass_on()
+    own_h.wait()
+    hid_spread.finish()
+    keep(x_all, hid_out, 9)
+    gate_chain.arrive(planes - 2)
+    up_chain.arrive(planes - 2)
+    keep(w_gate, gate_out, 10)
+    keep(w_up, up_out, 11)
+    if planes > 2:
+        down_chain.advance(1)
+
+    def mlp_copies(i, rows, wait):
+        slot = lax.rem(i, 2)
+        staged(wide, wide_sem, slot, normed2_out, rows, wait)
+        for j, out in enumerate((a_out, b_out, mixed_out)):
+            staged(narrow.at[j], narrow_sem.at[j], slot, out, rows, wait)
+
+    def mlp_block(i, _):
+        rows = pl.ds(pl.multiple_of(i * ROWS, ROWS), ROWS)
+        slot = lax.rem(i, 2)
+
+        @pl.when(i >= 2)
+        def _():
+            mlp_copies(i, rows, True)
+
+        hidden = x_all[rows, :].astype(F32)
+        r2 = lax.rsqrt(jnp.mean(hidden * hidden, axis=-1, keepdims=True) + EPSILON)
+        normed = (hidden * r2 * mlp_gain).astype(BF16)
+        wide[slot] = normed
+        gate = dot_nn(normed, w_gate[...])
+        up = dot_nn(normed, w_up[...])
+        sig = jax.nn.sigmoid(gate)
+        silu = gate * sig
+        narrow[2, slot] = (silu * up).astype(BF16)
+        narrow[1, slot] = silu.astype(BF16)
+        narrow[0, slot] = (up * sig * (1.0 + gate * (1.0 - sig))).astype(BF16)
+        mlp_copies(i, rows, False)
+        return 0
+
+    lax.fori_loop(0, blocks, mlp_block, 0)
+    for step in range(2, planes - 1):
+        down_chain.advance(step)
+    for i in range(max(blocks - 2, 0), blocks):
+        mlp_copies(i, pl.ds(i * ROWS, ROWS), True)
+    down_chain.arrive(planes - 2)
+    keep(w_down, down_out, 12)
+    for c in (attn_chain, gain_chain, gate_chain, up_chain, down_chain):
+        c.drain()
+    for s in (att_spread, hid_spread):
+        s.drain()
+    for copy in local_copies:
+        copy.wait()
+
+
+def forward(n, planes, heads, lengths, tokens, attn_shard, gate_shard, up_shard, down_shard, gain_shard, cos, sin):
+    per_device, width = tokens.shape
+    total = per_device * n
+    own = heads * HEAD_SIZE
+    columns = own + 2 * HEAD_SIZE
+    own_width = attn_shard.shape[1] - columns
+    own_ff = gate_shard.shape[1]
+    rows_shard = attn_shard.shape[0]
+    pairs = heads // 2
+    weights = [
+        ((planes * rows_shard, attn_shard.shape[1]), BF16),
+        ((planes * rows_shard, own_ff), BF16),
+        ((planes * rows_shard, own_ff), BF16),
+        ((planes * down_shard.shape[0], width), BF16),
+        ((planes * gain_shard.shape[0], gain_shard.shape[1]), F32),
+    ]
+    outs = [
+        ((total, width), BF16),
+        ((total, width), BF16),
+        ((total, own), BF16),
+        ((total, LANES), BF16),
+        ((total, LANES), BF16),
+        ((pairs, total, LANES), F32),
+        ((n, total, own), BF16),
+        ((total, width), BF16),
+        ((total, width), BF16),
+        ((total, own_ff), BF16),
+        ((total, own_ff), BF16),
+        ((total, own_ff), BF16),
+    ] + weights
+    scratch = weights + [
+        ((total, width), BF16),
+        ((total, columns), F32),
+        ((total, own), BF16),
+        ((total, LANES), BF16),
+        ((total, LANES), BF16),
+        ((pairs, total, LANES), F32),
+        ((total, own), BF16),
+        ((n, total, own), BF16),
+        ((total, own_width), BF16),
+        ((2, ROWS, width), BF16),
+        ((3, 2, ROWS, own_ff), BF16),
+    ]
+    steps = max(planes - 1, 1)
+    dma = pltpu.SemaphoreType.DMA
+    anywhere = pl.BlockSpec(memory_space=pl.ANY)
+    vmem = pl.BlockSpec(memory_space=pltpu.VMEM)
+    return pl.pallas_call(
+        functools.partial(forward_kernel, n, planes, heads),
+        in_specs=[pl.BlockSpec(memory_space=pltpu.SMEM), vmem] + [anywhere] * 5 + [vmem] * 2,
+        out_specs=[anywhere] * len(outs),
+        out_shape=[jax.ShapeDtypeStruct(*o) for o in outs],
+        scratch_shapes=[pltpu.VMEM(*s) for s in scratch]
+        + [dma((5, 2, steps)), dma((5, 2, steps)), dma((3, n)), dma((3, n)), dma((16,)), dma((2,)), dma((3, 2))],
+        compiler_params=pltpu.CompilerParams(
+            vmem_limit_bytes=VMEM_LIMIT, collective_id=1, has_side_effects=True
+        ),
+        cost_estimate=pl.CostEstimate(
+            flops=2 * total * width * (columns + own_width + 2 * own_ff),
+            bytes_accessed=60 * 1024 * 1024,
+            transcendentals=0,
+        ),
+        name="forward",
+    )(lengths, tokens, attn_shard, gate_shard, up_shard, down_shard, gain_shard, cos, sin)
 
 
 def own_columns(array, index, width):
@@ -551,16 +803,7 @@
     def ff_columns(array):
         return jnp.concatenate([own_columns(array, f * n_ctx + me, slab) for f in range(n_fsdp)], axis=1)
 
-    gain_shard = jnp.stack([attn_gain, mlp_gain]).reshape(1, 2 * rows_shard)
-    gains_all, _ = gather_planes(gain_shard)
-    gains = gains_all.reshape(n_fsdp, 2, rows_shard).transpose(1, 0, 2).reshape(2, 1, width).astype(F32)
-    w_attn, first = gather_planes(attn_shard)
-    w_qkv, w_out = w_attn[:, : split + 2 * HEAD_SIZE], w_attn[:, split + 2 * HEAD_SIZE :]
-    w_gate, second = gather_planes(after(ff_columns(gate_weight), first[0]))
-    w_up, second = gather_planes(after(ff_columns(up_weight), first[0]))
-    w_down, _ = gather_planes(
-        after(lax.dynamic_slice_in_dim(down_weight, me * slab, slab, axis=0), second[1])
-    )
+    gain_shard = jnp.tile(jnp.concatenate([attn_gain, mlp_gain]).astype(F32)[None], (8, 1))
 
     first_len = lengths[0, 0]
     given = jnp.arange(total, dtype=jnp.int32)
@@ -583,24 +826,36 @@
         blocks = array.reshape(n_ctx * n_ctx, block_rows, array.shape[1])
         return jnp.take(blocks, table, axis=0, mode="clip").reshape(array.shape)
 
-    x = lax.all_gather(tokens[0], "ctx", axis=0, tiled=True)
-    normed, qkv = project(x, gains[0], w_qkv)
-    attended, q_rot, k_rot, v_rows, lse = attention_forward(qkv, cos_table, sin_table, lengths[0], heads)
-    attended_all = lax.all_gather(attended, "ctx", axis=0, tiled=False)
-    hidden_own = out_projection(me_array, x, attended_all, w_out)
-    hidden_all = lax.all_gather(hidden_own, "ctx", axis=0, tiled=False)
-    cotangent_all = lax.all_gather(after(cotangent[0], attended), "ctx", axis=0, tiled=True)
+    cotangent_all = lax.all_gather(cotangent[0], "ctx", axis=0, tiled=True)
+    (
+        x, normed, q_rot, k_rot, v_rows, lse, attended_all, hidden_all, normed2, a, b, mixed, w_attn, w_gate, w_up, w_down, gains_all,
+    ) = forward(
+        n_ctx,
+        n_fsdp,
+        heads,
+        lengths[0],
+        tokens[0],
+        attn_shard,
+        ff_columns(gate_weight),
+        ff_columns(up_weight),
+        lax.dynamic_slice_in_dim(down_weight, me * slab, slab, axis=0),
+        gain_shard,
+        cos_table,
+        sin_table,
+    )
+    w_qkv, w_out = w_attn[:, : split + 2 * HEAD_SIZE], w_attn[:, split + 2 * HEAD_SIZE :]
+    gains = gains_all.reshape(n_fsdp, 8, 2, rows_shard)[:, 0].transpose(1, 0, 2).reshape(2, 1, width)
+    hidden_own = own_columns(hidden_all, me, own_width)
     grad_result = reorder(cotangent_all, dealt_of_given)
-    normed2, a, b, mixed = mlp_forward(hidden_all, gains[1], w_gate, w_up)
 
     mlp_grad = (RESIDUAL_SCALE * grad_result.astype(F32)).astype(BF16)
 
     def settle(left, right):
-        return settle_planes(dot_tn(left, right).astype(BF16))
+        return lax.psum_scatter(dot_tn(left, right).astype(BF16), "fsdp", scatter_dimension=0, tiled=True)
 
     down_part = settle(mixed, mlp_grad)
     ggrad, ugrad, hidden_part, mlp_gain_part = mlp_backward(
-        mlp_grad, a, b, hidden_all, gains[1], w_gate, w_up, w_down
+        n_ctx, mlp_grad, a, b, hidden_all, gains[1], w_gate, w_up, w_down
     )
     hidden_sum = lax.psum_scatter(hidden_part, "ctx", scatter_dimension=0, tiled=False)
     gate_part = settle(normed2, ggrad)
@@ -609,10 +864,13 @@
         hidden_sum, own_columns(grad_result, me, own_width), w_out, n_ctx
     )
     attended_grad = lax.psum_scatter(attended_part, "ctx", scatter_dimension=0, tiled=False)
-    out_part = settle_planes(
+    out_part = lax.psum_scatter(
         jnp.einsum("ctk,to->cko", attended_all, branch_grad, preferred_element_type=F32)
         .astype(BF16)
-        .reshape(width, own_width)
+        .reshape(width, own_width),
+        "fsdp",
+        scatter_dimension=0,
+        tiled=True,
     )
     dq, dkv = attention_backward(attended_grad, q_rot, k_rot, v_rows, lse, cos_table, sin_table, lengths[0])
     qkv_part = settle(normed, jnp.concatenate([dq, dkv], axis=1))
@@ -659,7 +917,7 @@
         gain_parts = gain_parts + lax.ppermute(gain_parts, "ctx", [(c, c ^ step) for c in range(n_ctx)])
         step *= 2
     gain_rows = gain_parts.reshape(2, n_fsdp, rows_shard).transpose(1, 0, 2).reshape(n_fsdp, 2 * rows_shard)
-    own_gains = settle_planes(gain_rows).reshape(2, rows_shard)
+    own_gains = lax.psum_scatter(gain_rows, "fsdp", scatter_dimension=0, tiled=True).reshape(2, rows_shard)
     return (
         activations,
         token_grad,

time: 1210 us -> 1150 us (0.950)
  starting transfers between devices: 241 us -> 4.49 us
  Pallas kernels: 192 us -> 386 us
  other arithmetic: 83.7 us -> 38.3 us
  blocking collectives: 0 us -> 12.9 us
    ppermute x66 -> x0, waiting for transfers between devices: 448 us -> none  [the longest x36 255 us: chain(): got = lax.ppermute(value, 'fsdp', [pair(q) for q in range(step + 1)])]
    reduce_scatter x0 -> x5, waiting for transfers between devices: none -> 270 us  [the longest x4 270 us: settle(): lax.psum_scatter(dot_tn(left, right).astype(BF16), 'fsdp', scatter_dimens...]
    ppermute x66 -> x0, starting transfers between devices: 209 us -> none  [the longest x36 131 us: chain(): got = lax.ppermute(value, 'fsdp', [pair(q) for q in range(step + 1)])]
    pallas_call x4 -> x1, Pallas kernels: 57.9 us -> 250 us  [forward(): pl.pallas_call(functools.partial(forward_kernel, n, planes, heads), in_sp...]
    all_gather x5, waiting for transfers between devices: 0.03 us -> 110 us  [whole(): return lax.all_gather(part, 'ctx', axis=0, tiled=False)]
    reduce_scatter x1, waiting for transfers between devices: 0.01 us -> 50.8 us  [local(): lax.psum_scatter(token_part, 'ctx', scatter_dimension=0, tiled=True)]
    all_gather x4 -> x1, waiting for transfers between devices: 49.2 us -> 0.02 us  [local(): cotangent_all = lax.all_gather(cotangent[0], 'ctx', axis=0, tiled=True)]
    reduce_scatter x1, waiting for transfers between devices: 19.9 us -> 63.5 us  [local(): lax.psum_scatter(after(result_part.astype(BF16), attended_grad), 'ctx', s...]
  transfers between devices with their start and end apart: 82 -> 18, of which waited for: 42 -> 14; matrix products, arithmetic and copies ran while one was open for 14% -> 11% of each run, Pallas kernels for 9% -> 31%
where the time goes in v3:
time: 1150 us; the launch traced here: 1140 us
  waiting for transfers between devices  578 us (50%)
  Pallas kernels  386 us (34%)
  matrix products  61.1 us (5%)
  local copies, waits for them, and re-layouts  41.4 us (4%)
  other arithmetic  38.3 us (3%)
  between operations  14.4 us (1%)
  blocking collectives  12.9 us (1%)
    reduce_scatter x4, waiting for transfers between devices, settle(): lax.psum_scatter(dot_tn(left, right).astype(BF16), 'fsdp', scatter_dimens...  270 us
    pallas_call x1, Pallas kernels, forward(): pl.pallas_call(functools.partial(forward_kernel, n, planes, heads), in_sp...  250 us
    all_gather x5, waiting for transfers between devices, whole(): return lax.all_gather(part, 'ctx', axis=0, tiled=False)  110 us
    reduce_scatter x1, waiting for transfers between devices, local(): lax.psum_scatter(after(result_part.astype(BF16), attended_grad), 'ctx', s...  63.5 us
    reduce_scatter x1, waiting for transfers between devices, local(): lax.psum_scatter(hidden_part, 'ctx', scatter_dimension=0, tiled=False)  63.4 us
    pallas_call x4, Pallas kernels, spread_columns(): pl.pallas_call(spread_kernel, grid=(groups, n), in_specs=[pl.BlockSpec((1...  53.2 us
    reduce_scatter x1, waiting for transfers between devices, local(): lax.psum_scatter(token_part, 'ctx', scatter_dimension=0, tiled=True)  50.8 us
    dot_general x4, matrix products, dot_tn(): lax.dot_general(a, b, (((0,), (0,)), ((), ())), preferred_element_type=F32)  42.5 us
  transfers between devices with their start and end apart: 18, of which 14 were waited for; matrix products, arithmetic and copies ran while one was open for 11% of the time, Pallas kernels for 31%

profile of v3, /device:TPU:9, one launch (start us, length us, event | category | flops | bytes accessed | tf_op | source)
XLA Modules:
  0.0 1137.2 jit_solution(235110849868912666)
XLA Ops:
  25.6 249.9 %forward.1 = (bf16[1536,2048]{1,0:T(8,128)(2,1)}, bf16[1536,2048]{1,0:T(8,128)(2,1)}, bf16[1536,256]{1,0:T(8,128)(2,1)}, bf16[1536,128]{1,0:T(8,128)(2,1)}, bf16...) custom-call(s32[2]{0:T(128)} %bitcast.85, ...), custom_call_target="tpu_custom_call" | custom-call | flops 16911433728 | bytes 62914560 | tf_op jit(solution)/shard_map/forward/pallas_call | solution.py:735
  291.3 32.2 %mlp_backward.1 = (bf16[1536,1024]{1,0:T(8,128)(2,1)}, bf16[1536,1024]{1,0:T(8,128)(2,1)}, bf16[8,1536,256]{2,1,0:T(8,128)(2,1)}, f32[1,2048]{1,0:T(1,128)}) custom-call(bf16[1536,2048]{1,0:T(8,128)(2,1)} %multiply_convert_fusion.grad_ref, bf16[1536,1024]{1,0:T(8,128)(2,1)} %get-tuple-element.43.a_ref, bf16[1536,1024]{1,0:T(8,128)(2,1)} %get-tuple-element.44.b_ref, ...), custom_call_target="tpu_custom_call" | custom-call | flops 19327352832 | bytes 44040192 | tf_op jit(solution)/shard_map/mlp_backward/pallas_call | solution.py:180
  327.9 63.4 %reduce-scatter.10.cloned.1.call-done = bf16[1,1536,256]{2,1,0:T(8,128)(2,1)} async-done(((bf16[8,1536,256]{2,1,0:T(8,128)(2,1)}), bf16[1,1536,256]{2,1,0:T(8,128)(2,1)}) %reduce-scatter.10.cloned.1.call-update) | async-done | bytes 786448 | tf_op jit(solution)/shard_map/reduce_scatter | solution.py:860
  405.2 12.4 %convolution_convert_fusion.2 = bf16[2048,1024]{1,0:T(8,128)(2,1)} fusion(bf16[1536,2048]{1,0:T(8,128)(2,1)} %get-tuple-element.66, bf16[1536,1024]{1,0:T(8,128)(2,1)} %get-tuple-element.67), kind=kOutput, calls=%fused_computation.10 | convolution fusion | flops 6444548096 | bytes 13631488 | tf_op jit(solution)/shard_map/dot_general | solution.py:34
  419.5 11.1 convolution_convert_fusion.1
  432.5 11.3 convolution_convert_fusion
  443.8 16.4 %reduce-scatter.12.cloned.1.call-done = bf16[1,1536,256]{2,1,0:T(8,128)(2,1)} async-done(((bf16[8,1536,256]{2,1,0:T(8,128)(2,1)}), bf16[1,1536,256]{2,1,0:T(8,128)(2,1)}) %reduce-scatter.12.cloned.1.call-update) | async-done | bytes 786448 | tf_op jit(solution)/shard_map/reduce_scatter | solution.py:866
  460.3 26.6 %attend_back.1 = (bf16[1536,256]{1,0:T(8,128)(2,1)}, bf16[1536,128]{1,0:T(8,128)(2,1)}) custom-call(s32[2]{0:T(128)} %bitcast.86, bf16[1536,256]{1,0:T(8,128)(2,1)} %bitcast.89, bf16[1536,256]{1,0:T(8,128)(2,1)} %get-tuple-element.52.q_ref, bf16[1536,128]{1,0:T(8,128)(2,1)} %get-tuple-element.53.k_ref, bf16[1536,128]{1,0:T(8,128)(2,1)} %get-tuple-element.54.v_ref, ...), custom_call_target="tpu_custom_call" | custom-call | flops 6039797760 | bytes 4718592 | tf_op jit(solution)/shard_map/attend_back/pallas_call | solution.py:102
  495.4 73.0 %reduce-scatter.22.cloned.1.call-done = bf16[512,1024]{1,0:T(8,128)(2,1)} async-done(((bf16[2048,1024]{1,0:T(8,128)(2,1)}), bf16[512,1024]{1,0:T(8,128)(2,1)}) %reduce-scatter.22.cloned.1.call-update) | async-done | bytes 1048592 | tf_op jit(solution)/shard_map/reduce_scatter | solution.py:854
  568.5 80.0 %reduce-scatter.24.cloned.1.call-done = bf16[512,1024]{1,0:T(8,128)(2,1)} async-done(((bf16[2048,1024]{1,0:T(8,128)(2,1)}), bf16[512,1024]{1,0:T(8,128)(2,1)}) %reduce-scatter.24.cloned.1.call-update) | async-done | bytes 1048592 | tf_op jit(solution)/shard_map/reduce_scatter | solution.py:854
  648.6 80.2 %reduce-scatter.26.cloned.1.call-done = bf16[256,2048]{1,0:T(8,128)(2,1)} async-done(((bf16[1024,2048]{1,0:T(8,128)(2,1)}), bf16[256,2048]{1,0:T(8,128)(2,1)}) %reduce-scatter.26.cloned.1.call-update) | async-done | bytes 1048592 | tf_op jit(solution)/shard_map/reduce_scatter | solution.py:854
  728.9 36.7 %reduce-scatter.18.cloned.1.call-done = bf16[512,384]{1,0:T(8,128)(2,1)} async-done(((bf16[2048,384]{1,0:T(8,128)(2,1)}), bf16[512,384]{1,0:T(8,128)(2,1)}) %reduce-scatter.18.cloned.1.call-update) | async-done | bytes 393232 | tf_op jit(solution)/shard_map/reduce_scatter | solution.py:854
  768.9 17.1 %token_backward.1 = (bf16[1536,2048]{1,0:T(8,128)(2,1)}, f32[1,2048]{1,0:T(1,128)}) custom-call(s32[1]{0:T(128)} %bitcast.17.me_ref, bf16[1536,256]{1,0:T(8,128)(2,1)} %get-tuple-element.56.dq_ref, bf16[1536,128]{1,0:T(8,128)(2,1)} %get-tuple-element.57.dkv_ref, bf16[2048,384]{1,0:T(8,128)(2,1)} %slice.38.w_ref, bf16[1536,2048]{1,0:T(8,128)(2,1)} %get-tuple-element.58.x_ref, ...), custom_call_target="tpu_custom_call" | custom-call | flops 2415919104 | bytes 16908288 | tf_op jit(solution)/shard_map/token_backward/pallas_call | solution.py:255
  795.9 13.0 %multiply_convert_fusion.1 = bf16[1536,2048]{1,0:T(8,128)(2,1)} fusion(bf16[1536,1280]{1,0:T(8,128)(2,1)} %bitcast.72, bf16[256,2048]{1,0:T(8,128)(2,1)S(1)} %fusion.3, bf16[1024,2048]{1,0:T(8,128)(2,1)} %get-tuple-element.42.down_ref), kind=kOutput, calls=%fused_computation.3 | convolution fusion | flops 8069840896 | bytes 15466496 | tf_op jit(solution)/shard_map/dot_general | solution.py:26
  823.1 12.9 %all-reduce = f32[4,1024]{1,0:T(4,128)S(1)} all-reduce(f32[4,1024]{1,0:T(4,128)S(1)} %bitcast.77), channel_id=12, replica_groups=mesh['ctx'=8,'fsdp'=4] {'fsdp'}, use_global_device_ids=true, to_apply=%region_5.6.clone | all-reduce | flops 4096 | bytes 32768
  837.3 15.9 %all-gather.19.cloned.1.call-done = bf16[4096,1024]{1,0:T(8,128)(2,1)} async-done(((bf16[512,1024]{1,0:T(8,128)(2,1)}), bf16[4096,1024]{1,0:T(8,128)(2,1)}) %all-gather.19.cloned.1.call-update) | async-done | bytes 8388624 | tf_op jit(solution)/shard_map/all_gather | solution.py:889
  853.2 20.6 %spread_columns.6 = f32[512,8192]{1,0:T(8,128)} custom-call(bf16[8,512,1024]{2,1,0:T(8,128)(2,1)} %bitcast.67), custom_call_target="tpu_custom_call" | custom-call | bytes 25165824 | tf_op jit(solution)/shard_map/spread_columns/pallas_call | solution.py:282
  873.7 35.8 %all-gather.21.cloned.1.call-done = bf16[4096,1024]{1,0:T(8,128)(2,1)} async-done(((bf16[512,1024]{1,0:T(8,128)(2,1)}), bf16[4096,1024]{1,0:T(8,128)(2,1)}) %all-gather.21.cloned.1.call-update) | async-done | bytes 8388624 | tf_op jit(solution)/shard_map/all_gather | solution.py:889
  909.5 20.6 %spread_columns.7 = f32[512,8192]{1,0:T(8,128)} custom-call(bf16[8,512,1024]{2,1,0:T(8,128)(2,1)} %bitcast.68), custom_call_target="tpu_custom_call" | custom-call | bytes 25165824 | tf_op jit(solution)/shard_map/spread_columns/pallas_call | solution.py:282
  930.1 35.6 %all-gather.23.cloned.1.call-done = bf16[2048,2048]{1,0:T(8,128)(2,1)} async-done(((bf16[256,2048]{1,0:T(8,128)(2,1)}), bf16[2048,2048]{1,0:T(8,128)(2,1)}) %all-gather.23.cloned.1.call-update) | async-done | bytes 8388624 | tf_op jit(solution)/shard_map/all_gather | solution.py:889
  965.7 11.7 %convert_element_type.72 = f32[2048,2048]{1,0:T(8,128)} convert(bf16[2048,2048]{1,0:T(8,128)(2,1)} %all-gather.23.cloned.1.call-done) | non-fusion elementwise | flops 4194304 | bytes 25165824 | tf_op jit(solution)/shard_map/convert_element_type | solution.py:891
  977.3 22.6 %all-gather.15.cloned.1.call-done = bf16[4096,384]{1,0:T(8,128)(2,1)} async-done(((bf16[512,384]{1,0:T(8,128)(2,1)}), bf16[4096,384]{1,0:T(8,128)(2,1)}) %all-gather.15.cloned.1.call-update) | async-done | bytes 3145744 | tf_op jit(solution)/shard_map/all_gather | solution.py:889
  1013.7 50.8 %reduce-scatter.16.cloned.1.call-done = bf16[192,2048]{1,0:T(8,128)(2,1)} async-done(((bf16[1536,2048]{1,0:T(8,128)(2,1)}), bf16[192,2048]{1,0:T(8,128)(2,1)}) %reduce-scatter.16.cloned.1.call-update) | async-done | bytes 786448 | tf_op jit(solution)/shard_map/reduce_scatter | solution.py:878
  1066.9 63.5 %reduce-scatter.14.cloned.1.call-done = bf16[192,2048]{1,0:T(8,128)(2,1)} async-done(((bf16[1536,2048]{1,0:T(8,128)(2,1)}), bf16[192,2048]{1,0:T(8,128)(2,1)}) %reduce-scatter.14.cloned.1.call-update) | async-done | bytes 786448 | tf_op jit(solution)/shard_map/reduce_scatter | solution.py:884
  (113 shorter events, 109.6 us)
Async XLA Ops:
  7.2 269.9 %all-gather.13.cloned.1.call-start = ((), (), s32[]{:S(2)}) async-start(), calls=%async_computation.18 | async-start | bytes 7077888 | tf_op jit(solution)/shard_map/all_gather | solution.py:829
  7.9 383.4 %reduce-scatter.10.cloned.1.call-start = ((), (), s32[]{:S(2)}) async-start(), calls=%async_computation.9 | async-start | bytes 7077888 | tf_op jit(solution)/shard_map/reduce_scatter | solution.py:860
  323.5 136.8 %reduce-scatter.12.cloned.1.call-start = ((), (), s32[]{:S(2)}) async-start(), calls=%async_computation.10 | async-start | bytes 7077888 | tf_op jit(solution)/shard_map/reduce_scatter | solution.py:866
  398.4 1.1 copy-start.6
  398.4 96.3 %reduce-scatter.20.cloned.1.call-start = ((), (), s32[]{:S(2)}) async-start(), calls=%async_computation.14 | async-start | bytes 1310720 | tf_op jit(solution)/shard_map/reduce_scatter | solution.py:867
  405.1 163.3 %reduce-scatter.22.cloned.1.call-start = ((), (), s32[]{:S(2)}) async-start(), calls=%async_computation.15 | async-start | bytes 5242880 | tf_op jit(solution)/shard_map/reduce_scatter | solution.py:854
  417.6 1.9 copy-start.7
  417.6 230.9 %reduce-scatter.24.cloned.1.call-start = ((), (), s32[]{:S(2)}) async-start(), calls=%async_computation.16 | async-start | bytes 5242880 | tf_op jit(solution)/shard_map/reduce_scatter | solution.py:854
  430.6 1.9 copy-start.1
  430.6 298.2 %reduce-scatter.26.cloned.1.call-start = ((), (), s32[]{:S(2)}) async-start(), calls=%async_computation.17 | async-start | bytes 5242880 | tf_op jit(solution)/shard_map/reduce_scatter | solution.py:854
  443.8 321.8 %reduce-scatter.18.cloned.1.call-start = ((), (), s32[]{:S(2)}) async-start(), calls=%async_computation.13 | async-start | bytes 1966080 | tf_op jit(solution)/shard_map/reduce_scatter | solution.py:854
  494.6 322.4 %all-gather.17.cloned.1.call-start = ((), (), s32[]{:S(2)}) async-start(), calls=%async_computation.20 | async-start | bytes 2359296 | tf_op jit(solution)/shard_map/all_gather | solution.py:889
  495.4 357.8 %all-gather.19.cloned.1.call-start = ((), (), s32[]{:S(2)}) async-start(), calls=%async_computation.21 | async-start | bytes 9437184 | tf_op jit(solution)/shard_map/all_gather | solution.py:889
  568.5 341.0 %all-gather.21.cloned.1.call-start = ((), (), s32[]{:S(2)}) async-start(), calls=%async_computation.22 | async-start | bytes 9437184 | tf_op jit(solution)/shard_map/all_gather | solution.py:889
  648.5 317.1 %all-gather.23.cloned.1.call-start = ((), (), s32[]{:S(2)}) async-start(), calls=%async_computation.23 | async-start | bytes 9437184 | tf_op jit(solution)/shard_map/all_gather | solution.py:889
  728.8 271.1 %all-gather.15.cloned.1.call-start = ((), (), s32[]{:S(2)}) async-start(), calls=%async_computation.19 | async-start | bytes 3538944 | tf_op jit(solution)/shard_map/all_gather | solution.py:889
  765.6 298.9 %reduce-scatter.16.cloned.1.call-start = ((), (), s32[]{:S(2)}) async-start(), calls=%async_computation.12 | async-start | bytes 7077888 | tf_op jit(solution)/shard_map/reduce_scatter | solution.py:878
  786.0 344.4 %reduce-scatter.14.cloned.1.call-start = ((), (), s32[]{:S(2)}) async-start(), calls=%async_computation.11 | async-start | bytes 7077888 | tf_op jit(solution)/shard_map/reduce_scatter | solution.py:884
  808.8 0.7 copy-start.3
  808.9 7.6 copy-start.5
  809.6 2.2 collective-permute-start
  811.8 3.4 collective-permute-start.1
  815.2 7.8 collective-permute-start.2
  999.9 6.1 copy-start
  (2 other events, 1.4 us)
Sparse Core Ops, SparseCore 0:
  9.9 74.8 all-gather.12
  323.6 67.6 reduce-scatter.9
  398.5 61.7 reduce-scatter.11
  463.0 25.0 reduce-scatter.19
  490.9 77.4 reduce-scatter.21
  571.2 77.2 reduce-scatter.23
  651.5 77.2 reduce-scatter.25
  731.7 33.8 reduce-scatter.17
  767.4 29.1 all-gather.16
  798.4 54.7 all-gather.18
  855.1 54.3 all-gather.20
  911.2 54.3 all-gather.22
  967.6 32.3 all-gather.14
  1003.1 61.3 reduce-scatter.15
  1068.7 61.7 reduce-scatter.13

commit v4 on v3

--- a/solution.py
+++ b/solution.py
@@ -273,17 +273,20 @@
 
 
 def spread_kernel(in_ref, out_ref):
-    out_ref[...] = in_ref[0].astype(F32)
+    slab = in_ref.shape[2]
+    for c in range(in_ref.shape[0]):
+        out_ref[:, c * slab : (c + 1) * slab] = in_ref[c].astype(F32)
 
 
 def spread_columns(pieces, slab, groups):
     n, rows, _ = pieces.shape
+    tile = 128
     out_shape = jax.ShapeDtypeStruct((rows, groups * n * slab), F32)
     return pl.pallas_call(
         spread_kernel,
-        grid=(groups, n),
-        in_specs=[pl.BlockSpec((1, rows, slab), lambda f, c: (c, 0, f))],
-        out_specs=pl.BlockSpec((rows, slab), lambda f, c: (0, f * n + c)),
+        grid=(groups, rows // tile),
+        in_specs=[pl.BlockSpec((n, tile, slab), lambda f, r: (0, r, f))],
+        out_specs=pl.BlockSpec((tile, n * slab), lambda f, r: (r, f)),
         out_shape=out_shape,
         compiler_params=params(),
         cost_estimate=cost(0, pieces, out_shape),
@@ -751,6 +754,658 @@
     )(lengths, tokens, attn_shard, gate_shard, up_shard, down_shard, gain_shard, cos, sin)
 
 
+CHUNK = 64
+
+
+def add_into(dst, src):
+    def step(i, _):
+        rows = pl.ds(pl.multiple_of(i * CHUNK, CHUNK), CHUNK)
+        dst[rows, :] = (dst[rows, :].astype(F32) + src[rows, :].astype(F32)).astype(dst.dtype)
+        return 0
+
+    if dst.shape[0] <= CHUNK:
+        dst[...] = dst[...] + src[...]
+    else:
+        lax.fori_loop(0, dst.shape[0] // CHUNK, step, 0)
+
+
+def fetch(src, dst, sem):
+    copy = pltpu.make_async_copy(src, dst, sem)
+    copy.start()
+    copy.wait()
+
+
+class Settle:
+    def __init__(self, block, landed, stage, planes, plane, send_sem, recv_sem, load_sem):
+        self.block, self.landed, self.stage = block, landed, stage
+        self.planes, self.plane = planes, plane
+        self.send_sem, self.recv_sem, self.load_sem = send_sem, recv_sem, load_sem
+
+    def slot(self, way, shard, at):
+        return shard if way == 0 else jnp.where(shard == at, self.planes, shard)
+
+    def sends(self, step):
+        p, last = self.plane, self.planes - 1
+        return (
+            (0, (p <= step) & (p < last), last - step + p, p + 1),
+            (1, (last - p <= step) & (p > 0), step - last + p, p - 1),
+        )
+
+    def receives(self, step):
+        p, last = self.plane, self.planes - 1
+        return (
+            (0, (p >= 1) & (p - 1 <= step), last - step + p - 1),
+            (1, (p <= last - 1) & (last - p - 1 <= step), step - last + p + 1),
+        )
+
+    def copy(self, way, step, shard, to):
+        return pltpu.make_async_remote_copy(
+            src_ref=self.block(shard),
+            dst_ref=self.landed.at[self.slot(way, shard, to)],
+            send_sem=self.send_sem.at[way, step],
+            recv_sem=self.recv_sem.at[way, step],
+            device_id={"fsdp": to},
+            device_id_type=MESH,
+        )
+
+    def start(self, step=0):
+        for way, active, shard, to in self.sends(step):
+
+            @pl.when(active)
+            def _(way=way, shard=shard, to=to):
+                self.copy(way, step, shard, to).start()
+
+    def take(self, step):
+        for way, active, shard in self.receives(step):
+
+            @pl.when(active)
+            def _(way=way, shard=shard):
+                self.copy(way, step, shard, self.plane).wait_recv()
+                fetch(self.landed.at[self.slot(way, shard, self.plane)], self.stage, self.load_sem)
+                add_into(self.block(shard), self.stage)
+
+    def advance(self, step):
+        self.take(step - 1)
+        self.start(step)
+
+    def drain(self):
+        for step in range(self.planes - 1):
+            for way, active, shard, to in self.sends(step):
+
+                @pl.when(active)
+                def _(way=way, shard=shard, to=to, step=step):
+                    self.copy(way, step, shard, to).wait_send()
+
+
+class Scatter:
+    def __init__(self, block, near, far, stage, n, me, send_sem, recv_sem, load_sem):
+        self.block, self.near, self.far, self.stage = block, near, far, stage
+        self.send_sem, self.recv_sem, self.load_sem = send_sem, recv_sem, load_sem
+        self.chips = n // 2
+        self.me, self.chip, self.core = me, me // 2, lax.rem(me, 2)
+
+    def target(self, k, core):
+        return lax.rem(self.chip + k, self.chips) * 2 + core
+
+    def copy(self, k, sem, src, dst, to):
+        return pltpu.make_async_remote_copy(
+            src_ref=src,
+            dst_ref=dst.at[k],
+            send_sem=self.send_sem.at[sem],
+            recv_sem=self.recv_sem.at[sem],
+            device_id={"ctx": to},
+            device_id_type=MESH,
+        )
+
+    def first(self, k):
+        other = 1 - self.core
+        return self.copy(k, k, self.block(self.target(k, other)), self.near, self.chip * 2 + other)
+
+    def second(self, k):
+        target = self.target(k, self.core)
+        return self.copy(k, self.chips + k, self.block(target), self.far, target)
+
+    def start(self):
+        for k in range(self.chips):
+            self.first(k).start()
+
+    def pass_on(self):
+        for k in range(1, self.chips):
+            self.first(k).wait_recv()
+            fetch(self.near.at[k], self.stage, self.load_sem)
+            add_into(self.block(self.target(k, self.core)), self.stage)
+            self.second(k).start()
+
+    def finish(self, total):
+        self.first(0).wait_recv()
+        fetch(self.near.at[0], self.stage, self.load_sem)
+        add_into(total, self.stage)
+        for k in range(1, self.chips):
+            self.second(k).wait_recv()
+            fetch(self.far.at[k], self.stage, self.load_sem)
+            add_into(total, self.stage)
+
+    def drain(self):
+        for k in range(self.chips):
+            self.first(k).wait_send()
+        for k in range(1, self.chips):
+            self.second(k).wait_send()
+
+
+def backward_kernel(
+    n,
+    planes,
+    heads,
+    length_ref,
+    grad_in,
+    mixed_in,
+    a_in,
+    b_in,
+    hidden_in,
+    normed2_in,
+    normed_in,
+    x_in,
+    att_in,
+    q_in,
+    k_in,
+    v_in,
+    lse_in,
+    cos_in,
+    sin_in,
+    attn_in,
+    gate_in,
+    up_in,
+    down_in,
+    gain_in,
+    token_out,
+    gain_out,
+    down_all,
+    gate_all,
+    up_all,
+    out_all,
+    qkv_all,
+    near1,
+    far1,
+    near2,
+    far2,
+    near3,
+    far3,
+    down_landed,
+    gate_landed,
+    up_landed,
+    out_landed,
+    qkv_landed,
+    w_attn,
+    w_gate,
+    w_up,
+    w_down,
+    p_down,
+    gains,
+    grad,
+    a_v,
+    b_v,
+    part,
+    hid_stage,
+    stage_tall,
+    stage_wide,
+    stage_col,
+    hidden_grad,
+    lse,
+    cos,
+    sin,
+    dk_sum,
+    dv_sum,
+    gain_own,
+    gain_all,
+    gain_landed,
+    gain_stage,
+    z_send,
+    z_recv,
+    s_send,
+    s_recv,
+    g_send,
+    g_recv,
+    load_sem,
+    hid_sem,
+    add_sem,
+):
+    me, plane = lax.axis_index("ctx"), lax.axis_index("fsdp")
+    total, width = grad.shape
+    per_device = total // n
+    own = heads * HEAD_SIZE
+    own_width = width // n
+    own_ff = a_v.shape[1]
+    rows_shard = width // planes
+    slab = own_ff // planes
+    blocks = total // ROWS
+    pairs = heads // 2
+    columns = own + LANES
+    last = planes - 2
+
+    def load(src, dst, index):
+        copy = pltpu.make_async_copy(src, dst, load_sem.at[index])
+        copy.start()
+        return copy
+
+    mixed_loads = [load(mixed_in.at[:, pl.ds(d * own_width, own_width)], part.at[d], d) for d in range(own_ff // own_width)]
+    grad_load = load(grad_in, grad, 8)
+    down_load = load(down_in, w_down, 9)
+    gate_load = load(gate_in, w_gate, 10)
+    up_load = load(up_in, w_up, 11)
+    a_load = load(a_in, a_v, 12)
+    b_load = load(b_in, b_v, 13)
+    attn_load = load(attn_in, w_attn, 14)
+    gain_load = load(gain_in, gains, 15)
+    greet(n, planes, me, plane, True)
+
+    def settle(index, block, landed, stage):
+        return Settle(block, landed, stage, planes, plane, z_send.at[index], z_recv.at[index], add_sem)
+
+    def rows_of(ref, rows):
+        return lambda d: ref.at[pl.ds(pl.multiple_of(d * rows, rows), rows)]
+
+    def out_block_of(d):
+        return w_down.at[pl.ds(0, rows_shard), pl.ds(pl.multiple_of(d * own_width, LANES), own_width)]
+
+    def qkv_block_of(d):
+        return w_down.at[pl.ds(rows_shard, rows_shard), pl.ds(pl.multiple_of(d * columns, LANES), columns)]
+
+    def gain_block_of(d):
+        return gain_own.at[:, pl.ds(pl.multiple_of(d * rows_shard, LANES), rows_shard)]
+
+    down_sum = settle(0, rows_of(p_down, slab), down_landed, stage_wide)
+    gate_sum = settle(1, rows_of(w_gate, rows_shard), gate_landed, stage_tall)
+    up_sum = settle(2, rows_of(w_up, rows_shard), up_landed, stage_tall)
+    out_sum = settle(3, out_block_of, out_landed, stage_tall.at[:, pl.ds(0, own_width)])
+    qkv_sum = settle(4, qkv_block_of, qkv_landed, stage_tall.at[:, pl.ds(0, columns)])
+    gain_sum = settle(5, gain_block_of, gain_landed, gain_stage)
+
+    def spread(index, src, dst):
+        return Spread(src, lambda c: dst.at[c], n, me, g_send.at[index], g_recv.at[index])
+
+    spreads = []
+
+    def give(index, sums, dst):
+        sums.take(last)
+        src = sums.block(plane)
+        mine = load(src, dst.at[me], 16 + index)
+        out = spread(index, src, dst)
+        out.start()
+        spreads.append((out, mine))
+        return out
+
+    def scatter(index, block, near, far, stage):
+        return Scatter(block, near, far, stage, n, me, s_send.at[index], s_recv.at[index], add_sem)
+
+    grad_load.wait()
+
+    def scale_block(i, _):
+        rows = pl.ds(pl.multiple_of(i * ROWS, ROWS), ROWS)
+        grad[rows, :] = (RESIDUAL_SCALE * grad[rows, :].astype(F32)).astype(BF16)
+        return 0
+
+    lax.fori_loop(0, blocks, scale_block, 0)
+    for copy in mixed_loads:
+        copy.wait()
+
+    def down_block(d, _):
+        p_down[pl.ds(pl.multiple_of(d * own_width, own_width), own_width), :] = dot_tn(part[d], grad[...]).astype(BF16)
+        return 0
+
+    lax.fori_loop(0, own_ff // own_width, down_block, 0)
+    down_sum.start()
+
+    for copy in (down_load, gate_load, up_load, a_load, b_load, attn_load, gain_load):
+        copy.wait()
+    half = gains.shape[1] // 2
+    attn_gain = jnp.concatenate([gains[f * 8 : f * 8 + 1, :half] for f in range(planes)], axis=1)
+    mlp_gain = jnp.concatenate([gains[f * 8 : f * 8 + 1, half:] for f in range(planes)], axis=1)
+    gain_own[...] = jnp.zeros_like(gain_own)
+
+    def stream(src, i, wait):
+        rows = pl.ds(pl.multiple_of(i * ROWS, ROWS), ROWS)
+        slot = lax.rem(i, 2)
+        copy = pltpu.make_async_copy(src.at[rows], hid_stage.at[slot], hid_sem.at[slot])
+        return copy.wait() if wait else copy.start()
+
+    stream(hidden_in, jnp.int32(0), False)
+
+    def mlp_block(i, _):
+        rows = pl.ds(pl.multiple_of(i * ROWS, ROWS), ROWS)
+
+        @pl.when(i + 1 < blocks)
+        def _():
+            stream(hidden_in, i + 1, False)
+
+        mixed_grad = dot_nt(grad[rows, :], w_down[...])
+        ggrad = (mixed_grad * a_v[rows, :].astype(F32)).astype(BF16)
+        ugrad = (mixed_grad * b_v[rows, :].astype(F32)).astype(BF16)
+        a_v[rows, :] = ggrad
+        b_v[rows, :] = ugrad
+        normed_grad = dot_nt(ggrad, w_gate[...]) + dot_nt(ugrad, w_up[...])
+        stream(hidden_in, i, True)
+        hidden = hid_stage[lax.rem(i, 2)].astype(F32)
+        r2 = lax.rsqrt(jnp.mean(hidden * hidden, axis=-1, keepdims=True) + EPSILON)
+        gain_own[0:1, :] += jnp.sum(normed_grad * (hidden * r2), axis=0, keepdims=True)
+        weighted = normed_grad * mlp_gain
+        mean = jnp.mean(weighted * hidden, axis=-1, keepdims=True)
+        piece = r2 * weighted - hidden * (r2 * r2 * r2 * mean)
+        for c in range(n):
+            part[c, rows, :] = piece[:, c * own_width : (c + 1) * own_width].astype(BF16)
+        return 0
+
+    lax.fori_loop(0, blocks, mlp_block, 0)
+    first = scatter(0, lambda c: part.at[c], near1, far1, stage_col)
+    first.start()
+    normed2_load = load(normed2_in, grad, 8)
+    down_sum.advance(1)
+    normed2_load.wait()
+
+    def columns_times(right, out):
+        def block(j, _):
+            lanes = pl.ds(pl.multiple_of(j * ROWS, ROWS), ROWS)
+            out[lanes, :] = dot_tn(grad[:, lanes], right[...]).astype(BF16)
+            return 0
+
+        lax.fori_loop(0, width // ROWS, block, 0)
+
+    columns_times(a_v, w_gate)
+    gate_sum.start()
+    first.pass_on()
+    columns_times(b_v, w_up)
+    up_sum.start()
+
+    att_loads = [load(att_in.at[c], grad.at[:, pl.ds(c * own, own)], c) for c in range(n)]
+    own_grad = load(grad_in.at[:, pl.ds(pl.multiple_of(me * own_width, LANES), own_width)], b_v.at[:, pl.ds(LANES, own_width)], 8)
+    q_load = load(q_in, a_v.at[:, pl.ds(0, own)], 9)
+    k_load = load(k_in, a_v.at[:, pl.ds(own, LANES)], 10)
+    v_load = load(v_in, a_v.at[:, pl.ds(own + LANES, LANES)], 11)
+    lse_load = load(lse_in, lse, 12)
+    cos_load = load(cos_in, cos, 13)
+    sin_load = load(sin_in, sin, 14)
+    own_grad.wait()
+
+    def begin(i, _):
+        rows = pl.ds(pl.multiple_of(i * ROWS, ROWS), ROWS)
+        hidden_grad[rows, :] = b_v[rows, LANES : LANES + own_width].astype(F32) + part[me, rows, :].astype(F32)
+        return 0
+
+    lax.fori_loop(0, blocks, begin, 0)
+    first.finish(hidden_grad)
+    first.drain()
+    if planes > 3:
+        down_sum.advance(2)
+
+    def branch_block(i, _):
+        rows = pl.ds(pl.multiple_of(i * ROWS, ROWS), ROWS)
+        branch = (RESIDUAL_SCALE * hidden_grad[rows, :]).astype(BF16)
+        b_v[rows, LANES : LANES + own_width] = branch
+        for c in range(n):
+            part[c, rows, :] = dot_nt(branch, w_attn[c * own : (c + 1) * own, columns:]).astype(BF16)
+        return 0
+
+    lax.fori_loop(0, blocks, branch_block, 0)
+    second = scatter(1, lambda c: part.at[c], near2, far2, stage_col)
+    second.start()
+    gate_sum.advance(1)
+    for copy in att_loads:
+        copy.wait()
+    heads_per_shard = rows_shard // own
+    for c in range(n):
+        place = out_block_of(c // heads_per_shard).at[pl.ds((c % heads_per_shard) * own, own)]
+        place[...] = dot_tn(grad[:, c * own : (c + 1) * own], b_v[:, LANES : LANES + own_width]).astype(BF16)
+    second.pass_on()
+    up_sum.advance(1)
+    out_sum.start()
+    normed_load = load(normed_in, grad, 15)
+    down_give = give(0, down_sum, down_all)
+    second.finish(part.at[me])
+    if planes > 3:
+        gate_sum.advance(2)
+
+    for copy in (q_load, k_load, v_load, lse_load, cos_load, sin_load):
+        copy.wait()
+    dk_sum[...] = jnp.zeros_like(dk_sum)
+    dv_sum[...] = jnp.zeros_like(dv_sum)
+    first_len = length_ref[0]
+    dq_at = own + 2 * LANES
+
+    def attend_pair(pair, _):
+        lanes = pl.ds(pl.multiple_of(pair * LANES, LANES), LANES)
+        dq_lanes = pl.ds(pl.multiple_of(dq_at + pair * LANES, LANES), LANES)
+        for block in range(blocks):
+            rows = pl.ds(block * ROWS, ROWS)
+            end = (block + 1) * ROWS
+            bias = mask_bias(first_len, block * ROWS, ROWS, end)
+            query, grads = a_v[rows, lanes], part[me, rows, lanes]
+            low = low_half(query.shape)
+            keys, values = a_v[:end, own : own + LANES], a_v[:end, own + LANES : own + 2 * LANES]
+            parts = []
+            for side in range(2):
+                chosen = low if side == 0 else jnp.logical_not(low)
+                own_query = jnp.where(chosen, query, jnp.zeros_like(query))
+                own_grads = jnp.where(chosen, grads, jnp.zeros_like(grads))
+                scores = dot_nt(own_query, keys) + bias
+                probs = jnp.exp(scores - lse[pair, rows, side : side + 1])
+                prob_grad = dot_nt(own_grads, values)
+                delta = jnp.sum(probs * prob_grad, axis=-1, keepdims=True)
+                score_grad = (probs * (prob_grad - delta)).astype(BF16)
+                parts.append(dot_nn(score_grad, keys))
+                dk_sum[:end, :] += dot_tn(score_grad, own_query)
+                dv_sum[:end, :] += dot_tn(probs.astype(BF16), own_grads)
+            dq = jnp.where(low_half(parts[0].shape), parts[0], parts[1]) * SCORE_SCALE
+            a_v[rows, dq_lanes] = (dq * cos[rows, :] - swap_halves(dq) * sin[rows, :]).astype(BF16)
+        return 0
+
+    lax.fori_loop(0, pairs, attend_pair, 0)
+    dk = dk_sum[...]
+    dk = dk + pltpu.roll(dk, HEAD_SIZE, 1)
+    dk = dk * cos[...] - swap_halves(dk) * sin[...]
+    dv = dv_sum[...]
+    dv = dv + pltpu.roll(dv, HEAD_SIZE, 1)
+    b_v[:, :LANES] = jnp.where(low_half(dk.shape), dk, dv).astype(BF16)
+    if planes > 3:
+        up_sum.advance(2)
+    out_sum.advance(1)
+
+    normed_load.wait()
+    dq_end = dq_at + own
+    for d in range(planes):
+        for j in range(rows_shard // ROWS):
+            lanes = slice(d * rows_shard + j * ROWS, d * rows_shard + (j + 1) * ROWS)
+            place = qkv_block_of(d).at[pl.ds(j * ROWS, ROWS)]
+            place[:, :own] = dot_tn(grad[:, lanes], a_v[:, dq_at:dq_end]).astype(BF16)
+            place[:, own:] = dot_tn(grad[:, lanes], b_v[:, :LANES]).astype(BF16)
+    qkv_sum.start()
+    if planes > 3:
+        out_sum.advance(2)
+    down_give.pass_on()
+
+    stream(x_in, jnp.int32(0), False)
+
+    def token_block(i, _):
+        rows = pl.ds(pl.multiple_of(i * ROWS, ROWS), ROWS)
+
+        @pl.when(i + 1 < blocks)
+        def _():
+            stream(x_in, i + 1, False)
+
+        normed_grad = dot_nt(a_v[rows, dq_at:dq_end], w_attn[:, :own]) + dot_nt(b_v[rows, :LANES], w_attn[:, own:columns])
+        stream(x_in, i, True)
+        x = hid_stage[lax.rem(i, 2)].astype(F32)
+        r1 = lax.rsqrt(jnp.mean(x * x, axis=-1, keepdims=True) + EPSILON)
+        gain_own[1:2, :] += jnp.sum(normed_grad * (x * r1), axis=0, keepdims=True)
+        weighted = normed_grad * attn_gain
+        mean = jnp.mean(weighted * x, axis=-1, keepdims=True)
+        piece = r1 * weighted - x * (r1 * r1 * r1 * mean)
+        for c in range(n):
+            lanes = slice(c * own_width, (c + 1) * own_width)
+            mine = jnp.where(me == c, hidden_grad[rows, :], 0.0)
+            grad[rows, lanes] = (piece[:, lanes] + mine).astype(BF16)
+        return 0
+
+    lax.fori_loop(0, blocks, token_block, 0)
+
+    def token_rows(c):
+        return grad.at[pl.ds(pl.multiple_of(c * per_device, per_device), per_device)]
+
+    third = scatter(2, token_rows, near3, far3, stage_wide.at[pl.ds(0, per_device)])
+    third.start()
+    gain_give = spread(5, gain_own, gain_all)
+    gain_mine = load(gain_own, gain_all.at[me], 21)
+    gain_give.start()
+    qkv_sum.advance(1)
+    gate_give = give(1, gate_sum, gate_all)
+    third.pass_on()
+    gain_give.pass_on()
+    if planes > 3:
+        qkv_sum.advance(2)
+    up_give = give(2, up_sum, up_all)
+    gain_give.finish()
+    gain_mine.wait()
+    gain_give.drain()
+    gain_own[...] = sum(gain_all[c] for c in range(n))
+    gain_sum.start()
+    token_out[...] = token_rows(me)[...].astype(F32)
+    third.finish(token_out)
+    gain_sum.advance(1)
+    out_give = give(3, out_sum, out_all)
+    if planes > 3:
+        gain_sum.advance(2)
+    gate_give.pass_on()
+    qkv_give = give(4, qkv_sum, qkv_all)
+    up_give.pass_on()
+    out_give.pass_on()
+    gain_sum.take(last)
+    gain_out[...] = gain_block_of(plane)[...]
+    qkv_give.pass_on()
+    for out, mine in spreads:
+        out.finish()
+        out.drain()
+        mine.wait()
+    for s in (second, third):
+        s.drain()
+    for s in (down_sum, gate_sum, up_sum, out_sum, qkv_sum, gain_sum):
+        s.drain()
+
+
+def backward(n, planes, heads, lengths, grad, saved, weights, cos, sin):
+    x, normed, q_rot, k_rot, v_rows, lse, att_all, hidden, normed2, a, b, mixed = saved
+    w_attn, w_gate, w_up, w_down, gains = weights
+    total, width = grad.shape
+    own = heads * HEAD_SIZE
+    own_width = width // n
+    own_ff = a.shape[1]
+    rows_shard = width // planes
+    slab = own_ff // planes
+    columns = own + LANES
+    chips = n // 2
+    per_device = total // n
+    col, row = (chips, total, own_width), (chips, per_device, width)
+    outs = [
+        ((per_device, width), F32),
+        ((8, rows_shard), F32),
+        ((n, slab, width), BF16),
+        ((n, rows_shard, own_ff), BF16),
+        ((n, rows_shard, own_ff), BF16),
+        ((n, rows_shard, own_width), BF16),
+        ((n, rows_shard, columns), BF16),
+        (col, BF16),
+        (col, BF16),
+        (col, BF16),
+        (col, BF16),
+        (row, BF16),
+        (row, BF16),
+        ((planes + 1, slab, width), BF16),
+        ((planes + 1, rows_shard, own_ff), BF16),
+        ((planes + 1, rows_shard, own_ff), BF16),
+        ((planes + 1, rows_shard, own_width), BF16),
+        ((planes + 1, rows_shard, columns), BF16),
+    ]
+    scratch = [
+        (w_attn.shape, BF16),
+        (w_gate.shape, BF16),
+        (w_up.shape, BF16),
+        (w_down.shape, BF16),
+        (w_down.shape, BF16),
+        (gains.shape, F32),
+        ((total, width), BF16),
+        ((total, own_ff), BF16),
+        ((total, own_ff), BF16),
+        ((n, total, own_width), BF16),
+        ((2, ROWS, width), BF16),
+        ((rows_shard, own_ff), BF16),
+        ((slab, width), BF16),
+        ((total, own_width), BF16),
+        ((total, own_width), F32),
+        (lse.shape, F32),
+        (cos.shape, F32),
+        (sin.shape, F32),
+        ((total, LANES), F32),
+        ((total, LANES), F32),
+        ((8, width), F32),
+        ((n, 8, width), F32),
+        ((planes + 1, 8, rows_shard), F32),
+        ((8, rows_shard), F32),
+    ]
+    steps = planes - 1
+    dma = pltpu.SemaphoreType.DMA
+    anywhere = pl.BlockSpec(memory_space=pl.ANY)
+    vmem = pl.BlockSpec(memory_space=pltpu.VMEM)
+    return pl.pallas_call(
+        functools.partial(backward_kernel, n, planes, heads),
+        in_specs=[pl.BlockSpec(memory_space=pltpu.SMEM)] + [anywhere] * 20,
+        out_specs=[vmem] * 2 + [anywhere] * (len(outs) - 2),
+        out_shape=[jax.ShapeDtypeStruct(*o) for o in outs],
+        scratch_shapes=[pltpu.VMEM(*s) for s in scratch]
+        + [
+            dma((6, 2, steps)),
+            dma((6, 2, steps)),
+            dma((3, n)),
+            dma((3, n)),
+            dma((6, n)),
+            dma((6, n)),
+            dma((24,)),
+            dma((2,)),
+            dma,
+        ],
+        compiler_params=pltpu.CompilerParams(
+            vmem_limit_bytes=60 * 1024 * 1024, collective_id=2, has_side_effects=True
+        ),
+        cost_estimate=pl.CostEstimate(
+            flops=16 * total * width * own_ff, bytes_accessed=100 * 1024 * 1024, transcendentals=0
+        ),
+        name="backward",
+    )(
+        lengths,
+        grad,
+        mixed,
+        a,
+        b,
+        hidden,
+        normed2,
+        normed,
+        x,
+        att_all,
+        q_rot,
+        k_rot,
+        v_rows,
+        lse,
+        cos,
+        sin,
+        w_attn,
+        w_gate,
+        w_up,
+        w_down,
+        gains,
+    )[:7]
+
+
+def kernel_fits(n, planes, total, width, own_ff):
+    held = 4 * width * own_ff + 2 * total * width + 2 * total * own_ff
+    return planes in (3, 4) and own_ff // planes >= total // n and n * own_ff >= 4 * width and 2 * held < 44 * 1024 * 1024 and (own_ff // planes) % LANES == 0
+
+
 def own_columns(array, index, width):
     return lax.dynamic_slice_in_dim(array, index * width, width, axis=1)
 
@@ -786,6 +1441,7 @@
     own_width = width // n_ctx
     ff = gate_weight.shape[1]
     slab = ff // (n_fsdp * n_ctx)
+    own_ff = slab * n_fsdp
     rows_shard = query_weight.shape[0]
 
     kv_head = me // sharing
@@ -848,60 +1504,83 @@
     hidden_own = own_columns(hidden_all, me, own_width)
     grad_result = reorder(cotangent_all, dealt_of_given)
 
-    mlp_grad = (RESIDUAL_SCALE * grad_result.astype(F32)).astype(BF16)
-
-    def settle(left, right):
-        return lax.psum_scatter(dot_tn(left, right).astype(BF16), "fsdp", scatter_dimension=0, tiled=True)
-
-    down_part = settle(mixed, mlp_grad)
-    ggrad, ugrad, hidden_part, mlp_gain_part = mlp_backward(
-        n_ctx, mlp_grad, a, b, hidden_all, gains[1], w_gate, w_up, w_down
-    )
-    hidden_sum = lax.psum_scatter(hidden_part, "ctx", scatter_dimension=0, tiled=False)
-    gate_part = settle(normed2, ggrad)
-    up_part = settle(normed2, ugrad)
-    hidden_grad, branch_grad, attended_part = branch_backward(
-        hidden_sum, own_columns(grad_result, me, own_width), w_out, n_ctx
-    )
-    attended_grad = lax.psum_scatter(attended_part, "ctx", scatter_dimension=0, tiled=False)
-    out_part = lax.psum_scatter(
-        jnp.einsum("ctk,to->cko", attended_all, branch_grad, preferred_element_type=F32)
-        .astype(BF16)
-        .reshape(width, own_width),
-        "fsdp",
-        scatter_dimension=0,
-        tiled=True,
-    )
-    dq, dkv = attention_backward(attended_grad, q_rot, k_rot, v_rows, lse, cos_table, sin_table, lengths[0])
-    qkv_part = settle(normed, jnp.concatenate([dq, dkv], axis=1))
-    token_part, attn_gain_part = token_backward(me_array, dq, dkv, w_qkv, x, gains[0], hidden_grad)
-    token_grad = lax.psum_scatter(token_part, "ctx", scatter_dimension=0, tiled=True).astype(F32)[None]
-
     both = jnp.concatenate([mixed, (hidden_own.astype(F32) * (1.0 / RESIDUAL_SCALE)).astype(BF16)], axis=1)
     column = lax.broadcasted_iota(jnp.int32, (own_width, width), 1) - me * own_width
     place = (column == lax.broadcasted_iota(jnp.int32, (own_width, width), 0)).astype(BF16)
     result_part = RESIDUAL_SCALE * dot_nn(reorder(both, given_of_dealt), jnp.concatenate([w_down, place], axis=0))
     activations = lax.psum_scatter(
-        after(result_part.astype(BF16), attended_grad), "ctx", scatter_dimension=0, tiled=True
+        result_part.astype(BF16), "ctx", scatter_dimension=0, tiled=True
     )[None]
 
-    def whole(part):
-        return lax.all_gather(part, "ctx", axis=0, tiled=False)
-
-    down_grad = whole(down_part).reshape(n_ctx * slab, width).astype(F32)
+    if kernel_fits(n_ctx, n_fsdp, total, width, own_ff):
+        token_grad, gain_rows, down_part, gate_part, up_part, out_part, qkv_part = backward(
+            n_ctx,
+            n_fsdp,
+            heads,
+            lengths[0],
+            grad_result,
+            (x, normed, q_rot, k_rot, v_rows, lse, attended_all, hidden_all, normed2, a, b, mixed),
+            (w_attn, w_gate, w_up, w_down, gains_all),
+            cos_table,
+            sin_table,
+        )
+        token_grad = token_grad[None]
+        own_gains = gain_rows[1::-1]
+    else:
+        mlp_grad = (RESIDUAL_SCALE * grad_result.astype(F32)).astype(BF16)
+
+        def settle(left, right):
+            return lax.psum_scatter(dot_tn(left, right).astype(BF16), "fsdp", scatter_dimension=0, tiled=True)
+
+        down_part = settle(mixed, mlp_grad)
+        ggrad, ugrad, hidden_part, mlp_gain_part = mlp_backward(
+            n_ctx, mlp_grad, a, b, hidden_all, gains[1], w_gate, w_up, w_down
+        )
+        hidden_sum = lax.psum_scatter(hidden_part, "ctx", scatter_dimension=0, tiled=False)
+        gate_part = settle(normed2, ggrad)
+        up_part = settle(normed2, ugrad)
+        hidden_grad, branch_grad, attended_part = branch_backward(
+            hidden_sum, own_columns(grad_result, me, own_width), w_out, n_ctx
+        )
+        attended_grad = lax.psum_scatter(attended_part, "ctx", scatter_dimension=0, tiled=False)
+        out_part = lax.psum_scatter(
+            jnp.einsum("ctk,to->cko", attended_all, branch_grad, preferred_element_type=F32)
+            .astype(BF16)
+            .reshape(width, own_width),
+            "fsdp",
+            scatter_dimension=0,
+            tiled=True,
+        )
+        dq, dkv = attention_backward(attended_grad, q_rot, k_rot, v_rows, lse, cos_table, sin_table, lengths[0])
+        qkv_part = settle(normed, jnp.concatenate([dq, dkv], axis=1))
+        token_part, attn_gain_part = token_backward(me_array, dq, dkv, w_qkv, x, gains[0], hidden_grad)
+        token_grad = lax.psum_scatter(token_part, "ctx", scatter_dimension=0, tiled=True).astype(F32)[None]
+
+        gain_parts = jnp.concatenate([attn_gain_part, mlp_gain_part], axis=0)
+        step = 1
+        while step < n_ctx:
+            gain_parts = gain_parts + lax.ppermute(gain_parts, "ctx", [(c, c ^ step) for c in range(n_ctx)])
+            step *= 2
+        gain_rows = gain_parts.reshape(2, n_fsdp, rows_shard).transpose(1, 0, 2).reshape(n_fsdp, 2 * rows_shard)
+        own_gains = lax.psum_scatter(gain_rows, "fsdp", scatter_dimension=0, tiled=True).reshape(2, rows_shard)
+        down_part, gate_part, up_part, out_part, qkv_part = [
+            lax.all_gather(p, "ctx", axis=0, tiled=False) for p in (down_part, gate_part, up_part, out_part, qkv_part)
+        ]
+
+    down_grad = down_part.reshape(n_ctx * slab, width).astype(F32)
     if slab % LANES == 0:
-        gate_grad = spread_columns(whole(gate_part), slab, n_fsdp)
-        up_grad = spread_columns(whole(up_part), slab, n_fsdp)
+        gate_grad = spread_columns(gate_part, slab, n_fsdp)
+        up_grad = spread_columns(up_part, slab, n_fsdp)
     else:
 
         def ff_whole(part):
-            pieces = whole(part).reshape(n_ctx, rows_shard, n_fsdp, slab)
+            pieces = part.reshape(n_ctx, rows_shard, n_fsdp, slab)
             return pieces.transpose(1, 2, 0, 3).reshape(rows_shard, ff).astype(F32)
 
         gate_grad = ff_whole(gate_part)
         up_grad = ff_whole(up_part)
-    out_grad = spread_columns(whole(out_part), own_width, 1)
-    qkv_all = whole(qkv_part)
+    out_grad = spread_columns(out_part, own_width, 1)
+    qkv_all = qkv_part
     query_grad = spread_columns(qkv_all, split, 1)
 
     def shared_heads(pieces):
@@ -911,13 +1590,6 @@
     key_grad = shared_heads(qkv_all[:, :, split : split + HEAD_SIZE])
     value_grad = shared_heads(qkv_all[:, :, split + HEAD_SIZE :])
 
-    gain_parts = jnp.concatenate([attn_gain_part, mlp_gain_part], axis=0)
-    step = 1
-    while step < n_ctx:
-        gain_parts = gain_parts + lax.ppermute(gain_parts, "ctx", [(c, c ^ step) for c in range(n_ctx)])
-        step *= 2
-    gain_rows = gain_parts.reshape(2, n_fsdp, rows_shard).transpose(1, 0, 2).reshape(n_fsdp, 2 * rows_shard)
-    own_gains = lax.psum_scatter(gain_rows, "fsdp", scatter_dimension=0, tiled=True).reshape(2, rows_shard)
     return (
         activations,
         token_grad,

time: 1150 us -> 795 us (0.69)
  waiting for transfers between devices: 578 us -> 0.72 us
  Pallas kernels: 386 us -> 702 us
  matrix products: 61.1 us -> 13 us
  local copies, waits for them, and re-layouts: 41.4 us -> 26.9 us
  blocking collectives: 12.9 us -> 0 us
    reduce_scatter x9 -> x1, waiting for transfers between devices: 464 us -> 0.01 us  [local(): lax.psum_scatter(result_part.astype(BF16), 'ctx', scatter_dimension=0, ti...]
    pallas_call x8 -> x5, Pallas kernels: 136 us -> 452 us  [the longest x1 416 us: backward(): pl.pallas_call(functools.partial(backward_kernel, n, planes, heads), in_s...]
    all_gather x5 -> x0, waiting for transfers between devices: 110 us -> none  [whole(): return lax.all_gather(part, 'ctx', axis=0, tiled=False)]
    dot_general x5 -> x0, matrix products: 48.1 us -> none  [the longest x4 42.5 us: dot_tn(): lax.dot_general(a, b, (((0,), (0,)), ((), ())), preferred_element_type=F32)]
    unnamed x1 -> x0, blocking collectives: 12.9 us -> none
  transfers between devices with their start and end apart: 18 -> 2, of which waited for: 14 -> 0; matrix products, arithmetic and copies ran while one was open for 11% -> 9% of each run, Pallas kernels for 31% -> 89%
where the time goes in v4:
time: 795 us; the launch traced here: 787 us
  Pallas kernels  702 us (88%)
  other arithmetic  29.9 us (4%)
  local copies, waits for them, and re-layouts  26.9 us (3%)
  between operations  14.4 us (2%)
  matrix products  13 us (2%)
    pallas_call x1, Pallas kernels, backward(): pl.pallas_call(functools.partial(backward_kernel, n, planes, heads), in_s...  416 us
    pallas_call x1, Pallas kernels, forward(): pl.pallas_call(functools.partial(forward_kernel, n, planes, heads), in_sp...  250 us
    pallas_call x4, Pallas kernels, spread_columns(): pl.pallas_call(spread_kernel, grid=(groups, rows // tile), in_specs=[pl.B...  35.9 us
  transfers between devices with their start and end apart: 2, of which 0 were waited for; matrix products, arithmetic and copies ran while one was open for 9% of the time, Pallas kernels for 89%

profile of v4, /device:TPU:9, one launch (start us, length us, event | category | flops | bytes accessed | tf_op | source)
XLA Modules:
  0.0 786.7 jit_solution(11688367981520622020)
XLA Ops:
  10.4 1.1 constant_dynamic-slice_fusion.10
  13.6 1.7 constant_dynamic-slice_fusion.4
  15.3 1.1 pad_maximum_fusion.2.up_shard
  17.5 2.4 constant_dynamic-slice_fusion.down_shard
  19.9 2.8 fusion.4
  22.7 2.4 pad_maximum_fusion.3
  25.7 249.9 %forward.1 = (bf16[1536,2048]{1,0:T(8,128)(2,1)}, bf16[1536,2048]{1,0:T(8,128)(2,1)}, bf16[1536,256]{1,0:T(8,128)(2,1)}, bf16[1536,128]{1,0:T(8,128)(2,1)}, bf16...) custom-call(s32[2]{0:T(128)} %bitcast.38, ...), custom_call_target="tpu_custom_call" | custom-call | flops 16911433728 | bytes 62914560 | tf_op jit(solution)/shard_map/forward/pallas_call | solution.py:738
  275.6 1.3 multiply_convert_fusion.1
  276.9 4.2 pad_maximum_fusion
  281.1 4.8 gather_fusion
  286.2 13.0 %multiply_convert_fusion = bf16[1536,2048]{1,0:T(8,128)(2,1)} fusion(bf16[1536,1280]{1,0:T(8,128)(2,1)} %bitcast.32, bf16[256,2048]{1,0:T(8,128)(2,1)S(1)} %fusion.3, bf16[1024,2048]{1,0:T(8,128)(2,1)} %get-tuple-element.37.down_in), kind=kOutput, calls=%fused_computation.2 | convolution fusion | flops 8069840896 | bytes 15466496 | tf_op jit(solution)/shard_map/dot_general | solution.py:26
  300.0 6.4 gather_fusion.1
  306.5 415.8 %backward.1 = (f32[192,2048]{1,0:T(8,128)}, f32[8,512]{1,0:T(8,128)}, bf16[8,256,2048]{2,1,0:T(8,128)(2,1)}, bf16[8,512,1024]{2,1,0:T(8,128)(2,1)}, bf16[8,512,1...) custom-call(s32[2]{0:T(128)} %bitcast.39, ...), custom_call_target="tpu_custom_call" | custom-call | flops 51539607552 | bytes 104857600 | tf_op jit(solution)/shard_map/backward/pallas_call | solution.py:1355
  722.2 13.7 %spread_columns.6 = f32[512,8192]{1,0:T(8,128)} custom-call(bf16[8,512,1024]{2,1,0:T(8,128)(2,1)} %get-tuple-element.56.in_ref), custom_call_target="tpu_custom_call" | custom-call | bytes 25165824 | tf_op jit(solution)/shard_map/spread_columns/pallas_call | solution.py:285
  735.9 13.7 %spread_columns.7 = f32[512,8192]{1,0:T(8,128)} custom-call(bf16[8,512,1024]{2,1,0:T(8,128)(2,1)} %get-tuple-element.57.in_ref), custom_call_target="tpu_custom_call" | custom-call | bytes 25165824 | tf_op jit(solution)/shard_map/spread_columns/pallas_call | solution.py:285
  749.6 4.3 spread_columns.4
  753.9 1.8 convert_bitcast_fusion
  755.7 2.2 copy.35
  757.9 1.3 copy.37
  759.8 1.3 copy.38
  761.1 4.2 spread_columns.5
  765.3 1.4 fusion.6
  766.7 11.8 %bitcast_convert_fusion = f32[2048,2048]{1,0:T(8,128)} fusion(bf16[8,256,2048]{2,1,0:T(8,128)(2,1)} %get-tuple-element.58), kind=kLoop, calls=%fused_computation.3 | loop fusion | flops 4194304 | bytes 25165824 | tf_op jit(solution)/shard_map/convert_element_type | solution.py:1570
  778.5 1.1 copy.40
  (34 shorter events, 8.5 us)
Async XLA Ops:
  7.2 292.8 %all-gather.3.cloned.1.call-start = ((), (), s32[]{:S(2)}) async-start(), calls=%async_computation.2 | async-start | bytes 7077888 | tf_op jit(solution)/shard_map/all_gather | solution.py:1485
  7.9 770.6 %reduce-scatter.2.cloned.1.call-start = ((), (), s32[]{:S(2)}) async-start(), calls=%async_computation.1 | async-start | bytes 7077888 | tf_op jit(solution)/shard_map/reduce_scatter | solution.py:1511
  299.2 0.7 copy-start.2
  749.6 4.4 copy-start
  766.7 11.8 %copy-start.1 = (f32[192,2048]{1,0:T(8,128)S(1)}, f32[192,2048]{1,0:T(8,128)}, u32[]{:S(2)}) copy-start(f32[192,2048]{1,0:T(8,128)} %get-tuple-element.52) | copy-start | bytes 4718596
Sparse Core Ops, SparseCore 0:
  9.9 75.0 all-gather.2
  299.3 85.3 reduce-scatter.1

commit v5 on v4

--- a/solution.py
+++ b/solution.py
@@ -385,6 +385,9 @@
             self.copy(self.src, self.at(self.chips - k), k, self.me).wait_recv()
             self.relay(k).start()
 
+    def late(self):
+        pass
+
     def finish(self):
         other = 1 - 2 * self.core
         for k in range(self.chips):
@@ -396,6 +399,84 @@
             self.out(k).wait_send()
         for k in range(self.chips):
             self.relay(k).wait_send()
+
+
+class Spread4:
+    def __init__(self, src, slot, n, me, send_sem, recv_sem):
+        self.src, self.slot, self.me = src, slot, me
+        self.send_sem, self.recv_sem = send_sem, recv_sem
+        self.core = lax.rem(me, 2)
+        self.other = 1 - self.core
+        chip = me // 2
+        self.near, self.side, self.far = square(chip)
+        self.chip = chip
+        self.half = src.shape[0] // 2
+
+    def copy(self, src, dst, sem, to):
+        return pltpu.make_async_remote_copy(
+            src_ref=src,
+            dst_ref=dst,
+            send_sem=self.send_sem.at[sem],
+            recv_sem=self.recv_sem.at[sem],
+            device_id={"ctx": to},
+            device_id_type=MESH,
+        )
+
+    def part(self, owner, which):
+        return self.slot(owner).at[pl.ds(which * self.half, self.half)]
+
+    def out(self, sem):
+        chip = self.near if sem == 1 else self.side
+        return self.copy(self.src, self.slot(self.me), sem, chip * 2 + self.core)
+
+    def onward(self, sem):
+        origin, to, which = (self.near, self.side, 0) if sem == 3 else (self.side, self.near, 1)
+        owner = origin * 2 + self.core
+        return self.copy(self.part(owner, which), self.part(owner, which), sem, to * 2 + self.core)
+
+    def relay(self, k):
+        owner = (self.chip, self.near, self.side, self.far)[k] * 2 + self.core
+        src = self.slot(owner) if k else self.src
+        return self.copy(src, self.slot(owner), 4 + k, self.chip * 2 + self.other)
+
+    def start(self):
+        self.out(1).start()
+        self.out(2).start()
+        self.relay(0).start()
+
+    def pass_on(self):
+        for k, chip in ((1, self.near), (2, self.side)):
+            owner = chip * 2 + self.core
+            self.copy(self.src, self.slot(owner), k, self.me).wait_recv()
+            self.onward(3 if k == 1 else 0).start()
+            self.relay(k).start()
+
+    def late(self):
+        owner = self.far * 2 + self.core
+        for sem, which in ((3, 0), (0, 1)):
+            self.copy(self.part(owner, which), self.part(owner, which), sem, self.me).wait_recv()
+        self.relay(3).start()
+
+    def finish(self):
+        for k, chip in enumerate((self.chip, self.near, self.side, self.far)):
+            owner = chip * 2 + self.other
+            self.copy(self.slot(owner), self.slot(owner), 4 + k, self.me).wait_recv()
+
+    def drain(self):
+        for sem in (1, 2):
+            self.out(sem).wait_send()
+        for sem in (3, 0):
+            self.onward(sem).wait_send()
+        for k in range(4):
+            self.relay(k).wait_send()
+
+
+def square(chip):
+    return chip + 1 - 2 * lax.rem(chip, 2), chip + 2 - 4 * (chip // 2), 3 - chip
+
+
+def spread_over(n, src, *rest):
+    return (Spread4 if n == 8 and src.shape[0] % 32 == 0 else Spread)(src, *rest)
 
 
 def greet(n, planes, me, plane, across):
@@ -511,8 +592,8 @@
     attn_chain.start(0)
     loads[1].wait()
     gain_chain.start(0)
-    x_spread = Spread(
-        tokens_ref, lambda c: x_all.at[pl.ds(c * per_device, per_device)], n, me, c_send.at[0], c_recv.at[0]
+    x_spread = spread_over(
+        n, tokens_ref, lambda c: x_all.at[pl.ds(c * per_device, per_device)], n, me, c_send.at[0], c_recv.at[0]
     )
     x_spread.start()
     for load in loads[2:]:
@@ -524,6 +605,7 @@
     gate_chain.start(0)
     up_chain.start(0)
     x_spread.pass_on()
+    x_spread.late()
     x_spread.finish()
     x_copy = pltpu.make_async_copy(x_all, x_out, keep_sem.at[0])
     x_copy.start()
@@ -598,7 +680,7 @@
         return 0
 
     lax.fori_loop(0, pairs, attend_pair, 0)
-    att_spread = Spread(own_att, lambda c: att_all.at[c], n, me, c_send.at[1], c_recv.at[1])
+    att_spread = spread_over(n, own_att, lambda c: att_all.at[c], n, me, c_send.at[1], c_recv.at[1])
     x_copy.wait()
     x_spread.drain()
     att_spread.start()
@@ -610,6 +692,7 @@
         gate_chain.advance(1)
         up_chain.advance(1)
     att_spread.pass_on()
+    att_spread.late()
     own_a.wait()
     att_spread.finish()
     keep(att_all, att_out, 8)
@@ -626,7 +709,7 @@
     def hid_slot(c):
         return x_all.at[:, pl.ds(pl.multiple_of(c * own_width, LANES), own_width)]
 
-    hid_spread = Spread(own_hid, hid_slot, n, me, c_send.at[2], c_recv.at[2])
+    hid_spread = spread_over(n, own_hid, hid_slot, n, me, c_send.at[2], c_recv.at[2])
     hid_spread.start()
     own_h = pltpu.make_async_copy(own_hid, hid_slot(me), keep_sem.at[5])
     own_h.start()
@@ -635,6 +718,7 @@
         up_chain.advance(step)
     down_chain.start(0)
     hid_spread.pass_on()
+    hid_spread.late()
     own_h.wait()
     hid_spread.finish()
     keep(x_all, hid_out, 9)
@@ -754,19 +838,19 @@
     )(lengths, tokens, attn_shard, gate_shard, up_shard, down_shard, gain_shard, cos, sin)
 
 
-CHUNK = 64
-
-
 def add_into(dst, src):
+    rows_in = dst.shape[0]
+    chunk = 64 if rows_in % 64 == 0 else 32
+
     def step(i, _):
-        rows = pl.ds(pl.multiple_of(i * CHUNK, CHUNK), CHUNK)
+        rows = pl.ds(pl.multiple_of(i * chunk, chunk), chunk)
         dst[rows, :] = (dst[rows, :].astype(F32) + src[rows, :].astype(F32)).astype(dst.dtype)
         return 0
 
-    if dst.shape[0] <= CHUNK:
+    if rows_in < chunk:
         dst[...] = dst[...] + src[...]
     else:
-        lax.fori_loop(0, dst.shape[0] // CHUNK, step, 0)
+        lax.fori_loop(0, rows_in // chunk, step, 0)
 
 
 def fetch(src, dst, sem):
@@ -838,58 +922,80 @@
 
 
 class Scatter:
-    def __init__(self, block, near, far, stage, n, me, send_sem, recv_sem, load_sem):
-        self.block, self.near, self.far, self.stage = block, near, far, stage
+    def __init__(self, block, near, far, stage, me, send_sem, recv_sem, load_sem):
+        self.block, self.landed, self.far, self.stage = block, near, far, stage
         self.send_sem, self.recv_sem, self.load_sem = send_sem, recv_sem, load_sem
-        self.chips = n // 2
-        self.me, self.chip, self.core = me, me // 2, lax.rem(me, 2)
-
-    def target(self, k, core):
-        return lax.rem(self.chip + k, self.chips) * 2 + core
-
-    def copy(self, k, sem, src, dst, to):
+        self.core = lax.rem(me, 2)
+        self.chip = me // 2
+        self.chips = (self.chip, *square(self.chip))
+        self.half = stage.shape[0] // 2
+
+    def rows(self, which):
+        return pl.ds(which * self.half, self.half)
+
+    def own(self, k):
+        return self.block(self.chips[k] * 2 + self.core)
+
+    def copy(self, src, dst, sem, chip, core):
         return pltpu.make_async_remote_copy(
             src_ref=src,
-            dst_ref=dst.at[k],
+            dst_ref=dst,
             send_sem=self.send_sem.at[sem],
             recv_sem=self.recv_sem.at[sem],
-            device_id={"ctx": to},
+            device_id={"ctx": chip * 2 + core},
             device_id_type=MESH,
         )
 
     def first(self, k):
         other = 1 - self.core
-        return self.copy(k, k, self.block(self.target(k, other)), self.near, self.chip * 2 + other)
-
-    def second(self, k):
-        target = self.target(k, self.core)
-        return self.copy(k, self.chips + k, self.block(target), self.far, target)
+        return self.copy(self.block(self.chips[k] * 2 + other), self.landed.at[k], k, self.chip, other)
+
+    def second(self, k, to, which):
+        place = self.far.at[to - 1 if k == to else 2, self.rows(which)]
+        sem = 4 + 2 * (to - 1) + which if k == to else 7 + to
+        return self.copy(self.own(k).at[self.rows(which)], place, sem, self.chips[to], self.core)
 
     def start(self):
-        for k in range(self.chips):
+        for k in (3, 1, 2, 0):
             self.first(k).start()
 
+    def add(self, k):
+        self.first(k).wait_recv()
+        fetch(self.landed.at[k], self.stage, self.load_sem)
+        add_into(self.own(k), self.stage)
+
     def pass_on(self):
-        for k in range(1, self.chips):
-            self.first(k).wait_recv()
-            fetch(self.near.at[k], self.stage, self.load_sem)
-            add_into(self.block(self.target(k, self.core)), self.stage)
-            self.second(k).start()
+        self.add(3)
+        self.second(3, 1, 0).start()
+        self.second(3, 2, 1).start()
+        self.add(1)
+        self.second(1, 1, 0).start()
+        self.add(2)
+        self.second(2, 2, 1).start()
+
+    def late(self):
+        for to, which, k in ((1, 0, 2), (2, 1, 1)):
+            self.second(3, to, which).wait_recv()
+            place = self.stage.at[self.rows(which)]
+            fetch(self.far.at[2, self.rows(which)], place, self.load_sem)
+            add_into(self.own(k).at[self.rows(which)], place)
+            self.second(k, k, which).start()
 
     def finish(self, total):
         self.first(0).wait_recv()
-        fetch(self.near.at[0], self.stage, self.load_sem)
+        fetch(self.landed.at[0], self.stage, self.load_sem)
         add_into(total, self.stage)
-        for k in range(1, self.chips):
-            self.second(k).wait_recv()
-            fetch(self.far.at[k], self.stage, self.load_sem)
+        for k in (1, 2):
+            for which in (0, 1):
+                self.second(k, k, which).wait_recv()
+            fetch(self.far.at[k - 1], self.stage, self.load_sem)
             add_into(total, self.stage)
 
     def drain(self):
-        for k in range(self.chips):
+        for k in range(4):
             self.first(k).wait_send()
-        for k in range(1, self.chips):
-            self.second(k).wait_send()
+        for k, to, which in ((3, 1, 0), (3, 2, 1), (1, 1, 0), (1, 1, 1), (2, 2, 0), (2, 2, 1)):
+            self.second(k, to, which).wait_send()
 
 
 def backward_kernel(
@@ -1021,12 +1127,11 @@
     gain_sum = settle(5, gain_block_of, gain_landed, gain_stage)
 
     def spread(index, src, dst):
-        return Spread(src, lambda c: dst.at[c], n, me, g_send.at[index], g_recv.at[index])
+        return spread_over(n, src, lambda c: dst.at[c], n, me, g_send.at[index], g_recv.at[index])
 
     spreads = []
 
     def give(index, sums, dst):
-        sums.take(last)
         src = sums.block(plane)
         mine = load(src, dst.at[me], 16 + index)
         out = spread(index, src, dst)
@@ -1035,7 +1140,7 @@
         return out
 
     def scatter(index, block, near, far, stage):
-        return Scatter(block, near, far, stage, n, me, s_send.at[index], s_recv.at[index], add_sem)
+        return Scatter(block, near, far, stage, me, s_send.at[index], s_recv.at[index], add_sem)
 
     grad_load.wait()
 
@@ -1084,6 +1189,11 @@
         b_v[rows, :] = ugrad
         normed_grad = dot_nt(ggrad, w_gate[...]) + dot_nt(ugrad, w_up[...])
         stream(hidden_in, i, True)
+
+        @pl.when(i == blocks - 2)
+        def _():
+            down_sum.advance(1)
+
         hidden = hid_stage[lax.rem(i, 2)].astype(F32)
         r2 = lax.rsqrt(jnp.mean(hidden * hidden, axis=-1, keepdims=True) + EPSILON)
         gain_own[0:1, :] += jnp.sum(normed_grad * (hidden * r2), axis=0, keepdims=True)
@@ -1098,7 +1208,6 @@
     first = scatter(0, lambda c: part.at[c], near1, far1, stage_col)
     first.start()
     normed2_load = load(normed2_in, grad, 8)
-    down_sum.advance(1)
     normed2_load.wait()
 
     def columns_times(right, out):
@@ -1113,7 +1222,8 @@
     gate_sum.start()
     first.pass_on()
     columns_times(b_v, w_up)
-    up_sum.start()
+    first.late()
+    down_sum.advance(2)
 
     att_loads = [load(att_in.at[c], grad.at[:, pl.ds(c * own, own)], c) for c in range(n)]
     own_grad = load(grad_in.at[:, pl.ds(pl.multiple_of(me * own_width, LANES), own_width)], b_v.at[:, pl.ds(LANES, own_width)], 8)
@@ -1133,8 +1243,6 @@
     lax.fori_loop(0, blocks, begin, 0)
     first.finish(hidden_grad)
     first.drain()
-    if planes > 3:
-        down_sum.advance(2)
 
     def branch_block(i, _):
         rows = pl.ds(pl.multiple_of(i * ROWS, ROWS), ROWS)
@@ -1155,13 +1263,13 @@
         place = out_block_of(c // heads_per_shard).at[pl.ds((c % heads_per_shard) * own, own)]
         place[...] = dot_tn(grad[:, c * own : (c + 1) * own], b_v[:, LANES : LANES + own_width]).astype(BF16)
     second.pass_on()
-    up_sum.advance(1)
-    out_sum.start()
     normed_load = load(normed_in, grad, 15)
+    down_sum.take(last)
+    up_sum.start()
+    second.late()
+    second.finish(part.at[me])
     down_give = give(0, down_sum, down_all)
-    second.finish(part.at[me])
-    if planes > 3:
-        gate_sum.advance(2)
+    gate_sum.advance(2)
 
     for copy in (q_load, k_load, v_load, lse_load, cos_load, sin_load):
         copy.wait()
@@ -1195,6 +1303,12 @@
                 dv_sum[:end, :] += dot_tn(probs.astype(BF16), own_grads)
             dq = jnp.where(low_half(parts[0].shape), parts[0], parts[1]) * SCORE_SCALE
             a_v[rows, dq_lanes] = (dq * cos[rows, :] - swap_halves(dq) * sin[rows, :]).astype(BF16)
+
+        @pl.when(pair == 0)
+        def _():
+            down_give.pass_on()
+            up_sum.advance(1)
+
         return 0
 
     lax.fori_loop(0, pairs, attend_pair, 0)
@@ -1204,9 +1318,11 @@
     dv = dv_sum[...]
     dv = dv + pltpu.roll(dv, HEAD_SIZE, 1)
     b_v[:, :LANES] = jnp.where(low_half(dk.shape), dk, dv).astype(BF16)
-    if planes > 3:
-        up_sum.advance(2)
-    out_sum.advance(1)
+    down_give.late()
+    gate_sum.take(last)
+    gate_give = give(1, gate_sum, gate_all)
+    up_sum.advance(2)
+    out_sum.start()
 
     normed_load.wait()
     dq_end = dq_at + own
@@ -1216,10 +1332,9 @@
             place = qkv_block_of(d).at[pl.ds(j * ROWS, ROWS)]
             place[:, :own] = dot_tn(grad[:, lanes], a_v[:, dq_at:dq_end]).astype(BF16)
             place[:, own:] = dot_tn(grad[:, lanes], b_v[:, :LANES]).astype(BF16)
+    gate_give.pass_on()
+    out_sum.advance(1)
     qkv_sum.start()
-    if planes > 3:
-        out_sum.advance(2)
-    down_give.pass_on()
 
     stream(x_in, jnp.int32(0), False)
 
@@ -1254,13 +1369,14 @@
     gain_give = spread(5, gain_own, gain_all)
     gain_mine = load(gain_own, gain_all.at[me], 21)
     gain_give.start()
+    gate_give.late()
+    third.pass_on()
+    out_sum.advance(2)
+    gain_give.pass_on()
+    up_sum.take(last)
+    up_give = give(2, up_sum, up_all)
+    third.late()
     qkv_sum.advance(1)
-    gate_give = give(1, gate_sum, gate_all)
-    third.pass_on()
-    gain_give.pass_on()
-    if planes > 3:
-        qkv_sum.advance(2)
-    up_give = give(2, up_sum, up_all)
     gain_give.finish()
     gain_mine.wait()
     gain_give.drain()
@@ -1268,17 +1384,21 @@
     gain_sum.start()
     token_out[...] = token_rows(me)[...].astype(F32)
     third.finish(token_out)
+    out_sum.take(last)
+    out_give = give(3, out_sum, out_all)
+    up_give.pass_on()
+    qkv_sum.advance(2)
     gain_sum.advance(1)
-    out_give = give(3, out_sum, out_all)
-    if planes > 3:
-        gain_sum.advance(2)
-    gate_give.pass_on()
+    out_give.pass_on()
+    up_give.late()
+    gain_sum.advance(2)
+    out_give.late()
+    qkv_sum.take(last)
     qkv_give = give(4, qkv_sum, qkv_all)
-    up_give.pass_on()
-    out_give.pass_on()
     gain_sum.take(last)
     gain_out[...] = gain_block_of(plane)[...]
     qkv_give.pass_on()
+    qkv_give.late()
     for out, mine in spreads:
         out.finish()
         out.drain()
@@ -1361,8 +1481,8 @@
         + [
             dma((6, 2, steps)),
             dma((6, 2, steps)),
-            dma((3, n)),
-            dma((3, n)),
+            dma((3, 10)),
+            dma((3, 10)),
             dma((6, n)),
             dma((6, n)),
             dma((24,)),
@@ -1403,7 +1523,7 @@
 
 def kernel_fits(n, planes, total, width, own_ff):
     held = 4 * width * own_ff + 2 * total * width + 2 * total * own_ff
-    return planes in (3, 4) and own_ff // planes >= total // n and n * own_ff >= 4 * width and 2 * held < 44 * 1024 * 1024 and (own_ff // planes) % LANES == 0
+    return planes == 4 and n == 8 and own_ff // planes >= total // n and n * own_ff >= 4 * width and 2 * held < 44 * 1024 * 1024 and (own_ff // planes) % LANES == 0
 
 
 def own_columns(array, index, width):

time: 795 us -> 726 us (0.913)
  Pallas kernels: 702 us -> 634 us
    pallas_call x1, Pallas kernels: 416 us -> 348 us  [backward(): pl.pallas_call(functools.partial(backward_kernel, n, planes, heads), in_s...]
  transfers between devices with their start and end apart: 2 -> 2, of which waited for: 0 -> 0; matrix products, arithmetic and copies ran while one was open for 9% -> 9% of each run, Pallas kernels for 89% -> 88%
where the time goes in v5:
time: 726 us; the launch traced here: 719 us
  Pallas kernels  634 us (87%)
  other arithmetic  29.9 us (4%)
  local copies, waits for them, and re-layouts  26.9 us (4%)
  between operations  14.5 us (2%)
  matrix products  13 us (2%)
    pallas_call x1, Pallas kernels, backward(): pl.pallas_call(functools.partial(backward_kernel, n, planes, heads), in_s...  348 us
    pallas_call x1, Pallas kernels, forward(): pl.pallas_call(functools.partial(forward_kernel, n, planes, heads), in_sp...  250 us
    pallas_call x4, Pallas kernels, spread_columns(): pl.pallas_call(spread_kernel, grid=(groups, rows // tile), in_specs=[pl.B...  35.9 us
  transfers between devices with their start and end apart: 2, of which 0 were waited for; matrix products, arithmetic and copies ran while one was open for 9% of the time, Pallas kernels for 88%

profile of v5, /device:TPU:9, one launch (start us, length us, event | category | flops | bytes accessed | tf_op | source)
XLA Modules:
  0.0 718.8 jit_solution(14583497643476148981)
XLA Ops:
  10.4 1.1 constant_dynamic-slice_fusion.10
  13.6 1.7 constant_dynamic-slice_fusion.4
  15.3 1.1 pad_maximum_fusion.2.up_shard
  17.5 2.4 constant_dynamic-slice_fusion.down_shard
  19.9 2.8 fusion.4
  22.7 2.4 pad_maximum_fusion.3
  25.7 249.9 %forward.1 = (bf16[1536,2048]{1,0:T(8,128)(2,1)}, bf16[1536,2048]{1,0:T(8,128)(2,1)}, bf16[1536,256]{1,0:T(8,128)(2,1)}, bf16[1536,128]{1,0:T(8,128)(2,1)}, bf16...) custom-call(s32[2]{0:T(128)} %bitcast.38, ...), custom_call_target="tpu_custom_call" | custom-call | flops 16911433728 | bytes 62914560 | tf_op jit(solution)/shard_map/forward/pallas_call | solution.py:822
  275.7 1.3 multiply_convert_fusion.1
  277.0 4.2 pad_maximum_fusion
  281.1 4.8 gather_fusion
  286.2 13.0 %multiply_convert_fusion = bf16[1536,2048]{1,0:T(8,128)(2,1)} fusion(bf16[1536,1280]{1,0:T(8,128)(2,1)} %bitcast.32, bf16[256,2048]{1,0:T(8,128)(2,1)S(1)} %fusion.3, bf16[1024,2048]{1,0:T(8,128)(2,1)} %get-tuple-element.37.down_in), kind=kOutput, calls=%fused_computation.2 | convolution fusion | flops 8069840896 | bytes 15466496 | tf_op jit(solution)/shard_map/dot_general | solution.py:26
  300.0 6.4 gather_fusion.1
  306.5 347.8 %backward.1 = (f32[192,2048]{1,0:T(8,128)}, f32[8,512]{1,0:T(8,128)}, bf16[8,256,2048]{2,1,0:T(8,128)(2,1)}, bf16[8,512,1024]{2,1,0:T(8,128)(2,1)}, bf16[8,512,1...) custom-call(s32[2]{0:T(128)} %bitcast.39, ...), custom_call_target="tpu_custom_call" | custom-call | flops 51539607552 | bytes 104857600 | tf_op jit(solution)/shard_map/backward/pallas_call | solution.py:1475
  654.3 13.7 %spread_columns.6 = f32[512,8192]{1,0:T(8,128)} custom-call(bf16[8,512,1024]{2,1,0:T(8,128)(2,1)} %get-tuple-element.56.in_ref), custom_call_target="tpu_custom_call" | custom-call | bytes 25165824 | tf_op jit(solution)/shard_map/spread_columns/pallas_call | solution.py:285
  667.9 13.7 %spread_columns.7 = f32[512,8192]{1,0:T(8,128)} custom-call(bf16[8,512,1024]{2,1,0:T(8,128)(2,1)} %get-tuple-element.57.in_ref), custom_call_target="tpu_custom_call" | custom-call | bytes 25165824 | tf_op jit(solution)/shard_map/spread_columns/pallas_call | solution.py:285
  681.6 4.3 spread_columns.4
  686.0 1.8 convert_bitcast_fusion
  687.7 2.2 copy.35
  689.9 1.3 copy.37
  691.8 1.3 copy.38
  693.1 4.2 spread_columns.5
  697.3 1.4 fusion.6
  698.7 11.8 %bitcast_convert_fusion = f32[2048,2048]{1,0:T(8,128)} fusion(bf16[8,256,2048]{2,1,0:T(8,128)(2,1)} %get-tuple-element.58), kind=kLoop, calls=%fused_computation.3 | loop fusion | flops 4194304 | bytes 25165824 | tf_op jit(solution)/shard_map/convert_element_type | solution.py:1690
  710.5 1.1 copy.40
  (34 shorter events, 8.5 us)
Async XLA Ops:
  7.2 292.8 %all-gather.3.cloned.1.call-start = ((), (), s32[]{:S(2)}) async-start(), calls=%async_computation.2 | async-start | bytes 7077888 | tf_op jit(solution)/shard_map/all_gather | solution.py:1605
  7.9 702.6 %reduce-scatter.2.cloned.1.call-start = ((), (), s32[]{:S(2)}) async-start(), calls=%async_computation.1 | async-start | bytes 7077888 | tf_op jit(solution)/shard_map/reduce_scatter | solution.py:1631
  299.2 0.7 copy-start.2
  681.6 4.4 copy-start
  698.7 11.8 %copy-start.1 = (f32[192,2048]{1,0:T(8,128)S(1)}, f32[192,2048]{1,0:T(8,128)}, u32[]{:S(2)}) copy-start(f32[192,2048]{1,0:T(8,128)} %get-tuple-element.52) | copy-start | bytes 4718596
Sparse Core Ops, SparseCore 0:
  9.9 59.0 all-gather.2
  299.3 67.5 reduce-scatter.1

commit v6 on v5

--- a/solution.py
+++ b/solution.py
@@ -19,7 +19,7 @@
 ROWS = 256
 BF16 = jnp.bfloat16
 F32 = jnp.float32
-VMEM_LIMIT = 56 * 1024 * 1024
+VMEM_LIMIT = 59 * 1024 * 1024
 
 
 def dot_nn(a, b):
@@ -272,6 +272,66 @@
     )(me, dq, dkv, w_qkv, x, gain, hidden_grad)
 
 
+def finish_kernel(slab, gate_ref, up_ref, down_ref, out_ref, qkv_ref, gate_out, up_out, down_out, out_out, q_out, k_out, v_out):
+    n = gate_ref.shape[0]
+    for src, dst, piece in ((gate_ref, gate_out, slab), (up_ref, up_out, slab), (out_ref, out_out, out_ref.shape[2])):
+        for c in range(n):
+            for f in range(src.shape[2] // piece):
+                at = (f * n + c) * piece
+                dst[:, at : at + piece] = src[c, :, f * piece : (f + 1) * piece].astype(F32)
+    down_out[...] = down_ref[...].astype(F32)
+    split = qkv_ref.shape[2] - LANES
+    for c in range(n):
+        q_out[:, c * split : (c + 1) * split] = qkv_ref[c, :, :split].astype(F32)
+    for pair in range(n // 2):
+        even = qkv_ref[2 * pair, :, split:].astype(F32)
+        odd = qkv_ref[2 * pair + 1, :, split:].astype(F32)
+        low = low_half(even.shape)
+        lanes = slice(pair * LANES, (pair + 1) * LANES)
+        k_out[:, lanes] = jnp.where(low, even, pltpu.roll(odd, HEAD_SIZE, 1))
+        v_out[:, lanes] = jnp.where(low, pltpu.roll(even, HEAD_SIZE, 1), odd)
+
+
+def finish(slab, gate, up, down, out, qkv):
+    n, rows, own_ff = gate.shape
+    width = n * out.shape[2]
+    steps = 16
+    tile, down_tile = rows // steps, down.shape[0] // steps
+    kv = n * HEAD_SIZE
+
+    def by_device(columns):
+        return pl.BlockSpec((n, tile, columns), lambda i: (0, i, 0))
+
+    def flat(height, columns):
+        return pl.BlockSpec((height, columns), lambda i: (i, 0))
+
+    outs = [
+        (flat(tile, n * own_ff), (rows, n * own_ff)),
+        (flat(tile, n * own_ff), (rows, n * own_ff)),
+        (flat(down_tile, width), down.shape),
+        (flat(tile, width), (rows, width)),
+        (flat(tile, width), (rows, width)),
+        (flat(tile, kv), (rows, kv)),
+        (flat(tile, kv), (rows, kv)),
+    ]
+    return pl.pallas_call(
+        functools.partial(finish_kernel, slab),
+        grid=(steps,),
+        in_specs=[
+            by_device(own_ff),
+            by_device(own_ff),
+            flat(down_tile, width),
+            by_device(out.shape[2]),
+            by_device(qkv.shape[2]),
+        ],
+        out_specs=[spec for spec, _ in outs],
+        out_shape=[jax.ShapeDtypeStruct(shape, F32) for _, shape in outs],
+        compiler_params=params(),
+        cost_estimate=cost(0, gate, gate, gate, up, up, up, down, down, down),
+        name="finish",
+    )(gate, up, down, out, qkv)
+
+
 def spread_kernel(in_ref, out_ref):
     slab = in_ref.shape[2]
     for c in range(in_ref.shape[0]):
@@ -509,9 +569,9 @@
     length_ref,
     tokens_ref,
     attn_shard,
-    gate_shard,
-    up_shard,
-    down_shard,
+    gate_ref,
+    up_ref,
+    down_ref,
     gain_shard,
     cos_ref,
     sin_ref,
@@ -546,6 +606,7 @@
     own_att,
     att_all,
     own_hid,
+    own_scaled,
     wide,
     narrow,
     z_send,
@@ -553,6 +614,7 @@
     c_send,
     c_recv,
     keep_sem,
+    load_sem,
     wide_sem,
     narrow_sem,
 ):
@@ -579,10 +641,23 @@
     attn_chain = chain(0, w_attn, rows_shard)
     gate_chain = chain(1, w_gate, rows_shard)
     up_chain = chain(2, w_up, rows_shard)
-    down_chain = chain(3, w_down, down_shard.shape[0])
+    slab = w_down.shape[0] // planes
+    down_chain = chain(3, w_down, slab)
     gain_chain = chain(4, gains, gain_shard.shape[0])
-    first = (attn_chain, attn_shard, 0), (gain_chain, gain_shard, 1), (gate_chain, gate_shard, 2), (up_chain, up_shard, 3), (down_chain, down_shard, 4)
-    loads = [pltpu.make_async_copy(shard, c.slot(plane), keep_sem.at[i]) for c, shard, i in first]
+    own_ff = w_gate.shape[1]
+    loads = [
+        pltpu.make_async_copy(shard, c.slot(plane), keep_sem.at[i])
+        for i, (c, shard) in enumerate(((attn_chain, attn_shard), (gain_chain, gain_shard)))
+    ]
+    for ref, c, at in ((gate_ref, gate_chain, 0), (up_ref, up_chain, 1)):
+        for f in range(ref.shape[1] // (n * slab)):
+            src = ref.at[:, pl.ds(pl.multiple_of((f * n + me) * slab, LANES), slab)]
+            dst = c.slot(plane).at[:, pl.ds(f * slab, slab)]
+            loads.append(pltpu.make_async_copy(src, dst, load_sem.at[at, f]))
+        if ref.shape[1] == own_ff:
+            loads.append(pltpu.make_async_copy(ref, c.slot(plane), load_sem.at[at, 0]))
+    down_src = down_ref if down_ref.shape[0] == slab else down_ref.at[pl.ds(pl.multiple_of(me * slab, slab), slab)]
+    loads.append(pltpu.make_async_copy(down_src, down_chain.slot(plane), load_sem.at[2, 0]))
     for load in loads:
         load.start()
     own_x = pltpu.make_async_copy(tokens_ref, x_all.at[pl.ds(me * per_device, per_device)], keep_sem.at[5])
@@ -702,7 +777,9 @@
         acc = jnp.zeros((ROWS, own_width), F32)
         for c in range(n):
             acc += dot_nn(att_all[c, rows, :], w_attn[c * own : (c + 1) * own, columns:])
-        own_hid[rows, :] = (own_hid[rows, :].astype(F32) + RESIDUAL_SCALE * acc).astype(BF16)
+        hidden = own_hid[rows, :].astype(F32) + RESIDUAL_SCALE * acc
+        own_hid[rows, :] = hidden.astype(BF16)
+        own_scaled[rows, :] = (hidden * (1.0 / RESIDUAL_SCALE)).astype(BF16)
         return 0
 
     lax.fori_loop(0, blocks, out_block, 0)
@@ -711,6 +788,7 @@
 
     hid_spread = spread_over(n, own_hid, hid_slot, n, me, c_send.at[2], c_recv.at[2])
     hid_spread.start()
+    keep(own_scaled, mixed_out.at[:, pl.ds(own_ff, own_width)], 13)
     own_h = pltpu.make_async_copy(own_hid, hid_slot(me), keep_sem.at[5])
     own_h.start()
     for step in range(2, planes - 1):
@@ -732,7 +810,7 @@
     def mlp_copies(i, rows, wait):
         slot = lax.rem(i, 2)
         staged(wide, wide_sem, slot, normed2_out, rows, wait)
-        for j, out in enumerate((a_out, b_out, mixed_out)):
+        for j, out in enumerate((a_out, b_out, mixed_out.at[:, pl.ds(0, own_ff)])):
             staged(narrow.at[j], narrow_sem.at[j], slot, out, rows, wait)
 
     def mlp_block(i, _):
@@ -772,20 +850,20 @@
         copy.wait()
 
 
-def forward(n, planes, heads, lengths, tokens, attn_shard, gate_shard, up_shard, down_shard, gain_shard, cos, sin):
+def forward(n, planes, heads, slab, lengths, tokens, attn_shard, gate, up, down, gain_shard, cos, sin):
     per_device, width = tokens.shape
     total = per_device * n
     own = heads * HEAD_SIZE
     columns = own + 2 * HEAD_SIZE
     own_width = attn_shard.shape[1] - columns
-    own_ff = gate_shard.shape[1]
+    own_ff = planes * slab
     rows_shard = attn_shard.shape[0]
     pairs = heads // 2
     weights = [
         ((planes * rows_shard, attn_shard.shape[1]), BF16),
         ((planes * rows_shard, own_ff), BF16),
         ((planes * rows_shard, own_ff), BF16),
-        ((planes * down_shard.shape[0], width), BF16),
+        ((own_ff, width), BF16),
         ((planes * gain_shard.shape[0], gain_shard.shape[1]), F32),
     ]
     outs = [
@@ -800,7 +878,7 @@
         ((total, width), BF16),
         ((total, own_ff), BF16),
         ((total, own_ff), BF16),
-        ((total, own_ff), BF16),
+        ((total, own_ff + own_width), BF16),
     ] + weights
     scratch = weights + [
         ((total, width), BF16),
@@ -811,6 +889,7 @@
         ((pairs, total, LANES), F32),
         ((total, own), BF16),
         ((n, total, own), BF16),
+        ((total, own_width), BF16),
         ((total, own_width), BF16),
         ((2, ROWS, width), BF16),
         ((3, 2, ROWS, own_ff), BF16),
@@ -825,7 +904,7 @@
         out_specs=[anywhere] * len(outs),
         out_shape=[jax.ShapeDtypeStruct(*o) for o in outs],
         scratch_shapes=[pltpu.VMEM(*s) for s in scratch]
-        + [dma((5, 2, steps)), dma((5, 2, steps)), dma((3, n)), dma((3, n)), dma((16,)), dma((2,)), dma((3, 2))],
+        + [dma((5, 2, steps)), dma((5, 2, steps)), dma((3, n)), dma((3, n)), dma((16,)), dma((3, planes)), dma((2,)), dma((3, 2))],
         compiler_params=pltpu.CompilerParams(
             vmem_limit_bytes=VMEM_LIMIT, collective_id=1, has_side_effects=True
         ),
@@ -835,7 +914,7 @@
             transcendentals=0,
         ),
         name="forward",
-    )(lengths, tokens, attn_shard, gate_shard, up_shard, down_shard, gain_shard, cos, sin)
+    )(lengths, tokens, attn_shard, gate, up, down, gain_shard, cos, sin)
 
 
 def add_into(dst, src):
@@ -1586,10 +1665,11 @@
     position = given - jnp.where(given >= first_len, first_len, 0)
     freq_index = jnp.arange(HEAD_SIZE // 2, dtype=F32)
     inverse = ROPE_BASE ** (-2.0 * freq_index / HEAD_SIZE)
-    angles = position.astype(F32)[:, None] * inverse[None, :]
-    cos, sin = jnp.cos(angles), jnp.sin(angles)
-    cos_table = jnp.concatenate([cos, cos, cos, cos], axis=1)
-    sin_table = jnp.concatenate([-sin, sin, -sin, sin], axis=1)
+    turns = jnp.tile(inverse, 4)
+    sign = jnp.tile(jnp.repeat(jnp.array([-1.0, 1.0], F32), HEAD_SIZE // 2), 2)
+    angles = position.astype(F32)[:, None] * turns[None, :]
+    cos_table = jnp.cos(angles)
+    sin_table = jnp.sin(angles) * sign[None, :]
 
     deal_rows = deal[0]
     slot_ids = jnp.arange(n_ctx, dtype=jnp.int32)
@@ -1602,29 +1682,34 @@
         blocks = array.reshape(n_ctx * n_ctx, block_rows, array.shape[1])
         return jnp.take(blocks, table, axis=0, mode="clip").reshape(array.shape)
 
+    ff_weights = gate_weight, up_weight, down_weight
+    if slab % LANES:
+        ff_weights = (
+            ff_columns(gate_weight),
+            ff_columns(up_weight),
+            lax.dynamic_slice_in_dim(down_weight, me * slab, slab, axis=0),
+        )
+
     cotangent_all = lax.all_gather(cotangent[0], "ctx", axis=0, tiled=True)
     (
-        x, normed, q_rot, k_rot, v_rows, lse, attended_all, hidden_all, normed2, a, b, mixed, w_attn, w_gate, w_up, w_down, gains_all,
+        x, normed, q_rot, k_rot, v_rows, lse, attended_all, hidden_all, normed2, a, b, both, w_attn, w_gate, w_up, w_down, gains_all,
     ) = forward(
         n_ctx,
         n_fsdp,
         heads,
+        slab,
         lengths[0],
         tokens[0],
         attn_shard,
-        ff_columns(gate_weight),
-        ff_columns(up_weight),
-        lax.dynamic_slice_in_dim(down_weight, me * slab, slab, axis=0),
+        *ff_weights,
         gain_shard,
         cos_table,
         sin_table,
     )
     w_qkv, w_out = w_attn[:, : split + 2 * HEAD_SIZE], w_attn[:, split + 2 * HEAD_SIZE :]
     gains = gains_all.reshape(n_fsdp, 8, 2, rows_shard)[:, 0].transpose(1, 0, 2).reshape(2, 1, width)
-    hidden_own = own_columns(hidden_all, me, own_width)
     grad_result = reorder(cotangent_all, dealt_of_given)
 
-    both = jnp.concatenate([mixed, (hidden_own.astype(F32) * (1.0 / RESIDUAL_SCALE)).astype(BF16)], axis=1)
     column = lax.broadcasted_iota(jnp.int32, (own_width, width), 1) - me * own_width
     place = (column == lax.broadcasted_iota(jnp.int32, (own_width, width), 0)).astype(BF16)
     result_part = RESIDUAL_SCALE * dot_nn(reorder(both, given_of_dealt), jnp.concatenate([w_down, place], axis=0))
@@ -1639,7 +1724,7 @@
             heads,
             lengths[0],
             grad_result,
-            (x, normed, q_rot, k_rot, v_rows, lse, attended_all, hidden_all, normed2, a, b, mixed),
+            (x, normed, q_rot, k_rot, v_rows, lse, attended_all, hidden_all, normed2, a, b, both),
             (w_attn, w_gate, w_up, w_down, gains_all),
             cos_table,
             sin_table,
@@ -1652,7 +1737,7 @@
         def settle(left, right):
             return lax.psum_scatter(dot_tn(left, right).astype(BF16), "fsdp", scatter_dimension=0, tiled=True)
 
-        down_part = settle(mixed, mlp_grad)
+        down_part = settle(both[:, :own_ff], mlp_grad)
         ggrad, ugrad, hidden_part, mlp_gain_part = mlp_backward(
             n_ctx, mlp_grad, a, b, hidden_all, gains[1], w_gate, w_up, w_down
         )
@@ -1687,28 +1772,33 @@
             lax.all_gather(p, "ctx", axis=0, tiled=False) for p in (down_part, gate_part, up_part, out_part, qkv_part)
         ]
 
-    down_grad = down_part.reshape(n_ctx * slab, width).astype(F32)
-    if slab % LANES == 0:
-        gate_grad = spread_columns(gate_part, slab, n_fsdp)
-        up_grad = spread_columns(up_part, slab, n_fsdp)
+    if slab % LANES == 0 and sharing == 1 and heads % 4 == 0:
+        gate_grad, up_grad, down_grad, out_grad, query_grad, key_grad, value_grad = finish(
+            slab, gate_part, up_part, down_part.reshape(n_ctx * slab, width), out_part, qkv_part
+        )
     else:
-
-        def ff_whole(part):
-            pieces = part.reshape(n_ctx, rows_shard, n_fsdp, slab)
-            return pieces.transpose(1, 2, 0, 3).reshape(rows_shard, ff).astype(F32)
-
-        gate_grad = ff_whole(gate_part)
-        up_grad = ff_whole(up_part)
-    out_grad = spread_columns(out_part, own_width, 1)
-    qkv_all = qkv_part
-    query_grad = spread_columns(qkv_all, split, 1)
-
-    def shared_heads(pieces):
-        pieces = pieces.astype(F32).reshape(KEY_VALUE_HEADS, sharing, rows_shard, HEAD_SIZE).sum(axis=1)
-        return pieces.transpose(1, 0, 2).reshape(rows_shard, KEY_VALUE_HEADS * HEAD_SIZE)
-
-    key_grad = shared_heads(qkv_all[:, :, split : split + HEAD_SIZE])
-    value_grad = shared_heads(qkv_all[:, :, split + HEAD_SIZE :])
+        down_grad = down_part.reshape(n_ctx * slab, width).astype(F32)
+        if slab % LANES == 0:
+            gate_grad = spread_columns(gate_part, slab, n_fsdp)
+            up_grad = spread_columns(up_part, slab, n_fsdp)
+        else:
+
+            def ff_whole(part):
+                pieces = part.reshape(n_ctx, rows_shard, n_fsdp, slab)
+                return pieces.transpose(1, 2, 0, 3).reshape(rows_shard, ff).astype(F32)
+
+            gate_grad = ff_whole(gate_part)
+            up_grad = ff_whole(up_part)
+        out_grad = spread_columns(out_part, own_width, 1)
+        qkv_all = qkv_part
+        query_grad = spread_columns(qkv_all, split, 1)
+
+        def shared_heads(pieces):
+            pieces = pieces.astype(F32).reshape(KEY_VALUE_HEADS, sharing, rows_shard, HEAD_SIZE).sum(axis=1)
+            return pieces.transpose(1, 0, 2).reshape(rows_shard, KEY_VALUE_HEADS * HEAD_SIZE)
+
+        key_grad = shared_heads(qkv_all[:, :, split : split + HEAD_SIZE])
+        value_grad = shared_heads(qkv_all[:, :, split + HEAD_SIZE :])
 
     return (
         activations,

time: 726 us -> 697 us (0.960)
  other arithmetic: 29.9 us -> 7.74 us
  local copies, waits for them, and re-layouts: 26.9 us -> 18.5 us
    convert_element_type x3 -> x1, other arithmetic: 13.7 us -> 0.65 us  [local(): angles = position.astype(F32)[:, None] * turns[None, :]]
    concatenate x4 -> x0, other arithmetic: 8.8 us -> none  [the longest x1 4.15 us: local(): jnp.concatenate([mixed, (hidden_own.astype(F32) * (1.0 / RESIDUAL_SCALE))...]
    pallas_call x4 -> x1, Pallas kernels: 35.9 us -> 32.3 us  [finish(): pl.pallas_call(functools.partial(finish_kernel, slab), grid=(steps,), in_...]
  transfers between devices with their start and end apart: 2 -> 2, of which waited for: 0 -> 0; matrix products, arithmetic and copies ran while one was open for 9% -> 5% of each run, Pallas kernels for 88% -> 92%
where the time goes in v6:
time: 697 us; the launch traced here: 685 us
  Pallas kernels  631 us (91%)
  local copies, waits for them, and re-layouts  18.5 us (3%)
  between operations  14.4 us (2%)
  matrix products  13 us (2%)
  other arithmetic  7.74 us (1%)
    pallas_call x1, Pallas kernels, backward(): pl.pallas_call(functools.partial(backward_kernel, n, planes, heads), in_s...  348 us
    pallas_call x1, Pallas kernels, forward(): pl.pallas_call(functools.partial(forward_kernel, n, planes, heads), in_sp...  250 us
    pallas_call x1, Pallas kernels, finish(): pl.pallas_call(functools.partial(finish_kernel, slab), grid=(steps,), in_...  32.3 us
  transfers between devices with their start and end apart: 2, of which 0 were waited for; matrix products, arithmetic and copies ran while one was open for 5% of the time, Pallas kernels for 92%

profile of v6, /device:TPU:9, one launch (start us, length us, event | category | flops | bytes accessed | tf_op | source)
XLA Modules:
  0.0 685.3 jit_solution(4221871979583955390)
XLA Ops:
  7.2 0.7 all-gather.3.cloned.1.call-update
  8.0 0.1 mul.70
  8.1 0.7 broadcast_in_dim.39
  8.8 0.1 tile.10
  8.9 0.1 mul.73
  9.0 0.8 select_reduce_fusion
  9.9 0.1 reshape.111
  10.0 0.7 maximum_convert_fusion
  10.7 0.7 subtract_convert_fusion
  11.3 1.1 constant_dynamic-slice_fusion.1
  12.5 1.1 constant_dynamic-slice_fusion
  13.6 1.0 pad_maximum_fusion.attn_shard
  14.6 4.3 fusion.4
  18.8 0.6 tile.8.gain_shard
  19.5 250.1 %forward.1 = (bf16[1536,2048]{1,0:T(8,128)(2,1)}, bf16[1536,2048]{1,0:T(8,128)(2,1)}, bf16[1536,256]{1,0:T(8,128)(2,1)}, bf16[1536,128]{1,0:T(8,128)(2,1)}, bf16...) custom-call(s32[2]{0:T(128)} %bitcast.29, ...), custom_call_target="tpu_custom_call" | custom-call | flops 16911433728 | bytes 62914560 | tf_op jit(solution)/shard_map/forward/pallas_call | solution.py:901
  269.6 4.8 gather_fusion
  274.4 0.2 fusion.3
  274.6 13.0 %multiply_convert_fusion = bf16[1536,2048]{1,0:T(8,128)(2,1)} fusion(bf16[1536,1280]{1,0:T(8,128)(2,1)} %bitcast.23, bf16[256,2048]{1,0:T(8,128)(2,1)S(1)} %fusion.3, bf16[1024,2048]{1,0:T(8,128)(2,1)} %get-tuple-element.43.down_in), kind=kOutput, calls=%fused_computation.2 | convolution fusion | flops 8069840896 | bytes 15466496 | tf_op jit(solution)/shard_map/dot_general | solution.py:26
  287.8 0.6 copy-done.1
  288.5 6.4 gather_fusion.1
  294.9 348.4 %backward.1 = (f32[192,2048]{1,0:T(8,128)}, f32[8,512]{1,0:T(8,128)}, bf16[8,256,2048]{2,1,0:T(8,128)(2,1)}, bf16[8,512,1024]{2,1,0:T(8,128)(2,1)}, bf16[8,512,1...) custom-call(s32[2]{0:T(128)} %bitcast.30, ...), custom_call_target="tpu_custom_call" | custom-call | flops 51539607552 | bytes 104857600 | tf_op jit(solution)/shard_map/backward/pallas_call | solution.py:1554
  643.4 32.3 %finish.1 = (f32[512,8192]{1,0:T(8,128)}, f32[512,8192]{1,0:T(8,128)}, f32[2048,2048]{1,0:T(8,128)}, f32[512,2048]{1,0:T(8,128)}, f32[512,2048]{1,0:T(8,128)}, /*index=5*/f32[512,512]{1,0:T(8,128)}, f32[512,512]{1,0:T(8,128)}) custom-call(bf16[8,512,1024]{2,1,0:T(8,128)(2,1)} %get-tuple-element.61.gate_ref, bf16[8,512,1024]{2,1,0:T(8,128)(2,1)} %get-tuple-element.62.up_ref, ...), custom_call_target="tpu_custom_call" | custom-call | bytes 75497472 | tf_op jit(solution)/shard_map/finish/pallas_call | solution.py:317
  675.7 1.4 fusion.6
  677.1 1.1 copy.27
  (22 shorter events, 0.5 us)
Async XLA Ops:
  7.2 281.3 %all-gather.3.cloned.1.call-start = ((), (), s32[]{:S(2)}) async-start(), calls=%async_computation.2 | async-start | bytes 7077888 | tf_op jit(solution)/shard_map/all_gather | solution.py:1693
  7.9 669.1 %reduce-scatter.2.cloned.1.call-start = ((), (), s32[]{:S(2)}) async-start(), calls=%async_computation.1 | async-start | bytes 7077888 | tf_op jit(solution)/shard_map/reduce_scatter | solution.py:1716
  287.6 0.7 copy-start.1
  643.4 33.7 %copy-start = (f32[192,2048]{1,0:T(8,128)S(1)}, f32[192,2048]{1,0:T(8,128)}, u32[]{:S(2)}) copy-start(f32[192,2048]{1,0:T(8,128)} %get-tuple-element.59) | copy-start | bytes 4718596
Sparse Core Ops, SparseCore 0:
  9.9 62.7 all-gather.2
  287.8 68.3 reduce-scatter.1

commit v7 on v6

--- a/solution.py
+++ b/solution.py
@@ -918,8 +918,8 @@
 
 
 def add_into(dst, src):
-    rows_in = dst.shape[0]
-    chunk = 64 if rows_in % 64 == 0 else 32
+    rows_in, columns = dst.shape
+    chunk = max(c for c in (256, 128, 64, 32) if c == 32 or (rows_in % c == 0 and c * columns <= 65536))
 
     def step(i, _):
         rows = pl.ds(pl.multiple_of(i * chunk, chunk), chunk)
@@ -1007,7 +1007,7 @@
         self.core = lax.rem(me, 2)
         self.chip = me // 2
         self.chips = (self.chip, *square(self.chip))
-        self.half = stage.shape[0] // 2
+        self.half = stage[0].shape[0] // 2
 
     def rows(self, which):
         return pl.ds(which * self.half, self.half)
@@ -1038,37 +1038,53 @@
         for k in (3, 1, 2, 0):
             self.first(k).start()
 
-    def add(self, k):
-        self.first(k).wait_recv()
-        fetch(self.landed.at[k], self.stage, self.load_sem)
-        add_into(self.own(k), self.stage)
+    def add_all(self, items):
+        pending = None
+
+        def complete(copy, dst, stage, then):
+            copy.wait()
+            add_into(dst, stage)
+            for remote in then:
+                remote.start()
+
+        for index, (arrivals, src, dst, then) in enumerate(items):
+            for remote in arrivals:
+                remote.wait_recv()
+            stage = self.stage[index % 2].at[pl.ds(0, dst.shape[0])]
+            copy = pltpu.make_async_copy(src, stage, self.load_sem.at[index % 2])
+            copy.start()
+            if pending is not None:
+                complete(*pending)
+            pending = (copy, dst, stage, then)
+        complete(*pending)
 
     def pass_on(self):
-        self.add(3)
-        self.second(3, 1, 0).start()
-        self.second(3, 2, 1).start()
-        self.add(1)
-        self.second(1, 1, 0).start()
-        self.add(2)
-        self.second(2, 2, 1).start()
+        self.add_all(
+            [
+                ([self.first(3)], self.landed.at[3], self.own(3), [self.second(3, 1, 0), self.second(3, 2, 1)]),
+                ([self.first(1)], self.landed.at[1], self.own(1), [self.second(1, 1, 0)]),
+                ([self.first(2)], self.landed.at[2], self.own(2), [self.second(2, 2, 1)]),
+            ]
+        )
 
     def late(self):
-        for to, which, k in ((1, 0, 2), (2, 1, 1)):
-            self.second(3, to, which).wait_recv()
-            place = self.stage.at[self.rows(which)]
-            fetch(self.far.at[2, self.rows(which)], place, self.load_sem)
-            add_into(self.own(k).at[self.rows(which)], place)
-            self.second(k, k, which).start()
+        self.add_all(
+            [
+                (
+                    [self.second(3, to, which)],
+                    self.far.at[2, self.rows(which)],
+                    self.own(k).at[self.rows(which)],
+                    [self.second(k, k, which)],
+                )
+                for to, which, k in ((1, 0, 2), (2, 1, 1))
+            ]
+        )
 
     def finish(self, total):
-        self.first(0).wait_recv()
-        fetch(self.landed.at[0], self.stage, self.load_sem)
-        add_into(total, self.stage)
+        items = [([self.first(0)], self.landed.at[0], total, [])]
         for k in (1, 2):
-            for which in (0, 1):
-                self.second(k, k, which).wait_recv()
-            fetch(self.far.at[k - 1], self.stage, self.load_sem)
-            add_into(total, self.stage)
+            items.append(([self.second(k, k, which) for which in (0, 1)], self.far.at[k - 1], total, []))
+        self.add_all(items)
 
     def drain(self):
         for k in range(4):
@@ -1153,6 +1169,7 @@
     load_sem,
     hid_sem,
     add_sem,
+    ring_sem,
 ):
     me, plane = lax.axis_index("ctx"), lax.axis_index("fsdp")
     total, width = grad.shape
@@ -1219,7 +1236,19 @@
         return out
 
     def scatter(index, block, near, far, stage):
-        return Scatter(block, near, far, stage, me, s_send.at[index], s_recv.at[index], add_sem)
+        return Scatter(block, near, far, stage, me, s_send.at[index], s_recv.at[index], ring_sem)
+
+    part_rows = total // 2
+    col_stages = [stage_col.at[pl.ds(i * part_rows, part_rows)] for i in range(2)]
+
+    def half_scatter(index, near, far, side):
+        rows = pl.ds(side * part_rows, part_rows)
+        return scatter(
+            2 * index + side, lambda c: part.at[c, rows], near.at[:, rows], far.at[:, rows], col_stages
+        )
+
+    first = [half_scatter(0, near1, far1, side) for side in range(2)]
+    second = [half_scatter(1, near2, far2, side) for side in range(2)]
 
     grad_load.wait()
 
@@ -1268,10 +1297,6 @@
         b_v[rows, :] = ugrad
         normed_grad = dot_nt(ggrad, w_gate[...]) + dot_nt(ugrad, w_up[...])
         stream(hidden_in, i, True)
-
-        @pl.when(i == blocks - 2)
-        def _():
-            down_sum.advance(1)
 
         hidden = hid_stage[lax.rem(i, 2)].astype(F32)
         r2 = lax.rsqrt(jnp.mean(hidden * hidden, axis=-1, keepdims=True) + EPSILON)
@@ -1281,27 +1306,38 @@
         piece = r2 * weighted - hidden * (r2 * r2 * r2 * mean)
         for c in range(n):
             part[c, rows, :] = piece[:, c * own_width : (c + 1) * own_width].astype(BF16)
+
+        @pl.when(i == blocks // 2 - 1)
+        def _():
+            first[0].start()
+
+        @pl.when(i == blocks - 2)
+        def _():
+            down_sum.advance(1)
+            first[0].pass_on()
+
         return 0
 
     lax.fori_loop(0, blocks, mlp_block, 0)
-    first = scatter(0, lambda c: part.at[c], near1, far1, stage_col)
-    first.start()
+    first[1].start()
     normed2_load = load(normed2_in, grad, 8)
     normed2_load.wait()
 
-    def columns_times(right, out):
+    def columns_times(right, out, low, high):
         def block(j, _):
             lanes = pl.ds(pl.multiple_of(j * ROWS, ROWS), ROWS)
             out[lanes, :] = dot_tn(grad[:, lanes], right[...]).astype(BF16)
             return 0
 
-        lax.fori_loop(0, width // ROWS, block, 0)
-
-    columns_times(a_v, w_gate)
+        lax.fori_loop(low, high, block, 0)
+
+    first[0].late()
+    columns_times(a_v, w_gate, 0, width // ROWS)
     gate_sum.start()
-    first.pass_on()
-    columns_times(b_v, w_up)
-    first.late()
+    first[1].pass_on()
+    columns_times(b_v, w_up, 0, width // ROWS // 2)
+    first[1].late()
+    columns_times(b_v, w_up, width // ROWS // 2, width // ROWS)
     down_sum.advance(2)
 
     att_loads = [load(att_in.at[c], grad.at[:, pl.ds(c * own, own)], c) for c in range(n)]
@@ -1320,8 +1356,9 @@
         return 0
 
     lax.fori_loop(0, blocks, begin, 0)
-    first.finish(hidden_grad)
-    first.drain()
+    for side in range(2):
+        first[side].finish(hidden_grad.at[pl.ds(side * part_rows, part_rows)])
+        first[side].drain()
 
     def branch_block(i, _):
         rows = pl.ds(pl.multiple_of(i * ROWS, ROWS), ROWS)
@@ -1329,11 +1366,16 @@
         b_v[rows, LANES : LANES + own_width] = branch
         for c in range(n):
             part[c, rows, :] = dot_nt(branch, w_attn[c * own : (c + 1) * own, columns:]).astype(BF16)
+
+        @pl.when(i == blocks // 2 - 1)
+        def _():
+            second[0].start()
+
         return 0
 
     lax.fori_loop(0, blocks, branch_block, 0)
-    second = scatter(1, lambda c: part.at[c], near2, far2, stage_col)
-    second.start()
+    second[1].start()
+    second[0].pass_on()
     gate_sum.advance(1)
     for copy in att_loads:
         copy.wait()
@@ -1341,12 +1383,13 @@
     for c in range(n):
         place = out_block_of(c // heads_per_shard).at[pl.ds((c % heads_per_shard) * own, own)]
         place[...] = dot_tn(grad[:, c * own : (c + 1) * own], b_v[:, LANES : LANES + own_width]).astype(BF16)
-    second.pass_on()
+    second[1].pass_on()
+    second[0].late()
     normed_load = load(normed_in, grad, 15)
     down_sum.take(last)
     up_sum.start()
-    second.late()
-    second.finish(part.at[me])
+    second[1].late()
+    second[0].finish(part.at[me, pl.ds(0, part_rows)])
     down_give = give(0, down_sum, down_all)
     gate_sum.advance(2)
 
@@ -1357,10 +1400,10 @@
     first_len = length_ref[0]
     dq_at = own + 2 * LANES
 
-    def attend_pair(pair, _):
+    def attend_pair(side, pair, _):
         lanes = pl.ds(pl.multiple_of(pair * LANES, LANES), LANES)
         dq_lanes = pl.ds(pl.multiple_of(dq_at + pair * LANES, LANES), LANES)
-        for block in range(blocks):
+        for block in range(side * (blocks // 2), (side + 1) * (blocks // 2)):
             rows = pl.ds(block * ROWS, ROWS)
             end = (block + 1) * ROWS
             bias = mask_bias(first_len, block * ROWS, ROWS, end)
@@ -1368,12 +1411,12 @@
             low = low_half(query.shape)
             keys, values = a_v[:end, own : own + LANES], a_v[:end, own + LANES : own + 2 * LANES]
             parts = []
-            for side in range(2):
-                chosen = low if side == 0 else jnp.logical_not(low)
+            for head in range(2):
+                chosen = low if head == 0 else jnp.logical_not(low)
                 own_query = jnp.where(chosen, query, jnp.zeros_like(query))
                 own_grads = jnp.where(chosen, grads, jnp.zeros_like(grads))
                 scores = dot_nt(own_query, keys) + bias
-                probs = jnp.exp(scores - lse[pair, rows, side : side + 1])
+                probs = jnp.exp(scores - lse[pair, rows, head : head + 1])
                 prob_grad = dot_nt(own_grads, values)
                 delta = jnp.sum(probs * prob_grad, axis=-1, keepdims=True)
                 score_grad = (probs * (prob_grad - delta)).astype(BF16)
@@ -1383,14 +1426,18 @@
             dq = jnp.where(low_half(parts[0].shape), parts[0], parts[1]) * SCORE_SCALE
             a_v[rows, dq_lanes] = (dq * cos[rows, :] - swap_halves(dq) * sin[rows, :]).astype(BF16)
 
-        @pl.when(pair == 0)
-        def _():
-            down_give.pass_on()
-            up_sum.advance(1)
+        if side:
+
+            @pl.when(pair == 0)
+            def _():
+                down_give.pass_on()
+                up_sum.advance(1)
 
         return 0
 
-    lax.fori_loop(0, pairs, attend_pair, 0)
+    lax.fori_loop(0, pairs, functools.partial(attend_pair, 0), 0)
+    second[1].finish(part.at[me, pl.ds(part_rows, part_rows)])
+    lax.fori_loop(0, pairs, functools.partial(attend_pair, 1), 0)
     dk = dk_sum[...]
     dk = dk + pltpu.roll(dk, HEAD_SIZE, 1)
     dk = dk * cos[...] - swap_halves(dk) * sin[...]
@@ -1443,7 +1490,7 @@
     def token_rows(c):
         return grad.at[pl.ds(pl.multiple_of(c * per_device, per_device), per_device)]
 
-    third = scatter(2, token_rows, near3, far3, stage_wide.at[pl.ds(0, per_device)])
+    third = scatter(4, token_rows, near3, far3, [hid_stage.at[i, pl.ds(0, per_device)] for i in range(2)])
     third.start()
     gain_give = spread(5, gain_own, gain_all)
     gain_mine = load(gain_own, gain_all.at[me], 21)
@@ -1482,7 +1529,7 @@
         out.finish()
         out.drain()
         mine.wait()
-    for s in (second, third):
+    for s in (*second, third):
         s.drain()
     for s in (down_sum, gate_sum, up_sum, out_sum, qkv_sum, gain_sum):
         s.drain()
@@ -1560,13 +1607,14 @@
         + [
             dma((6, 2, steps)),
             dma((6, 2, steps)),
-            dma((3, 10)),
-            dma((3, 10)),
+            dma((5, 10)),
+            dma((5, 10)),
             dma((6, n)),
             dma((6, n)),
             dma((24,)),
             dma((2,)),
             dma,
+            dma((2,)),
         ],
         compiler_params=pltpu.CompilerParams(
             vmem_limit_bytes=60 * 1024 * 1024, collective_id=2, has_side_effects=True
@@ -1602,7 +1650,7 @@
 
 def kernel_fits(n, planes, total, width, own_ff):
     held = 4 * width * own_ff + 2 * total * width + 2 * total * own_ff
-    return planes == 4 and n == 8 and own_ff // planes >= total // n and n * own_ff >= 4 * width and 2 * held < 44 * 1024 * 1024 and (own_ff // planes) % LANES == 0
+    return planes == 4 and total % (2 * ROWS) == 0 and n == 8 and own_ff // planes >= total // n and n * own_ff >= 4 * width and 2 * held < 44 * 1024 * 1024 and (own_ff // planes) % LANES == 0
 
 
 def own_columns(array, index, width):

time: 697 us -> 694 us (level)
  no operation moved by 1% of the time
where the time goes in v7:
time: 694 us; the launch traced here: 682 us
  Pallas kernels  628 us (90%)
  local copies, waits for them, and re-layouts  18.5 us (3%)
  between operations  14.3 us (2%)
  matrix products  13 us (2%)
  other arithmetic  7.74 us (1%)
    pallas_call x1, Pallas kernels, backward(): pl.pallas_call(functools.partial(backward_kernel, n, planes, heads), in_s...  345 us
    pallas_call x1, Pallas kernels, forward(): pl.pallas_call(functools.partial(forward_kernel, n, planes, heads), in_sp...  250 us
    pallas_call x1, Pallas kernels, finish(): pl.pallas_call(functools.partial(finish_kernel, slab), grid=(steps,), in_...  32.3 us
  transfers between devices with their start and end apart: 2, of which 0 were waited for; matrix products, arithmetic and copies ran while one was open for 5% of the time, Pallas kernels for 92%

profile of v7, /device:TPU:9, one launch (start us, length us, event | category | flops | bytes accessed | tf_op | source)
XLA Modules:
  0.0 682.1 jit_solution(12029200318131662323)
XLA Ops:
  7.2 0.7 all-gather.3.cloned.1.call-update
  8.0 0.1 mul.70
  8.1 0.7 broadcast_in_dim.39
  8.8 0.1 tile.10
  8.9 0.1 mul.73
  9.0 0.8 select_reduce_fusion
  9.9 0.1 reshape.111
  10.0 0.7 maximum_convert_fusion
  10.7 0.7 subtract_convert_fusion
  11.3 1.1 constant_dynamic-slice_fusion.1
  12.5 1.1 constant_dynamic-slice_fusion
  13.6 1.0 pad_maximum_fusion.attn_shard
  14.6 4.3 fusion.4
  18.8 0.6 tile.8.gain_shard
  19.5 250.1 %forward.1 = (bf16[1536,2048]{1,0:T(8,128)(2,1)}, bf16[1536,2048]{1,0:T(8,128)(2,1)}, bf16[1536,256]{1,0:T(8,128)(2,1)}, bf16[1536,128]{1,0:T(8,128)(2,1)}, bf16...) custom-call(s32[2]{0:T(128)} %bitcast.29, ...), custom_call_target="tpu_custom_call" | custom-call | flops 16911433728 | bytes 62914560 | tf_op jit(solution)/shard_map/forward/pallas_call | solution.py:901
  269.6 4.8 gather_fusion
  274.4 0.2 fusion.3
  274.6 13.0 %multiply_convert_fusion = bf16[1536,2048]{1,0:T(8,128)(2,1)} fusion(bf16[1536,1280]{1,0:T(8,128)(2,1)} %bitcast.23, bf16[256,2048]{1,0:T(8,128)(2,1)S(1)} %fusion.3, bf16[1024,2048]{1,0:T(8,128)(2,1)} %get-tuple-element.43.down_in), kind=kOutput, calls=%fused_computation.2 | convolution fusion | flops 8069840896 | bytes 15466496 | tf_op jit(solution)/shard_map/dot_general | solution.py:26
  287.8 0.6 copy-done.1
  288.5 6.4 gather_fusion.1
  294.9 345.3 %backward.1 = (f32[192,2048]{1,0:T(8,128)}, f32[8,512]{1,0:T(8,128)}, bf16[8,256,2048]{2,1,0:T(8,128)(2,1)}, bf16[8,512,1024]{2,1,0:T(8,128)(2,1)}, bf16[8,512,1...) custom-call(s32[2]{0:T(128)} %bitcast.30, ...), custom_call_target="tpu_custom_call" | custom-call | flops 51539607552 | bytes 104857600 | tf_op jit(solution)/shard_map/backward/pallas_call | solution.py:1601
  640.2 32.3 %finish.1 = (f32[512,8192]{1,0:T(8,128)}, f32[512,8192]{1,0:T(8,128)}, f32[2048,2048]{1,0:T(8,128)}, f32[512,2048]{1,0:T(8,128)}, f32[512,2048]{1,0:T(8,128)}, /*index=5*/f32[512,512]{1,0:T(8,128)}, f32[512,512]{1,0:T(8,128)}) custom-call(bf16[8,512,1024]{2,1,0:T(8,128)(2,1)} %get-tuple-element.61.gate_ref, bf16[8,512,1024]{2,1,0:T(8,128)(2,1)} %get-tuple-element.62.up_ref, ...), custom_call_target="tpu_custom_call" | custom-call | bytes 75497472 | tf_op jit(solution)/shard_map/finish/pallas_call | solution.py:317
  672.5 1.4 fusion.6
  673.9 1.1 copy.27
  (22 shorter events, 0.5 us)
Async XLA Ops:
  7.2 281.3 %all-gather.3.cloned.1.call-start = ((), (), s32[]{:S(2)}) async-start(), calls=%async_computation.2 | async-start | bytes 7077888 | tf_op jit(solution)/shard_map/all_gather | solution.py:1741
  7.9 666.0 %reduce-scatter.2.cloned.1.call-start = ((), (), s32[]{:S(2)}) async-start(), calls=%async_computation.1 | async-start | bytes 7077888 | tf_op jit(solution)/shard_map/reduce_scatter | solution.py:1764
  287.6 0.7 copy-start.1
  640.2 33.7 %copy-start = (f32[192,2048]{1,0:T(8,128)S(1)}, f32[192,2048]{1,0:T(8,128)}, u32[]{:S(2)}) copy-start(f32[192,2048]{1,0:T(8,128)} %get-tuple-element.59) | copy-start | bytes 4718596
Sparse Core Ops, SparseCore 0:
  9.9 62.7 all-gather.2
  287.8 73.6 reduce-scatter.1

commit v8 on v7

--- a/solution.py
+++ b/solution.py
@@ -270,6 +270,33 @@
         cost_estimate=cost(2 * total * width * w_qkv.shape[1], x, x, w_qkv, dq, dkv, hidden_grad),
         name="token_backward",
     )(me, dq, dkv, w_qkv, x, gain, hidden_grad)
+
+
+def result_kernel(me_ref, rows_ref, w_ref, out_ref):
+    depth = w_ref.shape[0]
+    own = rows_ref.shape[1] - depth
+    product = dot_nn(rows_ref[:, :depth], w_ref[...])
+    hidden = rows_ref[:, depth:].astype(F32)
+    for c in range(out_ref.shape[1] // own):
+        lanes = slice(c * own, (c + 1) * own)
+        mine = jnp.where(me_ref[0] == c, hidden, 0.0)
+        out_ref[:, lanes] = (RESIDUAL_SCALE * (product[:, lanes] + mine)).astype(BF16)
+
+
+def result_rows(me, rows, w_down):
+    total, columns = rows.shape
+    depth, width = w_down.shape
+    out_shape = jax.ShapeDtypeStruct((total, width), BF16)
+    return pl.pallas_call(
+        result_kernel,
+        grid=(total // ROWS,),
+        in_specs=[pl.BlockSpec(memory_space=pltpu.SMEM), row_block(columns), fixed(depth, width)],
+        out_specs=row_block(width),
+        out_shape=out_shape,
+        compiler_params=params(),
+        cost_estimate=cost(2 * total * depth * width, rows, w_down, out_shape),
+        name="result_rows",
+    )(me, rows, w_down)
 
 
 def finish_kernel(slab, gate_ref, up_ref, down_ref, out_ref, qkv_ref, gate_out, up_out, down_out, out_out, q_out, k_out, v_out):
@@ -1252,21 +1279,21 @@
 
     grad_load.wait()
 
-    def scale_block(i, _):
-        rows = pl.ds(pl.multiple_of(i * ROWS, ROWS), ROWS)
-        grad[rows, :] = (RESIDUAL_SCALE * grad[rows, :].astype(F32)).astype(BF16)
-        return 0
-
-    lax.fori_loop(0, blocks, scale_block, 0)
     for copy in mixed_loads:
         copy.wait()
 
-    def down_block(d, _):
-        p_down[pl.ds(pl.multiple_of(d * own_width, own_width), own_width), :] = dot_tn(part[d], grad[...]).astype(BF16)
+    def down_block(i, _):
+        d = jnp.where(i == 0, planes - 1, jnp.where(i == 1, 0, planes - i))
+        rows = pl.ds(pl.multiple_of(d * own_width, own_width), own_width)
+        p_down[rows, :] = (RESIDUAL_SCALE * dot_tn(part[d], grad[...])).astype(BF16)
+
+        @pl.when(i == 1)
+        def _():
+            down_sum.start()
+
         return 0
 
-    lax.fori_loop(0, own_ff // own_width, down_block, 0)
-    down_sum.start()
+    lax.fori_loop(0, planes, down_block, 0)
 
     for copy in (down_load, gate_load, up_load, a_load, b_load, attn_load, gain_load):
         copy.wait()
@@ -1290,7 +1317,7 @@
         def _():
             stream(hidden_in, i + 1, False)
 
-        mixed_grad = dot_nt(grad[rows, :], w_down[...])
+        mixed_grad = RESIDUAL_SCALE * dot_nt(grad[rows, :], w_down[...])
         ggrad = (mixed_grad * a_v[rows, :].astype(F32)).astype(BF16)
         ugrad = (mixed_grad * b_v[rows, :].astype(F32)).astype(BF16)
         a_v[rows, :] = ggrad
@@ -1497,32 +1524,32 @@
     gain_give.start()
     gate_give.late()
     third.pass_on()
+    gain_give.pass_on()
     out_sum.advance(2)
-    gain_give.pass_on()
-    up_sum.take(last)
-    up_give = give(2, up_sum, up_all)
     third.late()
-    qkv_sum.advance(1)
     gain_give.finish()
     gain_mine.wait()
     gain_give.drain()
     gain_own[...] = sum(gain_all[c] for c in range(n))
     gain_sum.start()
     token_out[...] = token_rows(me)[...].astype(F32)
+    qkv_sum.advance(1)
     third.finish(token_out)
+    up_sum.take(last)
+    up_give = give(2, up_sum, up_all)
+    gain_sum.advance(1)
     out_sum.take(last)
     out_give = give(3, out_sum, out_all)
+    qkv_sum.advance(2)
+    gain_sum.advance(2)
     up_give.pass_on()
-    qkv_sum.advance(2)
-    gain_sum.advance(1)
     out_give.pass_on()
     up_give.late()
-    gain_sum.advance(2)
-    out_give.late()
+    gain_sum.take(last)
+    gain_out[...] = gain_block_of(plane)[...]
     qkv_sum.take(last)
     qkv_give = give(4, qkv_sum, qkv_all)
-    gain_sum.take(last)
-    gain_out[...] = gain_block_of(plane)[...]
+    out_give.late()
     qkv_give.pass_on()
     qkv_give.late()
     for out, mine in spreads:
@@ -1650,7 +1677,7 @@
 
 def kernel_fits(n, planes, total, width, own_ff):
     held = 4 * width * own_ff + 2 * total * width + 2 * total * own_ff
-    return planes == 4 and total % (2 * ROWS) == 0 and n == 8 and own_ff // planes >= total // n and n * own_ff >= 4 * width and 2 * held < 44 * 1024 * 1024 and (own_ff // planes) % LANES == 0
+    return planes == 4 and total % (2 * ROWS) == 0 and n == 8 and own_ff // planes >= total // n and n * own_ff == planes * width and 2 * held < 44 * 1024 * 1024 and (own_ff // planes) % LANES == 0
 
 
 def own_columns(array, index, width):
@@ -1758,11 +1785,9 @@
     gains = gains_all.reshape(n_fsdp, 8, 2, rows_shard)[:, 0].transpose(1, 0, 2).reshape(2, 1, width)
     grad_result = reorder(cotangent_all, dealt_of_given)
 
-    column = lax.broadcasted_iota(jnp.int32, (own_width, width), 1) - me * own_width
-    place = (column == lax.broadcasted_iota(jnp.int32, (own_width, width), 0)).astype(BF16)
-    result_part = RESIDUAL_SCALE * dot_nn(reorder(both, given_of_dealt), jnp.concatenate([w_down, place], axis=0))
+    result_part = result_rows(me_array, reorder(both, given_of_dealt), w_down)
     activations = lax.psum_scatter(
-        result_part.astype(BF16), "ctx", scatter_dimension=0, tiled=True
+        result_part, "ctx", scatter_dimension=0, tiled=True
     )[None]
 
     if kernel_fits(n_ctx, n_fsdp, total, width, own_ff):

time: 694 us -> 689 us (level)
  matrix products: 13 us -> 0 us
  Pallas kernels: 628 us -> 636 us
    dot_general x1 -> x0, matrix products: 13 us -> none  [dot_nn(): lax.dot_general(a, b, (((1,), (0,)), ((), ())), preferred_element_type=F32)]
    pallas_call x0 -> x1, Pallas kernels: none -> 11.8 us  [result_rows(): pl.pallas_call(result_kernel, grid=(total // ROWS,), in_specs=[pl.BlockSp...]
  transfers between devices with their start and end apart: 2 -> 2, of which waited for: 0 -> 0; matrix products, arithmetic and copies ran while one was open for 5% -> 4% of each run, Pallas kernels for 92% -> 94%
where the time goes in v8:
time: 689 us; the launch traced here: 677 us
  Pallas kernels  636 us (92%)
  local copies, waits for them, and re-layouts  18.5 us (3%)
  between operations  14.4 us (2%)
  other arithmetic  7.52 us (1%)
    pallas_call x1, Pallas kernels, backward(): pl.pallas_call(functools.partial(backward_kernel, n, planes, heads), in_s...  342 us
    pallas_call x1, Pallas kernels, forward(): pl.pallas_call(functools.partial(forward_kernel, n, planes, heads), in_sp...  250 us
    pallas_call x1, Pallas kernels, finish(): pl.pallas_call(functools.partial(finish_kernel, slab), grid=(steps,), in_...  32.3 us
  transfers between devices with their start and end apart: 2, of which 0 were waited for; matrix products, arithmetic and copies ran while one was open for 4% of the time, Pallas kernels for 94%

profile of v8, /device:TPU:9, one launch (start us, length us, event | category | flops | bytes accessed | tf_op | source)
XLA Modules:
  0.0 677.3 jit_solution(10062618156572626372)
XLA Ops:
  7.2 0.7 all-gather.3.cloned.1.call-update
  8.0 0.1 mul.63
  8.1 0.7 broadcast_in_dim.39
  8.8 0.1 tile.10
  8.9 0.1 mul.66
  9.0 0.8 select_reduce_fusion
  9.9 0.1 reshape.115
  10.0 0.7 maximum_convert_fusion
  10.7 0.7 subtract_convert_fusion
  11.3 1.1 constant_dynamic-slice_fusion.1
  12.5 1.1 constant_dynamic-slice_fusion
  13.6 1.0 pad_maximum_fusion.attn_shard
  14.6 4.3 fusion
  18.8 0.6 tile.8.gain_shard
  19.5 250.1 %forward.1 = (bf16[1536,2048]{1,0:T(8,128)(2,1)}, bf16[1536,2048]{1,0:T(8,128)(2,1)}, bf16[1536,256]{1,0:T(8,128)(2,1)}, bf16[1536,128]{1,0:T(8,128)(2,1)}, bf16...) custom-call(s32[2]{0:T(128)} %bitcast.29, ...), custom_call_target="tpu_custom_call" | custom-call | flops 16911433728 | bytes 62914560 | tf_op jit(solution)/shard_map/forward/pallas_call | solution.py:928
  269.6 4.8 gather_fusion
  274.4 11.8 %result_rows.1 = bf16[1536,2048]{1,0:T(8,128)(2,1)} custom-call(s32[1]{0:T(128)} %bitcast.me_ref, bf16[1536,1280]{1,0:T(8,128)(2,1)} %bitcast.23, bf16[1024,2048]{1,0:T(8,128)(2,1)} %get-tuple-element.43.w_ref.down_in), custom_call_target="tpu_custom_call" | custom-call | flops 6442450944 | bytes 14417920 | tf_op jit(solution)/shard_map/result_rows/pallas_call | solution.py:290
  286.4 0.6 copy-done.1
  286.9 0.1 mul.72
  287.1 6.4 gather_fusion.1
  293.5 341.9 %backward.1 = (f32[192,2048]{1,0:T(8,128)}, f32[8,512]{1,0:T(8,128)}, bf16[8,256,2048]{2,1,0:T(8,128)(2,1)}, bf16[8,512,1024]{2,1,0:T(8,128)(2,1)}, bf16[8,512,1...) custom-call(s32[2]{0:T(128)} %bitcast.30, ...), custom_call_target="tpu_custom_call" | custom-call | flops 51539607552 | bytes 104857600 | tf_op jit(solution)/shard_map/backward/pallas_call | solution.py:1628
  635.4 32.3 %finish.1 = (f32[512,8192]{1,0:T(8,128)}, f32[512,8192]{1,0:T(8,128)}, f32[2048,2048]{1,0:T(8,128)}, f32[512,2048]{1,0:T(8,128)}, f32[512,2048]{1,0:T(8,128)}, /*index=5*/f32[512,512]{1,0:T(8,128)}, f32[512,512]{1,0:T(8,128)}) custom-call(bf16[8,512,1024]{2,1,0:T(8,128)(2,1)} %get-tuple-element.61.gate_ref, bf16[8,512,1024]{2,1,0:T(8,128)(2,1)} %get-tuple-element.62.up_ref, ...), custom_call_target="tpu_custom_call" | custom-call | bytes 75497472 | tf_op jit(solution)/shard_map/finish/pallas_call | solution.py:344
  667.7 1.4 fusion.1
  669.1 1.1 copy.27
  (20 shorter events, 0.4 us)
Async XLA Ops:
  7.2 279.9 %all-gather.3.cloned.1.call-start = ((), (), s32[]{:S(2)}) async-start(), calls=%async_computation.2 | async-start | bytes 7077888 | tf_op jit(solution)/shard_map/all_gather | solution.py:1768
  7.9 661.2 %reduce-scatter.2.cloned.1.call-start = ((), (), s32[]{:S(2)}) async-start(), calls=%async_computation.1 | async-start | bytes 7077888 | tf_op jit(solution)/shard_map/reduce_scatter | solution.py:1789
  286.3 0.7 copy-start.1
  635.4 33.7 %copy-start = (f32[192,2048]{1,0:T(8,128)S(1)}, f32[192,2048]{1,0:T(8,128)}, u32[]{:S(2)}) copy-start(f32[192,2048]{1,0:T(8,128)} %get-tuple-element.59) | copy-start | bytes 4718596
Sparse Core Ops, SparseCore 0:
  9.9 62.7 all-gather.2
  286.4 73.9 reduce-scatter.1

commit v9 on v8

--- a/solution.py
+++ b/solution.py
@@ -999,11 +999,21 @@
         )
 
     def start(self, step=0):
-        for way, active, shard, to in self.sends(step):
-
-            @pl.when(active)
+        ahead = [step + 1] if step else [0, 1]
+        for way in range(2):
+            end = self.plane == (0, self.planes - 1)[way]
+            _, active, shard, to = self.sends(step)[way]
+
+            @pl.when(active & jnp.logical_not(end))
             def _(way=way, shard=shard, to=to):
                 self.copy(way, step, shard, to).start()
+
+            @pl.when(end)
+            def _(way=way):
+                for later in ahead:
+                    if later < self.planes - 1:
+                        _, _, shard, to = self.sends(later)[way]
+                        self.copy(way, later, shard, to).start()
 
     def take(self, step):
         for way, active, shard in self.receives(step):
@@ -1287,13 +1297,10 @@
         rows = pl.ds(pl.multiple_of(d * own_width, own_width), own_width)
         p_down[rows, :] = (RESIDUAL_SCALE * dot_tn(part[d], grad[...])).astype(BF16)
 
-        @pl.when(i == 1)
-        def _():
-            down_sum.start()
-
         return 0
 
     lax.fori_loop(0, planes, down_block, 0)
+    down_sum.start()
 
     for copy in (down_load, gate_load, up_load, a_load, b_load, attn_load, gain_load):
         copy.wait()

time: 689 us -> 688 us (level)
  no operation moved by 1% of the time
where the time goes in v9:
time: 688 us; the launch traced here: 676 us
  Pallas kernels  635 us (92%)
  local copies, waits for them, and re-layouts  18.5 us (3%)
  between operations  14.4 us (2%)
  other arithmetic  7.52 us (1%)
    pallas_call x1, Pallas kernels, backward(): pl.pallas_call(functools.partial(backward_kernel, n, planes, heads), in_s...  341 us
    pallas_call x1, Pallas kernels, forward(): pl.pallas_call(functools.partial(forward_kernel, n, planes, heads), in_sp...  250 us
    pallas_call x1, Pallas kernels, finish(): pl.pallas_call(functools.partial(finish_kernel, slab), grid=(steps,), in_...  32.3 us
  transfers between devices with their start and end apart: 2, of which 0 were waited for; matrix products, arithmetic and copies ran while one was open for 4% of the time, Pallas kernels for 94%

profile of v9, /device:TPU:9, one launch (start us, length us, event | category | flops | bytes accessed | tf_op | source)
XLA Modules:
  0.0 676.4 jit_solution(15328750613314424769)
XLA Ops:
  7.2 0.7 all-gather.3.cloned.1.call-update
  8.0 0.1 mul.63
  8.1 0.7 broadcast_in_dim.39
  8.8 0.1 tile.10
  8.9 0.1 mul.66
  9.0 0.8 select_reduce_fusion
  9.9 0.1 reshape.115
  10.0 0.7 maximum_convert_fusion
  10.7 0.7 subtract_convert_fusion
  11.3 1.1 constant_dynamic-slice_fusion.1
  12.5 1.1 constant_dynamic-slice_fusion
  13.6 1.0 pad_maximum_fusion.attn_shard
  14.6 4.3 fusion
  18.8 0.6 tile.8.gain_shard
  19.5 250.1 %forward.1 = (bf16[1536,2048]{1,0:T(8,128)(2,1)}, bf16[1536,2048]{1,0:T(8,128)(2,1)}, bf16[1536,256]{1,0:T(8,128)(2,1)}, bf16[1536,128]{1,0:T(8,128)(2,1)}, bf16...) custom-call(s32[2]{0:T(128)} %bitcast.29, ...), custom_call_target="tpu_custom_call" | custom-call | flops 16911433728 | bytes 62914560 | tf_op jit(solution)/shard_map/forward/pallas_call | solution.py:928
  269.6 4.8 gather_fusion
  274.4 11.8 %result_rows.1 = bf16[1536,2048]{1,0:T(8,128)(2,1)} custom-call(s32[1]{0:T(128)} %bitcast.me_ref, bf16[1536,1280]{1,0:T(8,128)(2,1)} %bitcast.23, bf16[1024,2048]{1,0:T(8,128)(2,1)} %get-tuple-element.43.w_ref.down_in), custom_call_target="tpu_custom_call" | custom-call | flops 6442450944 | bytes 14417920 | tf_op jit(solution)/shard_map/result_rows/pallas_call | solution.py:290
  286.4 0.6 copy-done.1
  286.9 0.1 mul.72
  287.1 6.4 gather_fusion.1
  293.5 341.0 %backward.1 = (f32[192,2048]{1,0:T(8,128)}, f32[8,512]{1,0:T(8,128)}, bf16[8,256,2048]{2,1,0:T(8,128)(2,1)}, bf16[8,512,1024]{2,1,0:T(8,128)(2,1)}, bf16[8,512,1...) custom-call(s32[2]{0:T(128)} %bitcast.30, ...), custom_call_target="tpu_custom_call" | custom-call | flops 51539607552 | bytes 104857600 | tf_op jit(solution)/shard_map/backward/pallas_call | solution.py:1635
  634.5 32.3 %finish.1 = (f32[512,8192]{1,0:T(8,128)}, f32[512,8192]{1,0:T(8,128)}, f32[2048,2048]{1,0:T(8,128)}, f32[512,2048]{1,0:T(8,128)}, f32[512,2048]{1,0:T(8,128)}, /*index=5*/f32[512,512]{1,0:T(8,128)}, f32[512,512]{1,0:T(8,128)}) custom-call(bf16[8,512,1024]{2,1,0:T(8,128)(2,1)} %get-tuple-element.61.gate_ref, bf16[8,512,1024]{2,1,0:T(8,128)(2,1)} %get-tuple-element.62.up_ref, ...), custom_call_target="tpu_custom_call" | custom-call | bytes 75497472 | tf_op jit(solution)/shard_map/finish/pallas_call | solution.py:344
  666.8 1.4 fusion.1
  668.2 1.1 copy.27
  (20 shorter events, 0.4 us)
Async XLA Ops:
  7.2 279.9 %all-gather.3.cloned.1.call-start = ((), (), s32[]{:S(2)}) async-start(), calls=%async_computation.2 | async-start | bytes 7077888 | tf_op jit(solution)/shard_map/all_gather | solution.py:1775
  7.9 660.3 %reduce-scatter.2.cloned.1.call-start = ((), (), s32[]{:S(2)}) async-start(), calls=%async_computation.1 | async-start | bytes 7077888 | tf_op jit(solution)/shard_map/reduce_scatter | solution.py:1796
  286.2 0.7 copy-start.1
  634.5 33.7 %copy-start = (f32[192,2048]{1,0:T(8,128)S(1)}, f32[192,2048]{1,0:T(8,128)}, u32[]{:S(2)}) copy-start(f32[192,2048]{1,0:T(8,128)} %get-tuple-element.59) | copy-start | bytes 4718596
Sparse Core Ops, SparseCore 0:
  9.9 62.7 all-gather.2
  286.4 76.5 reduce-scatter.1

commit v10 on v9

--- a/solution.py
+++ b/solution.py
@@ -600,8 +600,7 @@
     up_ref,
     down_ref,
     gain_shard,
-    cos_ref,
-    sin_ref,
+    turns_ref,
     x_out,
     normed_out,
     q_out,
@@ -619,6 +618,8 @@
     up_out,
     down_out,
     gain_out,
+    cos_out,
+    sin_out,
     w_attn,
     w_gate,
     w_up,
@@ -636,6 +637,8 @@
     own_scaled,
     wide,
     narrow,
+    cos_ref,
+    sin_ref,
     z_send,
     z_recv,
     c_send,
@@ -698,6 +701,19 @@
         n, tokens_ref, lambda c: x_all.at[pl.ds(c * per_device, per_device)], n, me, c_send.at[0], c_recv.at[0]
     )
     x_spread.start()
+
+    def rotary_block(i, _):
+        rows = pl.ds(pl.multiple_of(i * ROWS, ROWS), ROWS)
+        given = i * ROWS + lax.broadcasted_iota(jnp.int32, (ROWS, LANES), 0)
+        lane = lax.broadcasted_iota(jnp.int32, (ROWS, LANES), 1)
+        position = given - jnp.where(given >= length_ref[0], length_ref[0], 0)
+        angle = position.astype(F32) * turns_ref[0:1, :]
+        cos_ref[rows, :] = jnp.cos(angle)
+        sine = jnp.sin(angle)
+        sin_ref[rows, :] = jnp.where(lax.rem(lane, HEAD_SIZE) < HEAD_SIZE // 2, -sine, sine)
+        return 0
+
+    lax.fori_loop(0, blocks, rotary_block, 0)
     for load in loads[2:]:
         load.wait()
     own_x.wait()
@@ -827,6 +843,8 @@
     own_h.wait()
     hid_spread.finish()
     keep(x_all, hid_out, 9)
+    keep(cos_ref, cos_out, 14)
+    keep(sin_ref, sin_out, 15)
     gate_chain.arrive(planes - 2)
     up_chain.arrive(planes - 2)
     keep(w_gate, gate_out, 10)
@@ -877,7 +895,7 @@
         copy.wait()
 
 
-def forward(n, planes, heads, slab, lengths, tokens, attn_shard, gate, up, down, gain_shard, cos, sin):
+def forward(n, planes, heads, slab, lengths, tokens, attn_shard, gate, up, down, gain_shard, turns):
     per_device, width = tokens.shape
     total = per_device * n
     own = heads * HEAD_SIZE
@@ -906,7 +924,7 @@
         ((total, own_ff), BF16),
         ((total, own_ff), BF16),
         ((total, own_ff + own_width), BF16),
-    ] + weights
+    ] + weights + [((total, LANES), F32)] * 2
     scratch = weights + [
         ((total, width), BF16),
         ((total, columns), F32),
@@ -920,6 +938,8 @@
         ((total, own_width), BF16),
         ((2, ROWS, width), BF16),
         ((3, 2, ROWS, own_ff), BF16),
+        ((total, LANES), F32),
+        ((total, LANES), F32),
     ]
     steps = max(planes - 1, 1)
     dma = pltpu.SemaphoreType.DMA
@@ -927,7 +947,7 @@
     vmem = pl.BlockSpec(memory_space=pltpu.VMEM)
     return pl.pallas_call(
         functools.partial(forward_kernel, n, planes, heads),
-        in_specs=[pl.BlockSpec(memory_space=pltpu.SMEM), vmem] + [anywhere] * 5 + [vmem] * 2,
+        in_specs=[pl.BlockSpec(memory_space=pltpu.SMEM), vmem] + [anywhere] * 5 + [vmem],
         out_specs=[anywhere] * len(outs),
         out_shape=[jax.ShapeDtypeStruct(*o) for o in outs],
         scratch_shapes=[pltpu.VMEM(*s) for s in scratch]
@@ -941,7 +961,7 @@
             transcendentals=0,
         ),
         name="forward",
-    )(lengths, tokens, attn_shard, gate, up, down, gain_shard, cos, sin)
+    )(lengths, tokens, attn_shard, gate, up, down, gain_shard, turns)
 
 
 def add_into(dst, src):
@@ -1742,16 +1762,9 @@
 
     gain_shard = jnp.tile(jnp.concatenate([attn_gain, mlp_gain]).astype(F32)[None], (8, 1))
 
-    first_len = lengths[0, 0]
-    given = jnp.arange(total, dtype=jnp.int32)
-    position = given - jnp.where(given >= first_len, first_len, 0)
     freq_index = jnp.arange(HEAD_SIZE // 2, dtype=F32)
     inverse = ROPE_BASE ** (-2.0 * freq_index / HEAD_SIZE)
-    turns = jnp.tile(inverse, 4)
-    sign = jnp.tile(jnp.repeat(jnp.array([-1.0, 1.0], F32), HEAD_SIZE // 2), 2)
-    angles = position.astype(F32)[:, None] * turns[None, :]
-    cos_table = jnp.cos(angles)
-    sin_table = jnp.sin(angles) * sign[None, :]
+    turns = jnp.tile(inverse, (8, 4))
 
     deal_rows = deal[0]
     slot_ids = jnp.arange(n_ctx, dtype=jnp.int32)
@@ -1774,7 +1787,7 @@
 
     cotangent_all = lax.all_gather(cotangent[0], "ctx", axis=0, tiled=True)
     (
-        x, normed, q_rot, k_rot, v_rows, lse, attended_all, hidden_all, normed2, a, b, both, w_attn, w_gate, w_up, w_down, gains_all,
+        x, normed, q_rot, k_rot, v_rows, lse, attended_all, hidden_all, normed2, a, b, both, w_attn, w_gate, w_up, w_down, gains_all, cos_table, sin_table,
     ) = forward(
         n_ctx,
         n_fsdp,
@@ -1785,8 +1798,7 @@
         attn_shard,
         *ff_weights,
         gain_shard,
-        cos_table,
-        sin_table,
+        turns,
     )
     w_qkv, w_out = w_attn[:, : split + 2 * HEAD_SIZE], w_attn[:, split + 2 * HEAD_SIZE :]
     gains = gains_all.reshape(n_fsdp, 8, 2, rows_shard)[:, 0].transpose(1, 0, 2).reshape(2, 1, width)
@@ -1810,7 +1822,7 @@
             sin_table,
         )
         token_grad = token_grad[None]
-        own_gains = gain_rows[1::-1]
+        own_gains = gain_rows[1], gain_rows[0]
     else:
         mlp_grad = (RESIDUAL_SCALE * grad_result.astype(F32)).astype(BF16)
 

time: 688 us -> 682 us (level)
  transfers between devices with their start and end apart: 2 -> 2, of which waited for: 0 -> 0; matrix products, arithmetic and copies ran while one was open for 4% -> 3% of each run, Pallas kernels for 94% -> 95%
where the time goes in v10:
time: 682 us; the launch traced here: 671 us
  Pallas kernels  634 us (93%)
  local copies, waits for them, and re-layouts  18.2 us (3%)
  between operations  14.5 us (2%)
    pallas_call x1, Pallas kernels, backward(): pl.pallas_call(functools.partial(backward_kernel, n, planes, heads), in_s...  341 us
    pallas_call x1, Pallas kernels, forward(): pl.pallas_call(functools.partial(forward_kernel, n, planes, heads), in_sp...  250 us
    pallas_call x1, Pallas kernels, finish(): pl.pallas_call(functools.partial(finish_kernel, slab), grid=(steps,), in_...  32.3 us
  transfers between devices with their start and end apart: 2, of which 0 were waited for; matrix products, arithmetic and copies ran while one was open for 3% of the time, Pallas kernels for 95%

profile of v10, /device:TPU:9, one launch (start us, length us, event | category | flops | bytes accessed | tf_op | source)
XLA Modules:
  0.0 670.5 jit_solution(1447604412586700340)
XLA Ops:
  7.2 0.7 all-gather.3.cloned.1.call-update
  7.9 0.0 reduce-scatter.2.cloned.1.call-start
  8.0 0.1 tile.18
  8.1 0.8 select_reduce_fusion
  8.9 0.1 add_bitcast_fusion
  8.9 0.1 copy.24
  9.0 0.1 reshape.107
  9.1 0.7 maximum_convert_fusion
  9.8 1.1 constant_dynamic-slice_fusion.1
  10.9 1.1 constant_dynamic-slice_fusion
  12.0 1.0 pad_maximum_fusion.attn_shard
  13.0 0.6 tile.16.gain_shard
  13.6 0.6 tile.19.turns_ref
  14.2 249.6 %forward.1 = (bf16[1536,2048]{1,0:T(8,128)(2,1)}, bf16[1536,2048]{1,0:T(8,128)(2,1)}, bf16[1536,256]{1,0:T(8,128)(2,1)}, bf16[1536,128]{1,0:T(8,128)(2,1)}, bf16...) custom-call(s32[2]{0:T(128)} %bitcast.28, ...), custom_call_target="tpu_custom_call" | custom-call | flops 16911433728 | bytes 62914560 | tf_op jit(solution)/shard_map/forward/pallas_call | solution.py:948
  263.8 4.8 gather_fusion
  268.6 11.5 %result_rows.1 = bf16[1536,2048]{1,0:T(8,128)(2,1)} custom-call(s32[1]{0:T(128)} %bitcast.me_ref, bf16[1536,1280]{1,0:T(8,128)(2,1)} %bitcast.21, bf16[1024,2048]{1,0:T(8,128)(2,1)} %get-tuple-element.45.w_ref.down_in), custom_call_target="tpu_custom_call" | custom-call | flops 6442450944 | bytes 14417920 | tf_op jit(solution)/shard_map/result_rows/pallas_call | solution.py:290
  280.2 0.1 add.46
  280.3 0.6 copy-done.1
  280.8 0.1 mul.40
  281.0 6.4 gather_fusion.1
  287.4 341.0 %backward.1 = (f32[192,2048]{1,0:T(8,128)}, f32[8,512]{1,0:T(8,128)}, bf16[8,256,2048]{2,1,0:T(8,128)(2,1)}, bf16[8,512,1024]{2,1,0:T(8,128)(2,1)}, bf16[8,512,1...) custom-call(s32[2]{0:T(128)} %bitcast.29, ...), custom_call_target="tpu_custom_call" | custom-call | flops 51539607552 | bytes 104857600 | tf_op jit(solution)/shard_map/backward/pallas_call | solution.py:1655
  628.5 32.3 %finish.1 = (f32[512,8192]{1,0:T(8,128)}, f32[512,8192]{1,0:T(8,128)}, f32[2048,2048]{1,0:T(8,128)}, f32[512,2048]{1,0:T(8,128)}, f32[512,2048]{1,0:T(8,128)}, /*index=5*/f32[512,512]{1,0:T(8,128)}, f32[512,512]{1,0:T(8,128)}) custom-call(bf16[8,512,1024]{2,1,0:T(8,128)(2,1)} %get-tuple-element.65.gate_ref, bf16[8,512,1024]{2,1,0:T(8,128)(2,1)} %get-tuple-element.66.up_ref, ...), custom_call_target="tpu_custom_call" | custom-call | bytes 75497472 | tf_op jit(solution)/shard_map/finish/pallas_call | solution.py:344
  660.8 1.4 fusion
  662.2 1.1 copy.26
  (15 shorter events, 0.1 us)
Async XLA Ops:
  7.2 273.8 %all-gather.3.cloned.1.call-start = ((), (), s32[]{:S(2)}) async-start(), calls=%async_computation.2 | async-start | bytes 7077888 | tf_op jit(solution)/shard_map/all_gather | solution.py:1788
  7.9 654.2 %reduce-scatter.2.cloned.1.call-start = ((), (), s32[]{:S(2)}) async-start(), calls=%async_computation.1 | async-start | bytes 7077888 | tf_op jit(solution)/shard_map/reduce_scatter | solution.py:1808
  280.1 0.7 copy-start.1
  628.5 33.7 %copy-start = (f32[192,2048]{1,0:T(8,128)S(1)}, f32[192,2048]{1,0:T(8,128)}, u32[]{:S(2)}) copy-start(f32[192,2048]{1,0:T(8,128)} %get-tuple-element.63) | copy-start | bytes 4718596
Sparse Core Ops, SparseCore 0:
  9.9 64.0 all-gather.2
  280.3 76.4 reduce-scatter.1

commit v11 on v10

--- a/solution.py
+++ b/solution.py
@@ -2,6 +2,7 @@
 
 import jax
 import jax.numpy as jnp
+import numpy as np
 from jax import lax
 from jax.experimental import pallas as pl
 from jax.experimental.pallas import tpu as pltpu
@@ -595,7 +596,9 @@
     heads,
     length_ref,
     tokens_ref,
-    attn_shard,
+    query_ref,
+    kv_shard,
+    out_ref,
     gate_ref,
     up_ref,
     down_ref,
@@ -651,7 +654,7 @@
     me, plane = lax.axis_index("ctx"), lax.axis_index("fsdp")
     per_device, width = tokens_ref.shape
     total = x_all.shape[0]
-    rows_shard = attn_shard.shape[0]
+    rows_shard = kv_shard.shape[0]
     own = own_att.shape[1]
     own_width = own_hid.shape[1]
     columns = qkv.shape[1]
@@ -675,10 +678,15 @@
     down_chain = chain(3, w_down, slab)
     gain_chain = chain(4, gains, gain_shard.shape[0])
     own_ff = w_gate.shape[1]
-    loads = [
-        pltpu.make_async_copy(shard, c.slot(plane), keep_sem.at[i])
-        for i, (c, shard) in enumerate(((attn_chain, attn_shard), (gain_chain, gain_shard)))
+    attn_slot = attn_chain.slot(plane)
+    query_src = query_ref.at[:, pl.ds(pl.multiple_of(me * own, LANES), own)]
+    out_src = out_ref.at[:, pl.ds(pl.multiple_of(me * own_width, LANES), own_width)]
+    attn_loads = [
+        pltpu.make_async_copy(query_src, attn_slot.at[:, pl.ds(0, own)], load_sem.at[2, 1]),
+        pltpu.make_async_copy(kv_shard, attn_slot.at[:, pl.ds(own, LANES)], load_sem.at[2, 2]),
+        pltpu.make_async_copy(out_src, attn_slot.at[:, pl.ds(columns, own_width)], load_sem.at[2, 3]),
     ]
+    loads = [pltpu.make_async_copy(gain_shard, gain_chain.slot(plane), keep_sem.at[1])]
     for ref, c, at in ((gate_ref, gate_chain, 0), (up_ref, up_chain, 1)):
         for f in range(ref.shape[1] // (n * slab)):
             src = ref.at[:, pl.ds(pl.multiple_of((f * n + me) * slab, LANES), slab)]
@@ -688,14 +696,15 @@
             loads.append(pltpu.make_async_copy(ref, c.slot(plane), load_sem.at[at, 0]))
     down_src = down_ref if down_ref.shape[0] == slab else down_ref.at[pl.ds(pl.multiple_of(me * slab, slab), slab)]
     loads.append(pltpu.make_async_copy(down_src, down_chain.slot(plane), load_sem.at[2, 0]))
-    for load in loads:
+    for load in (*attn_loads, *loads):
         load.start()
     own_x = pltpu.make_async_copy(tokens_ref, x_all.at[pl.ds(me * per_device, per_device)], keep_sem.at[5])
     own_x.start()
     greet(n, planes, me, plane, True)
+    for load in attn_loads:
+        load.wait()
+    attn_chain.start(0)
     loads[0].wait()
-    attn_chain.start(0)
-    loads[1].wait()
     gain_chain.start(0)
     x_spread = spread_over(
         n, tokens_ref, lambda c: x_all.at[pl.ds(c * per_device, per_device)], n, me, c_send.at[0], c_recv.at[0]
@@ -714,7 +723,7 @@
         return 0
 
     lax.fori_loop(0, blocks, rotary_block, 0)
-    for load in loads[2:]:
+    for load in loads[1:]:
         load.wait()
     own_x.wait()
     for step in range(1, planes - 1):
@@ -895,17 +904,17 @@
         copy.wait()
 
 
-def forward(n, planes, heads, slab, lengths, tokens, attn_shard, gate, up, down, gain_shard, turns):
+def forward(n, planes, heads, slab, lengths, tokens, query, kv_shard, out, gate, up, down, gain_shard, turns):
     per_device, width = tokens.shape
     total = per_device * n
     own = heads * HEAD_SIZE
     columns = own + 2 * HEAD_SIZE
-    own_width = attn_shard.shape[1] - columns
+    own_width = width // n
     own_ff = planes * slab
-    rows_shard = attn_shard.shape[0]
+    rows_shard = kv_shard.shape[0]
     pairs = heads // 2
     weights = [
-        ((planes * rows_shard, attn_shard.shape[1]), BF16),
+        ((planes * rows_shard, columns + own_width), BF16),
         ((planes * rows_shard, own_ff), BF16),
         ((planes * rows_shard, own_ff), BF16),
         ((own_ff, width), BF16),
@@ -947,11 +956,11 @@
     vmem = pl.BlockSpec(memory_space=pltpu.VMEM)
     return pl.pallas_call(
         functools.partial(forward_kernel, n, planes, heads),
-        in_specs=[pl.BlockSpec(memory_space=pltpu.SMEM), vmem] + [anywhere] * 5 + [vmem],
+        in_specs=[pl.BlockSpec(memory_space=pltpu.SMEM), vmem] + [anywhere] * 7 + [vmem],
         out_specs=[anywhere] * len(outs),
         out_shape=[jax.ShapeDtypeStruct(*o) for o in outs],
         scratch_shapes=[pltpu.VMEM(*s) for s in scratch]
-        + [dma((5, 2, steps)), dma((5, 2, steps)), dma((3, n)), dma((3, n)), dma((16,)), dma((3, planes)), dma((2,)), dma((3, 2))],
+        + [dma((5, 2, steps)), dma((5, 2, steps)), dma((3, n)), dma((3, n)), dma((16,)), dma((3, max(planes, 4))), dma((2,)), dma((3, 2))],
         compiler_params=pltpu.CompilerParams(
             vmem_limit_bytes=VMEM_LIMIT, collective_id=1, has_side_effects=True
         ),
@@ -961,7 +970,7 @@
             transcendentals=0,
         ),
         name="forward",
-    )(lengths, tokens, attn_shard, gate, up, down, gain_shard, turns)
+    )(lengths, tokens, query, kv_shard, out, gate, up, down, gain_shard, turns)
 
 
 def add_into(dst, src):
@@ -1747,12 +1756,10 @@
 
     kv_head = me // sharing
     split = heads * HEAD_SIZE
-    attn_shard = jnp.concatenate(
+    kv_shard = jnp.concatenate(
         [
-            own_columns(query_weight, me, split),
             own_columns(key_matrix, kv_head, HEAD_SIZE),
             own_columns(value_matrix, kv_head, HEAD_SIZE),
-            own_columns(out_weight, me, own_width),
         ],
         axis=1,
     )
@@ -1762,9 +1769,8 @@
 
     gain_shard = jnp.tile(jnp.concatenate([attn_gain, mlp_gain]).astype(F32)[None], (8, 1))
 
-    freq_index = jnp.arange(HEAD_SIZE // 2, dtype=F32)
-    inverse = ROPE_BASE ** (-2.0 * freq_index / HEAD_SIZE)
-    turns = jnp.tile(inverse, (8, 4))
+    freq_index = np.arange(HEAD_SIZE // 2)
+    turns = jnp.asarray(np.tile(ROPE_BASE ** (-2.0 * freq_index / HEAD_SIZE), (8, 4)), F32)
 
     deal_rows = deal[0]
     slot_ids = jnp.arange(n_ctx, dtype=jnp.int32)
@@ -1795,7 +1801,9 @@
         slab,
         lengths[0],
         tokens[0],
-        attn_shard,
+        query_weight,
+        kv_shard,
+        out_weight,
         *ff_weights,
         gain_shard,
         turns,

time: 682 us -> 680 us (level)
  no operation moved by 1% of the time
where the time goes in v11:
time: 680 us; the launch traced here: 669 us
  Pallas kernels  635 us (93%)
  local copies, waits for them, and re-layouts  16.4 us (2%)
  between operations  14.5 us (2%)
    pallas_call x1, Pallas kernels, backward(): pl.pallas_call(functools.partial(backward_kernel, n, planes, heads), in_s...  341 us
    pallas_call x1, Pallas kernels, forward(): pl.pallas_call(functools.partial(forward_kernel, n, planes, heads), in_sp...  249 us
    pallas_call x1, Pallas kernels, finish(): pl.pallas_call(functools.partial(finish_kernel, slab), grid=(steps,), in_...  32.3 us
  transfers between devices with their start and end apart: 2, of which 0 were waited for; matrix products, arithmetic and copies ran while one was open for 3% of the time, Pallas kernels for 95%

profile of v11, /device:TPU:9, one launch (start us, length us, event | category | flops | bytes accessed | tf_op | source)
XLA Modules:
  0.0 668.6 jit_solution(13053079349580436513)
XLA Ops:
  7.2 0.0 all-gather.3.cloned.1.call-start
  7.2 0.7 all-gather.3.cloned.1.call-update
  7.9 0.0 reduce-scatter.2.cloned.1.call-start
  8.0 0.8 select_reduce_fusion
  8.8 0.1 add_bitcast_fusion
  8.8 0.1 copy.25
  8.9 0.1 reshape.99
  9.0 0.7 maximum_convert_fusion
  9.7 1.1 constant_dynamic-slice_fusion
  10.8 0.8 pad_maximum_fusion.kv_shard
  11.6 0.6 tile.2.gain_shard
  12.2 249.5 %forward.1 = (bf16[1536,2048]{1,0:T(8,128)(2,1)}, bf16[1536,2048]{1,0:T(8,128)(2,1)}, bf16[1536,256]{1,0:T(8,128)(2,1)}, bf16[1536,128]{1,0:T(8,128)(2,1)}, bf16...) custom-call(s32[2]{0:T(128)} %bitcast.28, ...), custom_call_target="tpu_custom_call" | custom-call | flops 16911433728 | bytes 62914560 | tf_op jit(solution)/shard_map/forward/pallas_call | solution.py:957
  261.7 4.8 gather_fusion
  266.5 11.5 %result_rows.1 = bf16[1536,2048]{1,0:T(8,128)(2,1)} custom-call(s32[1]{0:T(128)} %bitcast.me_ref, bf16[1536,1280]{1,0:T(8,128)(2,1)} %bitcast.21, bf16[1024,2048]{1,0:T(8,128)(2,1)} %get-tuple-element.45.w_ref.down_in), custom_call_target="tpu_custom_call" | custom-call | flops 6442450944 | bytes 14417920 | tf_op jit(solution)/shard_map/result_rows/pallas_call | solution.py:291
  278.0 0.0 reduce-scatter.2.cloned.1.call-update
  278.1 0.1 add.41
  278.2 0.6 copy-done.1
  278.7 0.1 mul.32
  278.8 0.0 all-gather.3.cloned.1.call-done
  278.9 6.4 gather_fusion.1
  285.3 341.2 %backward.1 = (f32[192,2048]{1,0:T(8,128)}, f32[8,512]{1,0:T(8,128)}, bf16[8,256,2048]{2,1,0:T(8,128)(2,1)}, bf16[8,512,1024]{2,1,0:T(8,128)(2,1)}, bf16[8,512,1...) custom-call(s32[2]{0:T(128)} %bitcast.29, ...), custom_call_target="tpu_custom_call" | custom-call | flops 51539607552 | bytes 104857600 | tf_op jit(solution)/shard_map/backward/pallas_call | solution.py:1664
  626.5 32.3 %finish.1 = (f32[512,8192]{1,0:T(8,128)}, f32[512,8192]{1,0:T(8,128)}, f32[2048,2048]{1,0:T(8,128)}, f32[512,2048]{1,0:T(8,128)}, f32[512,2048]{1,0:T(8,128)}, /*index=5*/f32[512,512]{1,0:T(8,128)}, f32[512,512]{1,0:T(8,128)}) custom-call(bf16[8,512,1024]{2,1,0:T(8,128)(2,1)} %get-tuple-element.65.gate_ref, bf16[8,512,1024]{2,1,0:T(8,128)(2,1)} %get-tuple-element.66.up_ref, ...), custom_call_target="tpu_custom_call" | custom-call | bytes 75497472 | tf_op jit(solution)/shard_map/finish/pallas_call | solution.py:345
  658.8 1.4 fusion
  660.2 1.1 copy.27
  (10 shorter events, 0.0 us)
Async XLA Ops:
  7.2 271.7 %all-gather.3.cloned.1.call-start = ((), (), s32[]{:S(2)}) async-start(), calls=%async_computation.2 | async-start | bytes 7077888 | tf_op jit(solution)/shard_map/all_gather | solution.py:1794
  7.9 652.3 %reduce-scatter.2.cloned.1.call-start = ((), (), s32[]{:S(2)}) async-start(), calls=%async_computation.1 | async-start | bytes 7077888 | tf_op jit(solution)/shard_map/reduce_scatter | solution.py:1816
  278.0 0.7 copy-start.1
  626.5 33.7 %copy-start = (f32[192,2048]{1,0:T(8,128)S(1)}, f32[192,2048]{1,0:T(8,128)}, u32[]{:S(2)}) copy-start(f32[192,2048]{1,0:T(8,128)} %get-tuple-element.63) | copy-start | bytes 4718596
Sparse Core Ops, SparseCore 0:
  9.9 64.0 all-gather.2
  278.2 75.9 reduce-scatter.1
